TPU v7x, 512 devices: a whole 4x4x16 slice. The times are simulated.
512 devices in a mesh: leaf: 64 (over x, z), front: 8 (over y, core).
Axes of the slice: x: 4, y: 4, z: 16, core: 2. Of those that a mesh axis runs over, the one named last changes fastest.
Arguments:
- basis: bfloat16 [16, 90112], P(None, ('leaf', 'front')), may hold values from -6 to 6
- order: int32 [64, 1408], P('leaf'), may hold values from 0 to 1407, each once within a row
- leaf_inverse: bfloat16 [65536, 1024], P(('leaf', 'front')), may hold values from -0.1875 to 0.1875
- leaf_upper_inverse: bfloat16 [65536, 1024], P(('leaf', 'front')), may hold values from -0.1875 to 0.1875
- leaf_coupling_low: bfloat16 [8192, 2048], P(('leaf', 'front')), may hold values from -0.0625 to 0.0625
- leaf_coupling_up: bfloat16 [65536, 256], P(('leaf', 'front')), may hold values from -0.1875 to 0.1875
- sep_lower_inverse: bfloat16 [8192, 1792], P(('leaf', 'front')), may hold values from -4 to 4
- sep_upper_inverse: bfloat16 [8192, 1792], P(('leaf', 'front')), may hold values from -4 to 4
- sep_coupling_low: bfloat16 [8192, 1536], P(('leaf', 'front')), may hold values from -4 to 4
- sep_coupling_up: bfloat16 [8192, 1536], P(('leaf', 'front')), may hold values from -4 to 4
Outputs:
- shifted: bfloat16 [16, 90112], P(None, ('leaf', 'front'))
All inputs are finite; a program needn't handle non-finite values.
Results may differ from a plain program's by a relative error of at most 0.015.
Values may be sent and summed in bfloat16 or wider, within the bound.
No kernel may reach another device: no remote copies, remote signals or barrier semaphores. Data moves between devices by JAX's collectives and lax.ppermute only.
A program may use at most 64 MiB of HBM per device.

v0:
```python
import jax
import jax.numpy as jnp
from jax import lax
from jax.sharding import PartitionSpec as P

LEVELS = 3


def swapped(x, axis, stride):
    return lax.ppermute(x, axis, [(i, i ^ 1 << stride) for i in range(lax.axis_size(axis))])


def apply_rows(vector, matrix):
    return lax.dot_general(
        vector, matrix, (((1,), (1,)), ((), ())), preferred_element_type=jnp.float32
    )


def paired_vector(own_piece, level_idx, leaf_pos):
    joined = lax.all_gather(own_piece, "front", axis=1, tiled=True)
    for bit_pos in range(level_idx):
        partner = swapped(joined, "leaf", bit_pos)
        is_lower = leaf_pos // 2**bit_pos % 2 == 0
        joined = jnp.where(
            is_lower, jnp.concatenate([joined, partner], 1), jnp.concatenate([partner, joined], 1)
        )
    return joined


def node_vector(own_piece, level_idx, leaf_pos):
    gathered = paired_vector(own_piece, level_idx, leaf_pos)
    return gathered


def section_vector(own_piece):
    return lax.all_gather(own_piece, "front", axis=1, tiled=True)


def local(
    basis,
    order,
    leaf_inverse,
    leaf_upper_inverse,
    leaf_coupling_low,
    leaf_coupling_up,
    sep_lower_inverse,
    sep_upper_inverse,
    sep_coupling_low,
    sep_coupling_up,
):
    leaf_pos = lax.axis_index("leaf")
    front_pos = lax.axis_index("front")
    fronts = lax.axis_size("front")
    height = LEVELS
    block_cols, rows_dev = basis.shape
    sub_dev = leaf_inverse.shape[0]
    sep_dev = sep_lower_inverse.shape[0]
    unit_cols = fronts * sep_dev
    grouped = lax.all_gather(basis, "front", axis=1, tiled=True)
    ordered = jnp.take(grouped, order[0], axis=1)
    slot_grid = ordered.reshape(block_cols, fronts, rows_dev)
    leaf_rhs = slot_grid[:, :, :sub_dev].reshape(block_cols, fronts * sub_dev)
    own_slots = lax.dynamic_slice_in_dim(ordered, front_pos * rows_dev, rows_dev, 1)
    leaf_out = apply_rows(leaf_rhs, leaf_inverse).astype(jnp.bfloat16)
    section = section_vector(leaf_out)
    sibling = swapped(section, "leaf", 0)
    is_lower = leaf_pos % 2 == 0
    first_children = jnp.where(
        is_lower, jnp.concatenate([section, sibling], 1), jnp.concatenate([sibling, section], 1)
    )
    forward = []
    for level_idx in range(1, height + 1):
        slot_start = sub_dev + (level_idx - 1) * sep_dev
        own_rhs = own_slots[:, slot_start : slot_start + sep_dev].astype(jnp.float32)
        col_width = unit_cols * 2**level_idx
        if level_idx == 1:
            coupled = apply_rows(first_children, leaf_coupling_low)
        else:
            col_start = unit_cols * (2**level_idx - 4)
            children = node_vector(forward[-1], level_idx, leaf_pos)
            coupled = apply_rows(children, sep_coupling_low[:, col_start : col_start + col_width])
        reduced = (own_rhs - coupled).astype(jnp.bfloat16)
        gathered = node_vector(reduced, level_idx, leaf_pos)
        col_start = unit_cols * (2**level_idx - 2)
        forward.append(
            apply_rows(gathered, sep_lower_inverse[:, col_start : col_start + col_width]).astype(
                jnp.bfloat16
            )
        )
    backward = [None] * height
    for level_idx in range(height, 0, -1):
        col_width = unit_cols * 2**level_idx
        if level_idx < height:
            parent = node_vector(backward[level_idx], level_idx + 1, leaf_pos)
            col_start = unit_cols * (2 ** (level_idx + 1) - 4)
            coupled = apply_rows(parent, sep_coupling_up[:, col_start : col_start + 2 * col_width])
            carried = (forward[level_idx - 1].astype(jnp.float32) - coupled).astype(jnp.bfloat16)
        else:
            carried = forward[level_idx - 1]
        gathered = node_vector(carried, level_idx, leaf_pos)
        col_start = unit_cols * (2**level_idx - 2)
        backward[level_idx - 1] = apply_rows(
            gathered, sep_upper_inverse[:, col_start : col_start + col_width]
        ).astype(jnp.bfloat16)
    parent = node_vector(backward[0], 1, leaf_pos)
    leaf_rest = (leaf_out.astype(jnp.float32) - apply_rows(parent, leaf_coupling_up)).astype(
        jnp.bfloat16
    )
    leaf_final = apply_rows(section_vector(leaf_rest), leaf_upper_inverse).astype(jnp.bfloat16)
    solved = jnp.concatenate([leaf_final] + backward, axis=1)
    everyone = lax.all_gather(solved, "front", axis=1, tiled=True)
    placed = jnp.zeros_like(everyone).at[:, order[0]].set(everyone)
    return lax.dynamic_slice_in_dim(placed, front_pos * rows_dev, rows_dev, 1)


def solution(mesh):
    in_specs = (
        P(None, ("leaf", "front")),
        P("leaf", None),
        P(("leaf", "front"), None),
        P(("leaf", "front"), None),
        P(("leaf", "front"), None),
        P(("leaf", "front"), None),
        P(("leaf", "front"), None),
        P(("leaf", "front"), None),
        P(("leaf", "front"), None),
        P(("leaf", "front"), None),
    )
    out_specs = P(None, ("leaf", "front"))
    return jax.shard_map(local, mesh=mesh, in_specs=in_specs, out_specs=out_specs, check_vma=False)
```

profile of v0, /device:TPU:1, one launch (start us, length us, event | category | flops | bytes accessed | tf_op | source)
XLA Modules:
  0.0 372.2 jit_solution(16792970437759925007)
XLA Ops:
  0.8 19.4 %all-gather = bf16[8,176,16]{1,2,0:T(8,128)(2,1)S(1)} all-gather(bf16[1,176,16]{1,2,0:T(8,128)(2,1)S(1)} %bitcast.28), channel_id=1, replica_groups=mesh['leaf'=64,'front'=8] {'front'}, dimensions={0}, use_global_device_ids=true | all-gather | bytes 50688 | tf_op jit(solution)/shard_map/all_gather | solution.py:59
  25.0 11.4 %all_gather.46 = bf16[16,1024]{1,0:T(8,128)(2,1)S(1)} all-gather(bf16[16,128]{1,0:T(8,128)(2,1)S(1)} %convolution_convert_fusion.7), channel_id=1, replica_groups=mesh['leaf'=64,'front'=8] {'front'}, dimensions={1}, use_global_device_ids=true | all-gather | bytes 36864 | tf_op jit(solution)/shard_map/all_gather | solution.py:36
  41.2 14.1 %all_gather.47 = bf16[16,128]{0,1:T(8,128)(2,1)S(1)} all-gather(bf16[16,16]{0,1:T(8,128)(2,1)S(1)} %copy.37), channel_id=1, replica_groups=mesh['leaf'=64,'front'=8] {'front'}, dimensions={1}, use_global_device_ids=true | all-gather | bytes 4608 | tf_op jit(solution)/shard_map/all_gather | solution.py:20
  60.3 14.0 %all_gather.48 = bf16[16,128]{0,1:T(8,128)(2,1)S(1)} all-gather(bf16[16,16]{0,1:T(8,128)(2,1)S(1)} %copy.42), channel_id=1, replica_groups=mesh['leaf'=64,'front'=8] {'front'}, dimensions={1}, use_global_device_ids=true | all-gather | bytes 4608 | tf_op jit(solution)/shard_map/all_gather | solution.py:20
  84.5 15.1 %all_gather.49 = bf16[16,128]{0,1:T(8,128)(2,1)S(1)} all-gather(bf16[16,16]{0,1:T(8,128)(2,1)S(1)} %copy.47), channel_id=1, replica_groups=mesh['leaf'=64,'front'=8] {'front'}, dimensions={1}, use_global_device_ids=true | all-gather | bytes 4608 | tf_op jit(solution)/shard_map/all_gather | solution.py:20
  109.8 15.1 %all_gather.50 = bf16[16,128]{0,1:T(8,128)(2,1)S(1)} all-gather(bf16[16,16]{0,1:T(8,128)(2,1)S(1)} %copy.52), channel_id=1, replica_groups=mesh['leaf'=64,'front'=8] {'front'}, dimensions={1}, use_global_device_ids=true | all-gather | bytes 4608 | tf_op jit(solution)/shard_map/all_gather | solution.py:20
  135.0 4.8 %collective-permute-start.8 = (bf16[16,512]{1,0:T(8,128)(2,1)S(1)}, bf16[16,512]{1,0:T(8,128)(2,1)S(1)}, u32[]{:S(2)}, u32[]{:S(2)}) collective-permute-start(bf16[16,512]{1,0:T(8,128)(2,1)S(1)} %maximum_select_fusion.14), channel_id=1, source_target_pairs={{0,32},{8,40},{16,48},{24,56},{32,0},{40,8},{48,16},{56,24},{64,96... | collective-permute-start | bytes 49160 | tf_op jit(solution)/shard_map/ppermute | solution.py:10
  139.8 3.6 collective-permute-done.8
  143.6 16.2 %all_gather.51 = bf16[16,128]{0,1:T(8,128)(2,1)S(1)} all-gather(bf16[16,16]{0,1:T(8,128)(2,1)S(1)} %copy.57), channel_id=1, replica_groups=mesh['leaf'=64,'front'=8] {'front'}, dimensions={1}, use_global_device_ids=true | all-gather | bytes 4608 | tf_op jit(solution)/shard_map/all_gather | solution.py:20
  169.9 4.8 %collective-permute-start.11 = (bf16[16,512]{1,0:T(8,128)(2,1)S(1)}, bf16[16,512]{1,0:T(8,128)(2,1)S(1)}, u32[]{:S(2)}, u32[]{:S(2)}) collective-permute-start(bf16[16,512]{1,0:T(8,128)(2,1)S(1)} %maximum_select_fusion.15), channel_id=1, source_target_pairs={{0,32},{8,40},{16,48},{24,56},{32,0},{40,8},{48,16},{56,24},{64,96... | collective-permute-start | bytes 49160 | tf_op jit(solution)/shard_map/ppermute | solution.py:10
  174.6 3.7 collective-permute-done.11
  178.5 16.2 %all_gather.52 = bf16[16,128]{0,1:T(8,128)(2,1)S(1)} all-gather(bf16[16,16]{0,1:T(8,128)(2,1)S(1)} %copy.62), channel_id=1, replica_groups=mesh['leaf'=64,'front'=8] {'front'}, dimensions={1}, use_global_device_ids=true | all-gather | bytes 4608 | tf_op jit(solution)/shard_map/all_gather | solution.py:20
  204.9 4.8 %collective-permute-start.14 = (bf16[16,512]{1,0:T(8,128)(2,1)S(1)}, bf16[16,512]{1,0:T(8,128)(2,1)S(1)}, u32[]{:S(2)}, u32[]{:S(2)}) collective-permute-start(bf16[16,512]{1,0:T(8,128)(2,1)S(1)} %maximum_select_fusion.16), channel_id=1, source_target_pairs={{0,32},{8,40},{16,48},{24,56},{32,0},{40,8},{48,16},{56,24},{64,96... | collective-permute-start | bytes 49160 | tf_op jit(solution)/shard_map/ppermute | solution.py:10
  209.7 3.7 collective-permute-done.14
  213.6 16.2 %all_gather.53 = bf16[16,128]{0,1:T(8,128)(2,1)S(1)} all-gather(bf16[16,16]{0,1:T(8,128)(2,1)S(1)} %copy.67), channel_id=1, replica_groups=mesh['leaf'=64,'front'=8] {'front'}, dimensions={1}, use_global_device_ids=true | all-gather | bytes 4608 | tf_op jit(solution)/shard_map/all_gather | solution.py:20
  239.8 4.8 %collective-permute-start.17 = (bf16[16,512]{1,0:T(8,128)(2,1)S(1)}, bf16[16,512]{1,0:T(8,128)(2,1)S(1)}, u32[]{:S(2)}, u32[]{:S(2)}) collective-permute-start(bf16[16,512]{1,0:T(8,128)(2,1)S(1)} %maximum_select_fusion.17), channel_id=1, source_target_pairs={{0,32},{8,40},{16,48},{24,56},{32,0},{40,8},{48,16},{56,24},{64,96... | collective-permute-start | bytes 49160 | tf_op jit(solution)/shard_map/ppermute | solution.py:10
  244.6 3.7 collective-permute-done.17
  248.5 16.2 %all_gather.54 = bf16[16,128]{0,1:T(8,128)(2,1)S(1)} all-gather(bf16[16,16]{0,1:T(8,128)(2,1)S(1)} %copy.72), channel_id=1, replica_groups=mesh['leaf'=64,'front'=8] {'front'}, dimensions={1}, use_global_device_ids=true | all-gather | bytes 4608 | tf_op jit(solution)/shard_map/all_gather | solution.py:20
  274.9 15.1 %all_gather.55 = bf16[16,128]{0,1:T(8,128)(2,1)S(1)} all-gather(bf16[16,16]{0,1:T(8,128)(2,1)S(1)} %copy.77), channel_id=1, replica_groups=mesh['leaf'=64,'front'=8] {'front'}, dimensions={1}, use_global_device_ids=true | all-gather | bytes 4608 | tf_op jit(solution)/shard_map/all_gather | solution.py:20
  300.4 15.1 %all_gather.56 = bf16[16,128]{0,1:T(8,128)(2,1)S(1)} all-gather(bf16[16,16]{0,1:T(8,128)(2,1)S(1)} %copy.82), channel_id=1, replica_groups=mesh['leaf'=64,'front'=8] {'front'}, dimensions={1}, use_global_device_ids=true | all-gather | bytes 4608 | tf_op jit(solution)/shard_map/all_gather | solution.py:20
  320.4 14.0 %all_gather.57 = bf16[16,128]{0,1:T(8,128)(2,1)S(1)} all-gather(bf16[16,16]{0,1:T(8,128)(2,1)S(1)} %copy.87), channel_id=1, replica_groups=mesh['leaf'=64,'front'=8] {'front'}, dimensions={1}, use_global_device_ids=true | all-gather | bytes 4608 | tf_op jit(solution)/shard_map/all_gather | solution.py:20
  339.2 12.4 %all_gather.58 = bf16[16,1024]{1,0:T(8,128)(2,1)S(1)} all-gather(bf16[16,128]{1,0:T(8,128)(2,1)S(1)} %fusion.5), channel_id=1, replica_groups=mesh['leaf'=64,'front'=8] {'front'}, dimensions={1}, use_global_device_ids=true | all-gather | bytes 36864 | tf_op jit(solution)/shard_map/all_gather | solution.py:36
  351.9 12.9 %all-gather.1 = bf16[8,176,16]{1,2,0:T(8,128)(2,1)S(1)} all-gather(bf16[1,176,16]{1,2,0:T(8,128)(2,1)S(1)} %maximum_bitcast_fusion), channel_id=1, replica_groups=mesh['leaf'=64,'front'=8] {'front'}, dimensions={0}, use_global_device_ids=true | all-gather | bytes 50688 | tf_op jit(solution)/shard_map/all_gather | solution.py:111
  365.1 6.4 %scatter_custom_fusion = bf16[16,1408]{0,1:T(8,128)(2,1)S(1)} fusion(s32[1408]{0:T(1024)S(1)} %fusion.92, bf16[1408,16]{1,0:T(8,128)(2,1)S(1)} %bitcast.24, bf16[]{:T(256)} %constant.154.clone.1), kind=kCustom, calls=%fused_computation.22 | custom fusion | bytes 45058 | tf_op jit(solution)/shard_map/scatter | solution.py:112
  (137 shorter events, 108.2 us)
Async XLA Ops:
  36.4 4.6 %collective-permute-start = (bf16[16,1024]{1,0:T(8,128)(2,1)S(1)}, bf16[16,1024]{1,0:T(8,128)(2,1)S(1)}, u32[]{:S(2)}, u32[]{:S(2)}) collective-permute-start(bf16[16,1024]{1,0:T(8,128)(2,1)S(1)} %all_gather.46), channel_id=1, source_target_pairs={{0,8},{8,0},{16,24},{24,16},{32,40},{40,32},{48,56},{56,48},{64,72... | collective-permute-start | bytes 98312 | tf_op jit(solution)/shard_map/ppermute | solution.py:10
  55.3 4.6 %collective-permute-start.1 = (bf16[16,128]{0,1:T(8,128)(2,1)S(1)}, bf16[16,128]{0,1:T(8,128)(2,1)S(1)}, u32[]{:S(2)}, u32[]{:S(2)}) collective-permute-start(bf16[16,128]{0,1:T(8,128)(2,1)S(1)} %all_gather.47), channel_id=1, source_target_pairs={{0,8},{8,0},{16,24},{24,16},{32,40},{40,32},{48,56},{56,48},{64,72... | collective-permute-start | bytes 12296 | tf_op jit(solution)/shard_map/ppermute | solution.py:10
  74.2 4.6 %collective-permute-start.2 = (bf16[16,128]{0,1:T(8,128)(2,1)S(1)}, bf16[16,128]{0,1:T(8,128)(2,1)S(1)}, u32[]{:S(2)}, u32[]{:S(2)}) collective-permute-start(bf16[16,128]{0,1:T(8,128)(2,1)S(1)} %all_gather.48), channel_id=1, source_target_pairs={{0,8},{8,0},{16,24},{24,16},{32,40},{40,32},{48,56},{56,48},{64,72... | collective-permute-start | bytes 12296 | tf_op jit(solution)/shard_map/ppermute | solution.py:10
  79.0 5.3 %collective-permute-start.3 = (bf16[16,256]{1,0:T(8,128)(2,1)S(1)}, bf16[16,256]{1,0:T(8,128)(2,1)S(1)}, u32[]{:S(2)}, u32[]{:S(2)}) collective-permute-start(bf16[16,256]{1,0:T(8,128)(2,1)S(1)} %maximum_select_fusion.24), channel_id=1, source_target_pairs={{0,16},{8,24},{16,0},{24,8},{32,48},{40,56},{48,32},{56,40},{64,80... | collective-permute-start | bytes 24584 | tf_op jit(solution)/shard_map/ppermute | solution.py:10
  99.6 4.6 %collective-permute-start.4 = (bf16[16,128]{0,1:T(8,128)(2,1)S(1)}, bf16[16,128]{0,1:T(8,128)(2,1)S(1)}, u32[]{:S(2)}, u32[]{:S(2)}) collective-permute-start(bf16[16,128]{0,1:T(8,128)(2,1)S(1)} %all_gather.49), channel_id=1, source_target_pairs={{0,8},{8,0},{16,24},{24,16},{32,40},{40,32},{48,56},{56,48},{64,72... | collective-permute-start | bytes 12296 | tf_op jit(solution)/shard_map/ppermute | solution.py:10
  104.3 5.3 %collective-permute-start.5 = (bf16[16,256]{1,0:T(8,128)(2,1)S(1)}, bf16[16,256]{1,0:T(8,128)(2,1)S(1)}, u32[]{:S(2)}, u32[]{:S(2)}) collective-permute-start(bf16[16,256]{1,0:T(8,128)(2,1)S(1)} %maximum_select_fusion.25), channel_id=1, source_target_pairs={{0,16},{8,24},{16,0},{24,8},{32,48},{40,56},{48,32},{56,40},{64,80... | collective-permute-start | bytes 24584 | tf_op jit(solution)/shard_map/ppermute | solution.py:10
  124.9 4.6 %collective-permute-start.6 = (bf16[16,128]{0,1:T(8,128)(2,1)S(1)}, bf16[16,128]{0,1:T(8,128)(2,1)S(1)}, u32[]{:S(2)}, u32[]{:S(2)}) collective-permute-start(bf16[16,128]{0,1:T(8,128)(2,1)S(1)} %all_gather.50), channel_id=1, source_target_pairs={{0,8},{8,0},{16,24},{24,16},{32,40},{40,32},{48,56},{56,48},{64,72... | collective-permute-start | bytes 12296 | tf_op jit(solution)/shard_map/ppermute | solution.py:10
  129.7 5.3 %collective-permute-start.7 = (bf16[16,256]{1,0:T(8,128)(2,1)S(1)}, bf16[16,256]{1,0:T(8,128)(2,1)S(1)}, u32[]{:S(2)}, u32[]{:S(2)}) collective-permute-start(bf16[16,256]{1,0:T(8,128)(2,1)S(1)} %maximum_select_fusion.26), channel_id=1, source_target_pairs={{0,16},{8,24},{16,0},{24,8},{32,48},{40,56},{48,32},{56,40},{64,80... | collective-permute-start | bytes 24584 | tf_op jit(solution)/shard_map/ppermute | solution.py:10
  135.0 8.5 %collective-permute-start.8 = (bf16[16,512]{1,0:T(8,128)(2,1)S(1)}, bf16[16,512]{1,0:T(8,128)(2,1)S(1)}, u32[]{:S(2)}, u32[]{:S(2)}) collective-permute-start(bf16[16,512]{1,0:T(8,128)(2,1)S(1)} %maximum_select_fusion.14), channel_id=1, source_target_pairs={{0,32},{8,40},{16,48},{24,56},{32,0},{40,8},{48,16},{56,24},{64,96... | collective-permute-start | bytes 49160 | tf_op jit(solution)/shard_map/ppermute | solution.py:10
  159.8 4.6 %collective-permute-start.9 = (bf16[16,128]{0,1:T(8,128)(2,1)S(1)}, bf16[16,128]{0,1:T(8,128)(2,1)S(1)}, u32[]{:S(2)}, u32[]{:S(2)}) collective-permute-start(bf16[16,128]{0,1:T(8,128)(2,1)S(1)} %all_gather.51), channel_id=1, source_target_pairs={{0,8},{8,0},{16,24},{24,16},{32,40},{40,32},{48,56},{56,48},{64,72... | collective-permute-start | bytes 12296 | tf_op jit(solution)/shard_map/ppermute | solution.py:10
  164.5 5.3 %collective-permute-start.10 = (bf16[16,256]{1,0:T(8,128)(2,1)S(1)}, bf16[16,256]{1,0:T(8,128)(2,1)S(1)}, u32[]{:S(2)}, u32[]{:S(2)}) collective-permute-start(bf16[16,256]{1,0:T(8,128)(2,1)S(1)} %maximum_select_fusion.27), channel_id=1, source_target_pairs={{0,16},{8,24},{16,0},{24,8},{32,48},{40,56},{48,32},{56,40},{64,80... | collective-permute-start | bytes 24584 | tf_op jit(solution)/shard_map/ppermute | solution.py:10
  169.9 8.5 %collective-permute-start.11 = (bf16[16,512]{1,0:T(8,128)(2,1)S(1)}, bf16[16,512]{1,0:T(8,128)(2,1)S(1)}, u32[]{:S(2)}, u32[]{:S(2)}) collective-permute-start(bf16[16,512]{1,0:T(8,128)(2,1)S(1)} %maximum_select_fusion.15), channel_id=1, source_target_pairs={{0,32},{8,40},{16,48},{24,56},{32,0},{40,8},{48,16},{56,24},{64,96... | collective-permute-start | bytes 49160 | tf_op jit(solution)/shard_map/ppermute | solution.py:10
  194.7 4.8 %collective-permute-start.12 = (bf16[16,128]{0,1:T(8,128)(2,1)S(1)}, bf16[16,128]{0,1:T(8,128)(2,1)S(1)}, u32[]{:S(2)}, u32[]{:S(2)}) collective-permute-start(bf16[16,128]{0,1:T(8,128)(2,1)S(1)} %all_gather.52), channel_id=1, source_target_pairs={{0,8},{8,0},{16,24},{24,16},{32,40},{40,32},{48,56},{56,48},{64,72... | collective-permute-start | bytes 12296 | tf_op jit(solution)/shard_map/ppermute | solution.py:10
  199.6 5.3 %collective-permute-start.13 = (bf16[16,256]{1,0:T(8,128)(2,1)S(1)}, bf16[16,256]{1,0:T(8,128)(2,1)S(1)}, u32[]{:S(2)}, u32[]{:S(2)}) collective-permute-start(bf16[16,256]{1,0:T(8,128)(2,1)S(1)} %maximum_select_fusion.28), channel_id=1, source_target_pairs={{0,16},{8,24},{16,0},{24,8},{32,48},{40,56},{48,32},{56,40},{64,80... | collective-permute-start | bytes 24584 | tf_op jit(solution)/shard_map/ppermute | solution.py:10
  204.9 8.5 %collective-permute-start.14 = (bf16[16,512]{1,0:T(8,128)(2,1)S(1)}, bf16[16,512]{1,0:T(8,128)(2,1)S(1)}, u32[]{:S(2)}, u32[]{:S(2)}) collective-permute-start(bf16[16,512]{1,0:T(8,128)(2,1)S(1)} %maximum_select_fusion.16), channel_id=1, source_target_pairs={{0,32},{8,40},{16,48},{24,56},{32,0},{40,8},{48,16},{56,24},{64,96... | collective-permute-start | bytes 49160 | tf_op jit(solution)/shard_map/ppermute | solution.py:10
  229.7 4.6 %collective-permute-start.15 = (bf16[16,128]{0,1:T(8,128)(2,1)S(1)}, bf16[16,128]{0,1:T(8,128)(2,1)S(1)}, u32[]{:S(2)}, u32[]{:S(2)}) collective-permute-start(bf16[16,128]{0,1:T(8,128)(2,1)S(1)} %all_gather.53), channel_id=1, source_target_pairs={{0,8},{8,0},{16,24},{24,16},{32,40},{40,32},{48,56},{56,48},{64,72... | collective-permute-start | bytes 12296 | tf_op jit(solution)/shard_map/ppermute | solution.py:10
  234.5 5.3 %collective-permute-start.16 = (bf16[16,256]{1,0:T(8,128)(2,1)S(1)}, bf16[16,256]{1,0:T(8,128)(2,1)S(1)}, u32[]{:S(2)}, u32[]{:S(2)}) collective-permute-start(bf16[16,256]{1,0:T(8,128)(2,1)S(1)} %maximum_select_fusion.29), channel_id=1, source_target_pairs={{0,16},{8,24},{16,0},{24,8},{32,48},{40,56},{48,32},{56,40},{64,80... | collective-permute-start | bytes 24584 | tf_op jit(solution)/shard_map/ppermute | solution.py:10
  239.8 8.5 %collective-permute-start.17 = (bf16[16,512]{1,0:T(8,128)(2,1)S(1)}, bf16[16,512]{1,0:T(8,128)(2,1)S(1)}, u32[]{:S(2)}, u32[]{:S(2)}) collective-permute-start(bf16[16,512]{1,0:T(8,128)(2,1)S(1)} %maximum_select_fusion.17), channel_id=1, source_target_pairs={{0,32},{8,40},{16,48},{24,56},{32,0},{40,8},{48,16},{56,24},{64,96... | collective-permute-start | bytes 49160 | tf_op jit(solution)/shard_map/ppermute | solution.py:10
  264.6 4.6 %collective-permute-start.18 = (bf16[16,128]{0,1:T(8,128)(2,1)S(1)}, bf16[16,128]{0,1:T(8,128)(2,1)S(1)}, u32[]{:S(2)}, u32[]{:S(2)}) collective-permute-start(bf16[16,128]{0,1:T(8,128)(2,1)S(1)} %all_gather.54), channel_id=1, source_target_pairs={{0,8},{8,0},{16,24},{24,16},{32,40},{40,32},{48,56},{56,48},{64,72... | collective-permute-start | bytes 12296 | tf_op jit(solution)/shard_map/ppermute | solution.py:10
  269.4 5.3 %collective-permute-start.19 = (bf16[16,256]{1,0:T(8,128)(2,1)S(1)}, bf16[16,256]{1,0:T(8,128)(2,1)S(1)}, u32[]{:S(2)}, u32[]{:S(2)}) collective-permute-start(bf16[16,256]{1,0:T(8,128)(2,1)S(1)} %maximum_select_fusion.30), channel_id=1, source_target_pairs={{0,16},{8,24},{16,0},{24,8},{32,48},{40,56},{48,32},{56,40},{64,80... | collective-permute-start | bytes 24584 | tf_op jit(solution)/shard_map/ppermute | solution.py:10
  290.0 4.6 %collective-permute-start.20 = (bf16[16,128]{0,1:T(8,128)(2,1)S(1)}, bf16[16,128]{0,1:T(8,128)(2,1)S(1)}, u32[]{:S(2)}, u32[]{:S(2)}) collective-permute-start(bf16[16,128]{0,1:T(8,128)(2,1)S(1)} %all_gather.55), channel_id=1, source_target_pairs={{0,8},{8,0},{16,24},{24,16},{32,40},{40,32},{48,56},{56,48},{64,72... | collective-permute-start | bytes 12296 | tf_op jit(solution)/shard_map/ppermute | solution.py:10
  294.7 5.4 %collective-permute-start.21 = (bf16[16,256]{1,0:T(8,128)(2,1)S(1)}, bf16[16,256]{1,0:T(8,128)(2,1)S(1)}, u32[]{:S(2)}, u32[]{:S(2)}) collective-permute-start(bf16[16,256]{1,0:T(8,128)(2,1)S(1)} %maximum_select_fusion.31), channel_id=1, source_target_pairs={{0,16},{8,24},{16,0},{24,8},{32,48},{40,56},{48,32},{56,40},{64,80... | collective-permute-start | bytes 24584 | tf_op jit(solution)/shard_map/ppermute | solution.py:10
  315.5 4.6 %collective-permute-start.22 = (bf16[16,128]{0,1:T(8,128)(2,1)S(1)}, bf16[16,128]{0,1:T(8,128)(2,1)S(1)}, u32[]{:S(2)}, u32[]{:S(2)}) collective-permute-start(bf16[16,128]{0,1:T(8,128)(2,1)S(1)} %all_gather.56), channel_id=1, source_target_pairs={{0,8},{8,0},{16,24},{24,16},{32,40},{40,32},{48,56},{56,48},{64,72... | collective-permute-start | bytes 12296 | tf_op jit(solution)/shard_map/ppermute | solution.py:10
  334.4 4.6 %collective-permute-start.23 = (bf16[16,128]{0,1:T(8,128)(2,1)S(1)}, bf16[16,128]{0,1:T(8,128)(2,1)S(1)}, u32[]{:S(2)}, u32[]{:S(2)}) collective-permute-start(bf16[16,128]{0,1:T(8,128)(2,1)S(1)} %all_gather.57), channel_id=1, source_target_pairs={{0,8},{8,0},{16,24},{24,16},{32,40},{40,32},{48,56},{56,48},{64,72... | collective-permute-start | bytes 12296 | tf_op jit(solution)/shard_map/ppermute | solution.py:10
  (10 other events, 180.0 us)
where the time goes:
time: 373 us; the launch traced here: 372 us
  blocking collectives  223 us (60%)
  waiting for transfers between devices  73.5 us (20%)
  starting transfers between devices  57.7 us (15%)
  local copies, waits for them, and re-layouts  14.2 us (4%)
    all_gather x11, blocking collectives, paired_vector(): joined = lax.all_gather(own_piece, 'front', axis=1, tiled=True)  167 us
    ppermute x24, waiting for transfers between devices, swapped(): lax.ppermute(x, axis, [(i, i ^ 1 << stride) for i in range(lax.axis_size(...  73.5 us
    ppermute x24, starting transfers between devices, swapped(): lax.ppermute(x, axis, [(i, i ^ 1 << stride) for i in range(lax.axis_size(...  57.7 us
    all_gather x2, blocking collectives, section_vector(): return lax.all_gather(own_piece, 'front', axis=1, tiled=True)  23.8 us
    all_gather x1, blocking collectives, local(): grouped = lax.all_gather(basis, 'front', axis=1, tiled=True)  19.4 us
    all_gather x1, blocking collectives, local(): everyone = lax.all_gather(solved, 'front', axis=1, tiled=True)  12.9 us
  transfers between devices with their start and end apart: 24, of which 24 were waited for; matrix products, arithmetic and copies ran while one was open for 0% of the time, Pallas kernels for 0%

commit v1 on v0

v1 whole, which is shorter than its diff:
```python
import jax
import jax.numpy as jnp
from jax import lax
from jax.sharding import Mesh, PartitionSpec as P

AXES = ("sub", "a", "b", "c", "front")
PAIR = ("c", "front")
PLANES4 = ("b", "c")
PLANES8 = ("a", "b", "c")
BF = jnp.bfloat16
WIDE = 256


def mm(x, w):
    return lax.dot_general(x, w, (((1,), (1,)), ((), ())), preferred_element_type=jnp.float32)


def exchange(x, axes):
    return lax.all_to_all(x, axes, 0, 0)


def spread(x, axes):
    size = lax.axis_size(axes)
    return exchange(jnp.broadcast_to(x[None], (size,) + x.shape), axes)


def total(parts):
    return jnp.sum(parts.astype(jnp.float32), axis=0)


def local(
    basis,
    order,
    leaf_inverse,
    leaf_upper_inverse,
    leaf_coupling_low,
    leaf_coupling_up,
    sep_lower_inverse,
    sep_upper_inverse,
    sep_coupling_low,
    sep_coupling_up,
):
    ia, ib, ic = (lax.axis_index(n) for n in ("a", "b", "c"))
    f = lax.axis_index("front")
    leaf = 4 * ia + 2 * ib + ic

    with jax.named_scope("gather_basis"):
        cols = jnp.pad(basis, ((0, 0), (0, WIDE - 176)))
        grouped = spread(cols, "front")

    with jax.named_scope("move_level1"):
        low = jnp.transpose(leaf_coupling_low.reshape(16, 16, 128), (1, 0, 2))
        a1 = jnp.broadcast_to(sep_lower_inverse[None, :, :256], (16, 16, 256))
        got = exchange(jnp.concatenate([low, a1], 2), PAIR)
        low_cols = got[:, :, :128].reshape(256, 128)
        a1 = got[:, :, 128:].reshape(256, 256)

    with jax.named_scope("move_level2"):
        g2 = jnp.transpose(sep_coupling_low[:, :512].reshape(16, 2, 256), (1, 0, 2))
        g2 = jnp.broadcast_to(g2[:, None], (2, 2, 16, 256)).reshape(4, 16, 256)
        a2 = jnp.broadcast_to(sep_lower_inverse[None, :, 256:768], (4, 16, 512))
        got = exchange(jnp.concatenate([g2, a2], 2), PLANES4)
        got = lax.all_gather(got, "front", axis=1).reshape(512, 768)
        g2 = got[:, :256]
        a2 = got[:, 256:]

    with jax.named_scope("move_level3"):
        g3 = jnp.transpose(sep_coupling_low[:, 512:].reshape(16, 2, 512), (1, 0, 2))
        g3 = jnp.broadcast_to(g3[:, None], (2, 4, 16, 512)).reshape(8, 16, 512)
        g3 = exchange(g3, PLANES8).reshape(128, 512)

        def by_front(m):
            return jnp.transpose(m.reshape(16, 8, 8, 16), (2, 0, 1, 3)).reshape(8, 16, 128)

        a3 = by_front(sep_lower_inverse[:, 768:])
        h2 = by_front(sep_coupling_up[:, 512:])
        up = jnp.transpose(leaf_upper_inverse.reshape(128, 8, 128), (1, 0, 2))
        got = exchange(jnp.concatenate([a3, h2, up], 1), "front")
        a3 = got[:, :16].reshape(128, 128)
        h2 = got[:, 16:32].reshape(128, 128)
        up = got[:, 32:].reshape(1024, 128)
        a3 = spread(a3, PLANES8).reshape(1024, 128)
        b3 = spread(sep_upper_inverse[:, 768:], PLANES8).reshape(128, 1024)
        h2 = spread(h2, PLANES4).reshape(512, 128)

    with jax.named_scope("move_down"):
        down = jnp.concatenate([sep_upper_inverse[:, :768], sep_coupling_up[:, :512]], 1)
        got = spread(down, PLANES4).reshape(2, 2, 16, 1280)
        mine = lax.dynamic_index_in_dim(got, ib, 0, keepdims=False)
        b2 = lax.all_gather(got[:, :, :, 256:768].reshape(4, 16, 512), "front", axis=1).reshape(512, 512)
        mine = jnp.concatenate([mine[:, :, :256], mine[:, :, 768:]], 2)
        mine = lax.all_gather(mine, "front", axis=1).reshape(256, 768)
        b1 = mine[:, :256]
        h1 = mine[:, 256:]

    with jax.named_scope("order"):
        place = (order[0] // 176) * WIDE + order[0] % 176
        slots = place.reshape(8, 176)
        leaf_place = slots[:, :128].reshape(1024)
        own_place = lax.dynamic_index_in_dim(slots, f, 0, keepdims=False)[128:]
        wide = 8 * WIDE
        hot = (leaf_place[:, None] == lax.broadcasted_iota(jnp.int32, (1024, wide), 1)).astype(BF)
        own_hot = (own_place[:, None] == lax.broadcasted_iota(jnp.int32, (48, wide), 1)).astype(BF)
        lower = lax.dot_general(leaf_inverse, hot, (((1,), (0,)), ((), ())), preferred_element_type=jnp.float32)
        lower = jnp.concatenate([lower.astype(BF), own_hot], 0)
        upper = lax.dot_general(hot, up, (((0,), (0,)), ((), ())), preferred_element_type=jnp.float32)
        upper = jnp.concatenate([upper.astype(BF), own_hot.T], 1)

    with jax.named_scope("weights1"):
        row = lax.broadcasted_iota(jnp.int32, (384, 48), 0)
        col = lax.broadcasted_iota(jnp.int32, (384, 48), 1)
        target = jnp.where(col < 16, (ic * 8 + f) * 16 + col, 240 + col)
        keep = (row == target).astype(BF)
        first = jnp.concatenate([jnp.pad(-low_cols, ((0, 128), (0, 0))), keep], 1)

    with jax.named_scope("leaf_lower"):
        grouped = jnp.transpose(grouped, (1, 0, 2)).reshape(16, wide)
        own = mm(grouped, lower).astype(BF)
        y_leaf = own[:, :128]

    with jax.named_scope("level1_up"):
        got = spread(mm(own, first).astype(BF), PAIR)
        c1 = total(got[:, :, :256]).astype(BF)
        rest = jnp.transpose(got[:, :, 256:288], (1, 0, 2))
        rhs2 = rest[:, :, :16].reshape(16, 256)
        rhs3 = lax.dynamic_index_in_dim(rest.reshape(16, 2, 8, 32)[:, :, :, 16:], f, 2, keepdims=False).reshape(16, 32)
        y1 = mm(c1, a1).astype(BF)

    with jax.named_scope("level2_up"):
        half = lax.broadcasted_iota(jnp.int32, (16, 512), 1) // 256
        part = jnp.where(half == ib, jnp.concatenate([rhs2, rhs2], 1).astype(jnp.float32), 0.0) - mm(y1, g2)
        part = jnp.concatenate([part.astype(BF), jnp.pad(rhs3, ((0, 0), (0, 96)))], 1)
        got = lax.all_gather(part, "b")
        c2 = total(got[:, :, :512]).astype(BF)
        rhs3 = jnp.transpose(got[:, :, 512:544], (1, 0, 2)).reshape(16, 64)
        y2 = mm(c2, a2).astype(BF)

    with jax.named_scope("level3_up"):
        half = lax.broadcasted_iota(jnp.int32, (16, 128), 1) // 64
        part = jnp.where(half == ia, jnp.concatenate([rhs3, rhs3], 1).astype(jnp.float32), 0.0) - mm(y2, g3)
        c3 = total(lax.all_gather(part.astype(BF), "a")).astype(BF)
        y3 = total(spread(mm(c3, a3).astype(BF), "front")).astype(BF)

    with jax.named_scope("level3_down"):
        z3 = mm(y3, b3).astype(BF)
        got = spread(mm(z3, h2).astype(BF), "front")
        w2 = (y2.astype(jnp.float32) - total(got)).astype(BF)

    with jax.named_scope("local_down"):
        z2 = mm(w2, b2).astype(BF)
        w1 = (y1.astype(jnp.float32) - mm(z2, h1)).astype(BF)
        z1 = mm(w1, b1).astype(BF)
        w_leaf = (y_leaf.astype(jnp.float32) - mm(z1, leaf_coupling_up)).astype(BF)
        own = jnp.concatenate(
            [
                w_leaf,
                lax.dynamic_slice_in_dim(z1, (ic * 8 + f) * 16, 16, 1),
                lax.dynamic_slice_in_dim(z2, ((2 * ib + ic) * 8 + f) * 16, 16, 1),
                lax.dynamic_slice_in_dim(z3, leaf * 16, 16, 1),
            ],
            1,
        )

    with jax.named_scope("leaf_upper"):
        out = mm(own, upper).astype(BF)
        out = jnp.transpose(out.reshape(16, 8, WIDE), (1, 0, 2))
        return total(exchange(out, "front"))[:, :176].astype(BF)


def solution(mesh):
    fronts = mesh.shape["front"]
    grid = Mesh(mesh.devices.reshape(-1, 2, 2, 2, fronts), AXES)
    rows = P(AXES, None)
    in_specs = (P(None, AXES), P(AXES[:4], None)) + (rows,) * 8
    return jax.shard_map(local, mesh=grid, in_specs=in_specs, out_specs=P(None, AXES), check_vma=False)
```

time: 373 us -> 204 us (0.55)
  blocking collectives: 223 us -> 64.8 us
  waiting for transfers between devices: 73.5 us -> 42.4 us
  starting transfers between devices: 57.7 us -> 72.4 us
  matrix products: 1.88 us -> 6.39 us
    all_gather x15 -> x5, blocking collectives: 223 us -> 56.3 us  [the longest x1 15.2 us: local(): lax.all_gather(got[:, :, :, 256:768].reshape(4, 16, 512), 'front', axis=1)]
    ppermute x24 -> x0, waiting for transfers between devices: 73.5 us -> none  [swapped(): lax.ppermute(x, axis, [(i, i ^ 1 << stride) for i in range(lax.axis_size(...]
    all_to_all x0 -> x12, starting transfers between devices: none -> 72.4 us  [exchange(): return lax.all_to_all(x, axes, 0, 0)]
    ppermute x24 -> x0, starting transfers between devices: 57.7 us -> none  [swapped(): lax.ppermute(x, axis, [(i, i ^ 1 << stride) for i in range(lax.axis_size(...]
    all_to_all x0 -> x12, waiting for transfers between devices: none -> 42.4 us  [exchange(): return lax.all_to_all(x, axes, 0, 0)]
    all_to_all x0 -> x1, blocking collectives: none -> 8.48 us  [exchange(): return lax.all_to_all(x, axes, 0, 0)]
    scatter x1 -> x0, local copies, waits for them, and re-layouts: 6.41 us -> none  [local(): placed = jnp.zeros_like(everyone).at[:, order[0]].set(everyone)]
    broadcast_in_dim x0 -> x12, local copies, waits for them, and re-layouts: none -> 6.21 us  [the longest x8 5.53 us: spread(): return exchange(jnp.broadcast_to(x[None], (size,) + x.shape), axes)]
  transfers between devices with their start and end apart: 24 -> 12, of which waited for: 24 -> 8; matrix products, arithmetic and copies ran while one was open for 0% -> 6% of each run, Pallas kernels for 0% -> 0%
where the time goes in v1:
time: 204 us; the launch traced here: 202 us
  starting transfers between devices  72.4 us (35%)
  blocking collectives  64.8 us (32%)
  waiting for transfers between devices  42.4 us (21%)
  local copies, waits for them, and re-layouts  11.3 us (6%)
  matrix products  6.39 us (3%)
  other arithmetic  4.3 us (2%)
    all_to_all x12, starting transfers between devices, exchange(): return lax.all_to_all(x, axes, 0, 0)  72.4 us
    all_to_all x12, waiting for transfers between devices, exchange(): return lax.all_to_all(x, axes, 0, 0)  42.4 us
    all_gather x1, blocking collectives, local(): lax.all_gather(got[:, :, :, 256:768].reshape(4, 16, 512), 'front', axis=1)  15.2 us
    all_gather x1, blocking collectives, local(): got = lax.all_gather(got, 'front', axis=1).reshape(512, 768)  14.1 us
    all_gather x1, blocking collectives, local(): mine = lax.all_gather(mine, 'front', axis=1).reshape(256, 768)  13.8 us
    all_gather x1, blocking collectives, local(): c3 = total(lax.all_gather(part.astype(BF), 'a')).astype(BF)  8.91 us
    all_to_all x1, blocking collectives, exchange(): return lax.all_to_all(x, axes, 0, 0)  8.48 us
    broadcast_in_dim x8, local copies, waits for them, and re-layouts, spread(): return exchange(jnp.broadcast_to(x[None], (size,) + x.shape), axes)  5.53 us
  transfers between devices with their start and end apart: 12, of which 8 were waited for; matrix products, arithmetic and copies ran while one was open for 6% of the time, Pallas kernels for 0%

profile of v1, /device:TPU:1, one launch (start us, length us, event | category | flops | bytes accessed | tf_op | source)
XLA Modules:
  0.0 202.1 jit_solution(6708307797923921404)
XLA Ops:
  1.4 10.1 %all-to-all-start = ((bf16[8,16,256]{2,1,0:T(8,128)(2,1)}), bf16[8,16,256]{2,1,0:T(8,128)(2,1)S(1)}, u32[]{:S(2)}, u32[]{:S(2)}) async-start(bf16[8,16,256]{2,1,0:T(8,128)(2,1)} %broadcast_in_dim.34), calls=%async_computation | async-start | bytes 131072 | tf_op jit(solution)/shard_map/gather_basis/all_to_all | solution.py:19
  18.4 4.8 %all-to-all-start.5 = ((bf16[8,160,128]{2,1,0:T(8,128)(2,1)}), bf16[8,160,128]{2,1,0:T(8,128)(2,1)S(1)}, u32[]{:S(2)}, u32[]{:S(2)}) async-start(bf16[8,160,128]{2,1,0:T(8,128)(2,1)} %copy.57), calls=%async_computation.5 | async-start | bytes 655360 | tf_op jit(solution)/shard_map/move_level3/all_to_all | solution.py:19
  23.3 7.1 %all-to-all-done.5 = bf16[8,160,128]{2,1,0:T(8,128)(2,1)S(1)} async-done(((bf16[8,160,128]{2,1,0:T(8,128)(2,1)}), bf16[8,160,128]{2,1,0:T(8,128)(2,1)S(1)}, u32[]{:S(2)}, u32[]{:S(2)}) %all-to-all-start.5) | async-done | bytes 327712 | tf_op jit(solution)/shard_map/move_level3/all_to_all | solution.py:19
  33.8 4.6 %all-to-all-done.3 = bf16[4,16,768]{2,1,0:T(8,128)(2,1)S(1)} async-done(((bf16[4,16,768]{2,1,0:T(8,128)(2,1)}), bf16[4,16,768]{2,1,0:T(8,128)(2,1)S(1)}, u32[]{:S(2)}, u32[]{:S(2)}) %all-to-all-start.3) | async-done | bytes 98336 | tf_op jit(solution)/shard_map/move_level2/all_to_all | solution.py:19
  39.1 7.1 %all-to-all-start.4 = ((bf16[8,16,512]{2,1,0:T(8,128)(2,1)}), bf16[8,16,512]{2,1,0:T(8,128)(2,1)S(1)}, u32[]{:S(2)}, u32[]{:S(2)}) async-start(bf16[8,16,512]{2,1,0:T(8,128)(2,1)} %bitcast.15), calls=%async_computation.4 | async-start | bytes 262144 | tf_op jit(solution)/shard_map/move_level3/all_to_all | solution.py:19
  46.3 10.1 %all-to-all-done.4 = bf16[8,16,512]{2,1,0:T(8,128)(2,1)S(1)} async-done(((bf16[8,16,512]{2,1,0:T(8,128)(2,1)}), bf16[8,16,512]{2,1,0:T(8,128)(2,1)S(1)}, u32[]{:S(2)}, u32[]{:S(2)}) %all-to-all-start.4) | async-done | bytes 131104 | tf_op jit(solution)/shard_map/move_level3/all_to_all | solution.py:19
  56.4 7.0 %all-to-all-start.1 = ((bf16[16,16,384]{2,1,0:T(8,128)(2,1)}), bf16[16,16,384]{2,1,0:T(8,128)(2,1)S(1)}, u32[]{:S(2)}, u32[]{:S(2)}) async-start(bf16[16,16,384]{2,1,0:T(8,128)(2,1)} %pad_maximum_fusion.1), calls=%async_computation.1 | async-start | bytes 393216 | tf_op jit(solution)/shard_map/move_level1/all_to_all | solution.py:19
  65.4 4.8 %all-to-all-done.1 = bf16[16,16,384]{2,1,0:T(8,128)(2,1)S(1)} async-done(((bf16[16,16,384]{2,1,0:T(8,128)(2,1)}), bf16[16,16,384]{2,1,0:T(8,128)(2,1)S(1)}, u32[]{:S(2)}, u32[]{:S(2)}) %all-to-all-start.1) | async-done | bytes 196640 | tf_op jit(solution)/shard_map/move_level1/all_to_all | solution.py:19
  70.9 3.3 %all-to-all-start.11 = ((bf16[4,16,1280]{2,1,0:T(8,128)(2,1)}), bf16[4,16,1280]{2,1,0:T(8,128)(2,1)S(1)}, u32[]{:S(2)}, u32[]{:S(2)}) async-start(bf16[4,16,1280]{2,1,0:T(8,128)(2,1)} %broadcast_in_dim.98), calls=%async_computation.11 | async-start | bytes 327680 | tf_op jit(solution)/shard_map/move_down/all_to_all | solution.py:19
  74.7 4.4 %all-to-all-done.11 = bf16[4,16,1280]{2,1,0:T(8,128)(2,1)S(1)} async-done(((bf16[4,16,1280]{2,1,0:T(8,128)(2,1)}), bf16[4,16,1280]{2,1,0:T(8,128)(2,1)S(1)}, u32[]{:S(2)}, u32[]{:S(2)}) %all-to-all-start.11) | async-done | bytes 163872 | tf_op jit(solution)/shard_map/move_down/all_to_all | solution.py:19
  79.8 5.7 %all-to-all-start.2 = ((bf16[16,16,384]{2,1,0:T(8,128)(2,1)}), bf16[16,16,384]{2,1,0:T(8,128)(2,1)S(1)}, u32[]{:S(2)}, u32[]{:S(2)}) async-start(bf16[16,16,384]{2,1,0:T(8,128)(2,1)} %broadcast_in_dim.36), calls=%async_computation.2 | async-start | bytes 393216 | tf_op jit(solution)/shard_map/level1_up/all_to_all | solution.py:19
  87.5 4.8 %all-to-all-done.2 = bf16[16,16,384]{2,1,0:T(8,128)(2,1)S(1)} async-done(((bf16[16,16,384]{2,1,0:T(8,128)(2,1)}), bf16[16,16,384]{2,1,0:T(8,128)(2,1)S(1)}, u32[]{:S(2)}, u32[]{:S(2)}) %all-to-all-start.2) | async-done | bytes 196640 | tf_op jit(solution)/shard_map/level1_up/all_to_all | solution.py:19
  93.0 3.4 %all-to-all-start.6 = ((bf16[8,128,128]{2,1,0:T(8,128)(2,1)}), bf16[8,128,128]{2,1,0:T(8,128)(2,1)S(1)}, u32[]{:S(2)}, u32[]{:S(2)}) async-start(bf16[8,128,128]{2,1,0:T(8,128)(2,1)} %broadcast_in_dim.45), calls=%async_computation.6 | async-start | bytes 524288 | tf_op jit(solution)/shard_map/move_level3/all_to_all | solution.py:19
  96.4 14.1 %all-gather = bf16[4,128,768]{2,1,0:T(8,128)(2,1)S(1)} all-gather(bf16[4,16,768]{2,1,0:T(8,128)(2,1)S(1)} %all-to-all-done.3), channel_id=2, replica_groups=mesh['sub'=8,'a'=2,'b'=2,'c'=2,'front'=8] {'front'}, dimensions={1}, use_global_device_ids=true | all-gather | bytes 884736 | tf_op jit(solution)/shard_map/move_level2/all_gather | solution.py:63
  111.4 4.3 %all-gather.1 = bf16[32,640]{1,0:T(8,128)(2,1)S(1)} all-gather(bf16[16,640]{1,0:T(8,128)(2,1)S(1)} %fusion.33), channel_id=3, replica_groups=mesh['sub'=8,'a'=2,'b'=2,'c'=2,'front'=8] {'b'}, dimensions={0}, use_global_device_ids=true | all-gather | bytes 61440 | tf_op jit(solution)/shard_map/level2_up/all_gather | solution.py:133
  116.5 9.6 %all-to-all-start.8 = ((bf16[8,16,1024]{2,1,0:T(8,128)(2,1)}), bf16[8,16,1024]{2,1,0:T(8,128)(2,1)S(1)}, u32[]{:S(2)}, u32[]{:S(2)}) async-start(bf16[8,16,1024]{2,1,0:T(8,128)(2,1)} %broadcast_in_dim.47), calls=%async_computation.8 | async-start | bytes 524288 | tf_op jit(solution)/shard_map/move_level3/all_to_all | solution.py:19
  126.6 8.9 %all-gather.2 = bf16[32,128]{1,0:T(8,128)(2,1)S(1)} all-gather(bf16[16,128]{1,0:T(8,128)(2,1)S(1)} %fusion.9), channel_id=4, replica_groups=mesh['sub'=8,'a'=2,'b'=2,'c'=2,'front'=8] {'a'}, dimensions={0}, use_global_device_ids=true | all-gather | bytes 12288 | tf_op jit(solution)/shard_map/level3_up/all_gather | solution.py:141
  138.4 9.6 %all-to-all-start.7 = ((bf16[8,16,1024]{2,1,0:T(8,128)(2,1)}), bf16[8,16,1024]{2,1,0:T(8,128)(2,1)S(1)}, u32[]{:S(2)}, u32[]{:S(2)}) async-start(bf16[8,16,1024]{2,1,0:T(8,128)(2,1)} %broadcast_in_dim.46), calls=%async_computation.7 | async-start | bytes 524288 | tf_op jit(solution)/shard_map/level3_up/all_to_all | solution.py:19
  148.0 15.2 %all_gather.33 = bf16[4,8,16,512]{3,2,1,0:T(8,128)(2,1)S(1)} all-gather(bf16[4,1,16,512]{3,2,1,0:T(8,128)(2,1)S(1)} %bitcast.99), channel_id=1, replica_groups=mesh['sub'=8,'a'=2,'b'=2,'c'=2,'front'=8] {'front'}, dimensions={1}, use_global_device_ids=true | all-gather | bytes 589824 | tf_op jit(solution)/shard_map/move_down/all_gather | solution.py:90
  163.8 3.3 %all-to-all-start.9 = ((bf16[4,128,128]{2,1,0:T(8,128)(2,1)}), bf16[4,128,128]{2,1,0:T(8,128)(2,1)S(1)}, u32[]{:S(2)}, u32[]{:S(2)}) async-start(bf16[4,128,128]{2,1,0:T(8,128)(2,1)} %broadcast_in_dim.49), calls=%async_computation.9 | async-start | bytes 262144 | tf_op jit(solution)/shard_map/move_level3/all_to_all | solution.py:19
  167.4 4.6 %all-to-all-done.9 = bf16[4,128,128]{2,1,0:T(8,128)(2,1)S(1)} async-done(((bf16[4,128,128]{2,1,0:T(8,128)(2,1)}), bf16[4,128,128]{2,1,0:T(8,128)(2,1)S(1)}, u32[]{:S(2)}, u32[]{:S(2)}) %all-to-all-start.9) | async-done | bytes 131104 | tf_op jit(solution)/shard_map/move_level3/all_to_all | solution.py:19
  172.8 5.1 %all-to-all-start.10 = ((bf16[8,16,512]{2,1,0:T(8,128)(2,1)}), bf16[8,16,512]{2,1,0:T(8,128)(2,1)S(1)}, u32[]{:S(2)}, u32[]{:S(2)}) async-start(bf16[8,16,512]{2,1,0:T(8,128)(2,1)} %broadcast_in_dim.50), calls=%async_computation.10 | async-start | bytes 262144 | tf_op jit(solution)/shard_map/level3_down/all_to_all | solution.py:19
  177.8 13.8 %all-gather.3 = bf16[2,128,768]{2,1,0:T(8,128)(2,1)S(1)} all-gather(bf16[2,16,768]{2,1,0:T(8,128)(2,1)S(1)} %pad_maximum_fusion.3), channel_id=5, replica_groups=mesh['sub'=8,'a'=2,'b'=2,'c'=2,'front'=8] {'front'}, dimensions={1}, use_global_device_ids=true | all-gather | bytes 442368 | tf_op jit(solution)/shard_map/move_down/all_gather | solution.py:92
  193.0 8.5 %all_to_all.65 = bf16[8,16,256]{2,1,0:T(8,128)(2,1)S(1)} all-to-all(bf16[8,16,256]{2,1,0:T(8,128)(2,1)S(1)} %bitcast.102), channel_id=1, replica_groups=mesh['sub'=8,'a'=2,'b'=2,'c'=2,'front'=8] {'front'}, dimensions={0} | all-to-all | bytes 131072 | tf_op jit(solution)/shard_map/leaf_upper/all_to_all | solution.py:19
  (121 shorter events, 27.3 us)
Async XLA Ops:
  0.0 63.5 %copy-start = (bf16[128,1024]{1,0:T(8,128)(2,1)S(1)}, bf16[128,1024]{1,0:T(8,128)(2,1)}, u32[]{:S(2)}) copy-start(bf16[128,1024]{1,0:T(8,128)(2,1)} %param.12) | copy-start | bytes 786436
  0.0 14.3 %slice-start.6 = ((bf16[16,1792]{1,0:T(8,128)(2,1)}), bf16[16,1024]{1,0:T(8,128)(2,1)S(1)}, s32[]{:S(2)}) async-start(bf16[16,1792]{1,0:T(8,128)(2,1)} %param.16), calls=%async_computation.19 | async-start | bytes 65536 | tf_op jit(solution)/shard_map/move_level3/slice | solution.py:75
  0.0 14.2 %slice-start.7 = ((bf16[16,1536]{1,0:T(8,128)(2,1)}), bf16[16,512]{1,0:T(8,128)(2,1)S(1)}, s32[]{:S(2)}) async-start(bf16[16,1536]{1,0:T(8,128)(2,1)} %param.18), calls=%async_computation.20 | async-start | bytes 32768 | tf_op jit(solution)/shard_map/move_level2/slice | solution.py:59
  0.0 14.2 %slice-start.8 = ((bf16[16,1536]{1,0:T(8,128)(2,1)}), bf16[16,1024]{1,0:T(8,128)(2,1)S(1)}, s32[]{:S(2)}) async-start(bf16[16,1536]{1,0:T(8,128)(2,1)} %param.18), calls=%async_computation.21 | async-start | bytes 65536 | tf_op jit(solution)/shard_map/move_level3/slice | solution.py:68
  1.4 17.0 %all-to-all-start = ((bf16[8,16,256]{2,1,0:T(8,128)(2,1)}), bf16[8,16,256]{2,1,0:T(8,128)(2,1)S(1)}, u32[]{:S(2)}, u32[]{:S(2)}) async-start(bf16[8,16,256]{2,1,0:T(8,128)(2,1)} %broadcast_in_dim.34), calls=%async_computation | async-start | bytes 131072 | tf_op jit(solution)/shard_map/gather_basis/all_to_all | solution.py:19
  13.0 1.9 slice-start.2
  14.3 1.2 copy-start.1
  15.7 1.4 slice-start.4
  16.1 1.7 slice-start.5
  17.1 6.2 %slice-start = ((bf16[16,1792]{1,0:T(8,128)(2,1)}), bf16[16,768]{1,0:T(8,128)(2,1)S(1)}, s32[]{:S(2)}) async-start(bf16[16,1792]{1,0:T(8,128)(2,1)} %param.17), calls=%async_computation.13 | async-start | bytes 49152 | tf_op jit(solution)/shard_map/move_down/slice | solution.py:87
  17.1 6.2 %slice-start.3 = ((bf16[16,1536]{1,0:T(8,128)(2,1)}), bf16[16,512]{1,0:T(8,128)(2,1)S(1)}, s32[]{:S(2)}) async-start(bf16[16,1536]{1,0:T(8,128)(2,1)} %param.19), calls=%async_computation.16 | async-start | bytes 32768 | tf_op jit(solution)/shard_map/move_down/slice | solution.py:87
  18.4 11.9 %all-to-all-start.5 = ((bf16[8,160,128]{2,1,0:T(8,128)(2,1)}), bf16[8,160,128]{2,1,0:T(8,128)(2,1)S(1)}, u32[]{:S(2)}, u32[]{:S(2)}) async-start(bf16[8,160,128]{2,1,0:T(8,128)(2,1)} %copy.57), calls=%async_computation.5 | async-start | bytes 655360 | tf_op jit(solution)/shard_map/move_level3/all_to_all | solution.py:19
  30.4 8.0 %all-to-all-start.3 = ((bf16[4,16,768]{2,1,0:T(8,128)(2,1)}), bf16[4,16,768]{2,1,0:T(8,128)(2,1)S(1)}, u32[]{:S(2)}, u32[]{:S(2)}) async-start(bf16[4,16,768]{2,1,0:T(8,128)(2,1)} %pad_maximum_fusion.2), calls=%async_computation.3 | async-start | bytes 196608 | tf_op jit(solution)/shard_map/move_level2/all_to_all | solution.py:19
  39.1 17.4 %all-to-all-start.4 = ((bf16[8,16,512]{2,1,0:T(8,128)(2,1)}), bf16[8,16,512]{2,1,0:T(8,128)(2,1)S(1)}, u32[]{:S(2)}, u32[]{:S(2)}) async-start(bf16[8,16,512]{2,1,0:T(8,128)(2,1)} %bitcast.15), calls=%async_computation.4 | async-start | bytes 262144 | tf_op jit(solution)/shard_map/move_level3/all_to_all | solution.py:19
  56.4 13.8 %all-to-all-start.1 = ((bf16[16,16,384]{2,1,0:T(8,128)(2,1)}), bf16[16,16,384]{2,1,0:T(8,128)(2,1)S(1)}, u32[]{:S(2)}, u32[]{:S(2)}) async-start(bf16[16,16,384]{2,1,0:T(8,128)(2,1)} %pad_maximum_fusion.1), calls=%async_computation.1 | async-start | bytes 393216 | tf_op jit(solution)/shard_map/move_level1/all_to_all | solution.py:19
  70.9 8.3 %all-to-all-start.11 = ((bf16[4,16,1280]{2,1,0:T(8,128)(2,1)}), bf16[4,16,1280]{2,1,0:T(8,128)(2,1)S(1)}, u32[]{:S(2)}, u32[]{:S(2)}) async-start(bf16[4,16,1280]{2,1,0:T(8,128)(2,1)} %broadcast_in_dim.98), calls=%async_computation.11 | async-start | bytes 327680 | tf_op jit(solution)/shard_map/move_down/all_to_all | solution.py:19
  79.8 12.4 %all-to-all-start.2 = ((bf16[16,16,384]{2,1,0:T(8,128)(2,1)}), bf16[16,16,384]{2,1,0:T(8,128)(2,1)S(1)}, u32[]{:S(2)}, u32[]{:S(2)}) async-start(bf16[16,16,384]{2,1,0:T(8,128)(2,1)} %broadcast_in_dim.36), calls=%async_computation.2 | async-start | bytes 393216 | tf_op jit(solution)/shard_map/level1_up/all_to_all | solution.py:19
  93.0 22.7 %all-to-all-start.6 = ((bf16[8,128,128]{2,1,0:T(8,128)(2,1)}), bf16[8,128,128]{2,1,0:T(8,128)(2,1)S(1)}, u32[]{:S(2)}, u32[]{:S(2)}) async-start(bf16[8,128,128]{2,1,0:T(8,128)(2,1)} %broadcast_in_dim.45), calls=%async_computation.6 | async-start | bytes 524288 | tf_op jit(solution)/shard_map/move_level3/all_to_all | solution.py:19
  110.5 5.2 %slice-start.1 = ((bf16[16,1792]{1,0:T(8,128)(2,1)}), bf16[16,1024]{1,0:T(8,128)(2,1)S(1)}, s32[]{:S(2)}) async-start(bf16[16,1792]{1,0:T(8,128)(2,1)} %param.17), calls=%async_computation.14 | async-start | bytes 65536 | tf_op jit(solution)/shard_map/move_level3/slice | solution.py:83
  116.5 21.2 %all-to-all-start.8 = ((bf16[8,16,1024]{2,1,0:T(8,128)(2,1)}), bf16[8,16,1024]{2,1,0:T(8,128)(2,1)S(1)}, u32[]{:S(2)}, u32[]{:S(2)}) async-start(bf16[8,16,1024]{2,1,0:T(8,128)(2,1)} %broadcast_in_dim.47), calls=%async_computation.8 | async-start | bytes 524288 | tf_op jit(solution)/shard_map/move_level3/all_to_all | solution.py:19
  138.4 24.7 %all-to-all-start.7 = ((bf16[8,16,1024]{2,1,0:T(8,128)(2,1)}), bf16[8,16,1024]{2,1,0:T(8,128)(2,1)S(1)}, u32[]{:S(2)}, u32[]{:S(2)}) async-start(bf16[8,16,1024]{2,1,0:T(8,128)(2,1)} %broadcast_in_dim.46), calls=%async_computation.7 | async-start | bytes 524288 | tf_op jit(solution)/shard_map/level3_up/all_to_all | solution.py:19
  163.8 8.2 %all-to-all-start.9 = ((bf16[4,128,128]{2,1,0:T(8,128)(2,1)}), bf16[4,128,128]{2,1,0:T(8,128)(2,1)S(1)}, u32[]{:S(2)}, u32[]{:S(2)}) async-start(bf16[4,128,128]{2,1,0:T(8,128)(2,1)} %broadcast_in_dim.49), calls=%async_computation.9 | async-start | bytes 262144 | tf_op jit(solution)/shard_map/move_level3/all_to_all | solution.py:19
  172.8 18.9 %all-to-all-start.10 = ((bf16[8,16,512]{2,1,0:T(8,128)(2,1)}), bf16[8,16,512]{2,1,0:T(8,128)(2,1)S(1)}, u32[]{:S(2)}, u32[]{:S(2)}) async-start(bf16[8,16,512]{2,1,0:T(8,128)(2,1)} %broadcast_in_dim.50), calls=%async_computation.10 | async-start | bytes 262144 | tf_op jit(solution)/shard_map/level3_down/all_to_all | solution.py:19
  177.8 14.5 %copy-start.2 = (bf16[128,256]{1,0:T(8,128)(2,1)S(1)}, bf16[128,256]{1,0:T(8,128)(2,1)}, u32[]{:S(2)}) copy-start(bf16[128,256]{1,0:T(8,128)(2,1)} %param.15) | copy-start | bytes 196612

commit v2 on v1

v2 whole, which is shorter than its diff:
```python
import jax
import jax.numpy as jnp
from jax import lax
from jax.sharding import Mesh, PartitionSpec as P

AXES = ("sub", "a", "b", "c", "front")
PAIR = ("c", "front")
BF = jnp.bfloat16
WIDE = 256


def mm(x, w):
    return lax.dot_general(x, w, (((1,), (1,)), ((), ())), preferred_element_type=jnp.float32)


def exchange(x, axes):
    return lax.all_to_all(x, axes, 0, 0)


def spread(x, axes):
    size = lax.axis_size(axes)
    return exchange(jnp.broadcast_to(x[None], (size,) + x.shape), axes)


def total(parts):
    return jnp.sum(parts.astype(jnp.float32), axis=0)


def swap(x, axis):
    return lax.ppermute(x, axis, [(0, 1), (1, 0)])


def ordered(mine, other, index, at):
    low = jnp.where(index == 0, mine, other)
    high = jnp.where(index == 0, other, mine)
    return jnp.stack([low, high], at)


def columns(m, index, width):
    return lax.dynamic_slice_in_dim(m, index * width, width, 1)


def local(
    basis,
    order,
    leaf_inverse,
    leaf_upper_inverse,
    leaf_coupling_low,
    leaf_coupling_up,
    sep_lower_inverse,
    sep_upper_inverse,
    sep_coupling_low,
    sep_coupling_up,
):
    ia, ib, ic = (lax.axis_index(n) for n in ("a", "b", "c"))
    f = lax.axis_index("front")
    leaf = 4 * ia + 2 * ib + ic

    with jax.named_scope("first_exchange"):
        cols = jnp.pad(basis, ((0, 0), (0, WIDE - 176)))
        same = jnp.concatenate([cols, sep_lower_inverse[:, :256]], 1)
        low = jnp.transpose(leaf_coupling_low.reshape(16, 16, 128), (1, 0, 2))

        def by_front(m, groups):
            m = jnp.transpose(m.reshape(16, groups, 8, 16), (2, 0, 1, 3))
            return m.reshape(8, 16, groups * 16)

        moved = jnp.concatenate(
            [
                by_front(sep_lower_inverse[:, 768:], 8),
                by_front(sep_coupling_up[:, 512:], 8),
                jnp.pad(by_front(sep_lower_inverse[:, 256:768], 4), ((0, 0), (0, 0), (0, 64))),
            ],
            2,
        )
        moved = jnp.broadcast_to(moved[None], (2, 8, 16, 384)).reshape(16, 16, 384)
        same = jnp.broadcast_to(same[None], (16, 16, 512))
        got = exchange(jnp.concatenate([same, low, moved], 2), PAIR)
        grouped = lax.dynamic_slice_in_dim(got[:, :, :WIDE], ic * 8, 8, 0)
        a1 = got[:, :, 256:512].reshape(256, 256)
        low_cols = got[:, :, 512:640].reshape(256, 128)
        a3 = got[:, :, 640:768].reshape(2, 8, 16, 128)
        h2 = got[:, :, 768:896].reshape(2, 8, 16, 128)
        a2 = got[:, :, 896:960].reshape(2, 8, 16, 64)

    with jax.named_scope("planes_level2"):
        g2 = sep_coupling_low[:, :512]
        b2 = sep_upper_inverse[:, 256:768]
        mine = jnp.concatenate([columns(g2, ib, 256), b2], 1)
        other = swap(jnp.concatenate([columns(g2, 1 - ib, 256), b2], 1), "b")
        mine = ordered(mine, other, ib, 0).reshape(32, 768)
        down = jnp.concatenate([sep_coupling_up[:, :512], sep_upper_inverse[:, :256]], 1)
        mine = jnp.concatenate([mine, down], 0)
        other = swap(mine, "c")
        both = ordered(mine[:32].reshape(2, 16, 768), other[:32].reshape(2, 16, 768), ic, 1).reshape(64, 768)
        down = ordered(mine[32:], other[32:], ic, 0).reshape(32, 768)
        g2 = both[:, :256]
        b2 = both[:, 256:]

    with jax.named_scope("planes_level3"):
        g3 = sep_coupling_low[:, 512:]
        b3 = sep_upper_inverse[:, 768:]
        mine = jnp.concatenate([columns(g3, ia, 512), b3], 1)
        other = swap(jnp.concatenate([columns(g3, 1 - ia, 512), b3], 1), "a")
        mine = ordered(mine, other, ia, 0)
        mine = ordered(mine, swap(mine, "b"), ib, 1)
        mine = ordered(mine, swap(mine, "c"), ic, 2).reshape(128, 1536)
        g3 = mine[:, :512]
        b3 = mine[:, 512:]

    with jax.named_scope("planes_columns"):
        mine = jnp.concatenate([a2, jnp.zeros_like(a2), h2], 3)
        mine = ordered(mine, swap(mine, "b"), ib, 0).reshape(512, 256)
        a2 = mine[:, :64]
        h2 = mine[:, 128:]
        a3 = ordered(a3, swap(a3, "a"), ia, 0)
        a3 = ordered(a3, swap(a3, "b"), ib, 1).reshape(1024, 128)

    with jax.named_scope("gather_down"):
        tail = jnp.concatenate([down[:, :512], jnp.pad(down[:, 512:], ((0, 0), (0, 256)))], 0)
        tail = jnp.concatenate([b2, tail], 1)
        got = lax.all_gather(jnp.concatenate([leaf_upper_inverse, tail], 0), "front")
        up = lax.dynamic_slice_in_dim(got[:, :128], f * 128, 128, 2).reshape(1024, 128)
        b2 = jnp.transpose(got[:, 128:, :512].reshape(8, 4, 16, 512), (1, 0, 2, 3)).reshape(512, 512)
        h1 = jnp.transpose(got[:, 128:160, 512:].reshape(8, 2, 16, 512), (1, 0, 2, 3)).reshape(256, 512)
        b1 = jnp.transpose(got[:, 160:, 512:768].reshape(8, 2, 16, 256), (1, 0, 2, 3)).reshape(256, 256)

    with jax.named_scope("order"):
        place = (order[0] // 176) * WIDE + order[0] % 176
        slots = place.reshape(8, 176)
        leaf_place = slots[:, :128].reshape(1024)
        own_place = lax.dynamic_index_in_dim(slots, f, 0, keepdims=False)[128:]
        wide = 8 * WIDE
        hot = (leaf_place[:, None] == lax.broadcasted_iota(jnp.int32, (1024, wide), 1)).astype(BF)
        own_hot = (own_place[:, None] == lax.broadcasted_iota(jnp.int32, (48, wide), 1)).astype(BF)
        lower = lax.dot_general(leaf_inverse, hot, (((1,), (0,)), ((), ())), preferred_element_type=jnp.float32)
        lower = jnp.concatenate([lower.astype(BF), own_hot], 0)
        upper = lax.dot_general(hot, up, (((0,), (0,)), ((), ())), preferred_element_type=jnp.float32)
        upper = jnp.concatenate([upper.astype(BF), own_hot.T], 1)

    with jax.named_scope("weights1"):
        row = lax.broadcasted_iota(jnp.int32, (384, 48), 0)
        col = lax.broadcasted_iota(jnp.int32, (384, 48), 1)
        target = jnp.where(col < 16, (ic * 8 + f) * 16 + col, 240 + col)
        keep = (row == target).astype(BF)
        first = jnp.concatenate([jnp.pad(-low_cols, ((0, 128), (0, 0))), keep], 1)

    with jax.named_scope("leaf_lower"):
        grouped = jnp.transpose(grouped, (1, 0, 2)).reshape(16, wide)
        own = mm(grouped, lower).astype(BF)
        y_leaf = own[:, :128]

    with jax.named_scope("level1_up"):
        got = spread(mm(own, first).astype(BF), PAIR)
        c1 = total(got[:, :, :256]).astype(BF)
        rest = lax.dynamic_index_in_dim(got[:, :, 256:288].reshape(2, 8, 16, 32), f, 1, keepdims=False)
        rhs2 = jnp.transpose(rest[:, :, :16], (1, 0, 2)).reshape(16, 32)
        rhs3 = jnp.transpose(rest[:, :, 16:], (1, 0, 2)).reshape(16, 32)
        y1 = mm(c1, a1).astype(BF)

    with jax.named_scope("level2_up"):
        half = lax.broadcasted_iota(jnp.int32, (16, 64), 1) // 32
        part = jnp.where(half == ib, jnp.concatenate([rhs2, rhs2], 1).astype(jnp.float32), 0.0) - mm(y1, g2)
        part = jnp.concatenate([part.astype(BF), jnp.pad(rhs3, ((0, 0), (0, 32)))], 1)
        got = lax.all_gather(part, "b")
        c2 = total(got[:, :, :64]).astype(BF)
        rhs3 = jnp.transpose(got[:, :, 64:96], (1, 0, 2)).reshape(16, 64)
        y2 = total(spread(mm(c2, a2).astype(BF), "front")).astype(BF)

    with jax.named_scope("level3_up"):
        half = lax.broadcasted_iota(jnp.int32, (16, 128), 1) // 64
        part = jnp.where(half == ia, jnp.concatenate([rhs3, rhs3], 1).astype(jnp.float32), 0.0) - mm(y2, g3)
        c3 = total(lax.all_gather(part.astype(BF), "a")).astype(BF)
        y3 = total(spread(mm(c3, a3).astype(BF), "front")).astype(BF)

    with jax.named_scope("level3_down"):
        z3 = mm(y3, b3).astype(BF)
        got = spread(mm(z3, h2).astype(BF), "front")
        w2 = (y2.astype(jnp.float32) - total(got)).astype(BF)

    with jax.named_scope("local_down"):
        z2 = mm(w2, b2).astype(BF)
        w1 = (y1.astype(jnp.float32) - mm(z2, h1)).astype(BF)
        z1 = mm(w1, b1).astype(BF)
        w_leaf = (y_leaf.astype(jnp.float32) - mm(z1, leaf_coupling_up)).astype(BF)
        own = jnp.concatenate(
            [
                w_leaf,
                columns(z1, ic * 8 + f, 16),
                columns(z2, (2 * ib + ic) * 8 + f, 16),
                columns(z3, leaf, 16),
            ],
            1,
        )

    with jax.named_scope("leaf_upper"):
        out = mm(own, upper).astype(BF)
        out = jnp.transpose(out.reshape(16, 8, WIDE), (1, 0, 2))
        return total(exchange(out, "front"))[:, :176].astype(BF)


def solution(mesh):
    fronts = mesh.shape["front"]
    grid = Mesh(mesh.devices.reshape(-1, 2, 2, 2, fronts), AXES)
    rows = P(AXES, None)
    in_specs = (P(None, AXES), P(AXES[:4], None)) + (rows,) * 8
    return jax.shard_map(local, mesh=grid, in_specs=in_specs, out_specs=P(None, AXES), check_vma=False)
```

time: 204 us -> 161 us (0.79)
  blocking collectives: 64.8 us -> 30.2 us
  starting transfers between devices: 72.4 us -> 50.8 us
  between operations: 0.5 us -> 14.2 us
  local copies, waits for them, and re-layouts: 11.3 us -> 15.8 us
  waiting for transfers between devices: 42.4 us -> 39.6 us
    all_to_all x12 -> x4, starting transfers between devices: 72.4 us -> 23.3 us  [exchange(): return lax.all_to_all(x, axes, 0, 0)]
    all_gather x3 -> x0, blocking collectives: 43.1 us -> none  [the longest x1 15.2 us: local(): lax.all_gather(got[:, :, :, 256:768].reshape(4, 16, 512), 'front', axis=1)]
    all_to_all x12 -> x4, waiting for transfers between devices: 42.4 us -> 10.2 us  [exchange(): return lax.all_to_all(x, axes, 0, 0)]
    ppermute x0 -> x8, waiting for transfers between devices: none -> 29.3 us  [swap(): return lax.ppermute(x, axis, [(0, 1), (1, 0)])]
    ppermute x0 -> x8, starting transfers between devices: none -> 27.4 us  [swap(): return lax.ppermute(x, axis, [(0, 1), (1, 0)])]
    all_to_all x1 -> x2, blocking collectives: 8.48 us -> 19 us  [exchange(): return lax.all_to_all(x, axes, 0, 0)]
    slice x24 -> x22, local copies, waits for them, and re-layouts: 0.19 us -> 10.2 us  [the longest x1 1.87 us: local(): got[:, :128]]
    broadcast_in_dim x8 -> x4, local copies, waits for them, and re-layouts: 5.53 us -> 2.17 us  [spread(): return exchange(jnp.broadcast_to(x[None], (size,) + x.shape), axes)]
  transfers between devices with their start and end apart: 12 -> 13, of which waited for: 8 -> 8; matrix products, arithmetic and copies ran while one was open for 6% -> 9% of each run, Pallas kernels for 0% -> 0%
where the time goes in v2:
time: 161 us; the launch traced here: 160 us
  starting transfers between devices  50.8 us (32%)
  waiting for transfers between devices  39.6 us (25%)
  blocking collectives  30.2 us (19%)
  local copies, waits for them, and re-layouts  15.8 us (10%)
  between operations  14.2 us (9%)
  matrix products  6.19 us (4%)
  other arithmetic  3.35 us (2%)
    ppermute x8, waiting for transfers between devices, swap(): return lax.ppermute(x, axis, [(0, 1), (1, 0)])  29.3 us
    ppermute x8, starting transfers between devices, swap(): return lax.ppermute(x, axis, [(0, 1), (1, 0)])  27.4 us
    all_to_all x4, starting transfers between devices, exchange(): return lax.all_to_all(x, axes, 0, 0)  23.3 us
    all_to_all x2, blocking collectives, exchange(): return lax.all_to_all(x, axes, 0, 0)  19 us
    all_to_all x4, waiting for transfers between devices, exchange(): return lax.all_to_all(x, axes, 0, 0)  10.2 us
    all_gather x1, blocking collectives, local(): c3 = total(lax.all_gather(part.astype(BF), 'a')).astype(BF)  7.1 us
    all_gather x1, blocking collectives, local(): got = lax.all_gather(part, 'b')  4.09 us
  transfers between devices with their start and end apart: 13, of which 8 were waited for; matrix products, arithmetic and copies ran while one was open for 9% of the time, Pallas kernels for 0%

profile of v2, /device:TPU:1, one launch (start us, length us, event | category | flops | bytes accessed | tf_op | source)
XLA Modules:
  0.0 160.1 jit_solution(8293752014217535078)
XLA Ops:
  8.1 9.6 %collective-permute-start.3 = (bf16[16,1536]{1,0:T(8,128)(2,1)S(1)}, bf16[16,1536]{1,0:T(8,128)(2,1)S(1)}, u32[]{:S(2)}, u32[]{:S(2)}) collective-permute-start(bf16[16,1536]{1,0:T(8,128)(2,1)S(1)} %pad_maximum_fusion.9), channel_id=1, source_target_pairs={{0,32},{32,0},{1,33},{33,1},{2,34},{34,2},{3,35},{35,3},{4,36},{36... | collective-permute-start | bytes 147464 | tf_op jit(solution)/shard_map/planes_level3/ppermute | solution.py:30
  19.3 4.9 %collective-permute-start = (bf16[16,768]{1,0:T(8,128)(2,1)S(1)}, bf16[16,768]{1,0:T(8,128)(2,1)S(1)}, u32[]{:S(2)}, u32[]{:S(2)}) collective-permute-start(bf16[16,768]{1,0:T(8,128)(2,1)S(1)} %pad_maximum_fusion.14), channel_id=1, source_target_pairs={{0,16},{16,0},{1,17},{17,1},{2,18},{18,2},{3,19},{19,3},{4,20},{20... | collective-permute-start | bytes 73736 | tf_op jit(solution)/shard_map/planes_level2/ppermute | solution.py:30
  28.0 7.1 %all-to-all-start = ((bf16[16,16,1024]{2,1,0:T(8,128)(2,1)}), bf16[16,16,1024]{2,1,0:T(8,128)(2,1)S(1)}, u32[]{:S(2)}, u32[]{:S(2)}) async-start(bf16[16,16,1024]{2,1,0:T(8,128)(2,1)} %pad_maximum_fusion), calls=%async_computation | async-start | bytes 1048576 | tf_op jit(solution)/shard_map/first_exchange/all_to_all | solution.py:17
  39.2 3.3 %collective-permute-start.1 = (bf16[48,768]{1,0:T(8,128)(2,1)S(1)}, bf16[48,768]{1,0:T(8,128)(2,1)S(1)}, u32[]{:S(2)}, u32[]{:S(2)}) collective-permute-start(bf16[48,768]{1,0:T(8,128)(2,1)S(1)} %maximum_maximum_fusion), channel_id=1, source_target_pairs={{0,8},{8,0},{1,9},{9,1},{2,10},{10,2},{3,11},{11,3},{4,12},{12,4},... | collective-permute-start | bytes 221192 | tf_op jit(solution)/shard_map/planes_level2/ppermute | solution.py:30
  42.6 1.9 %collective-permute-start.4 = (bf16[2,16,1536]{2,1,0:T(8,128)(2,1)S(1)}, bf16[2,16,1536]{2,1,0:T(8,128)(2,1)S(1)}, u32[]{:S(2)}, u32[]{:S(2)}) collective-permute-start(bf16[2,16,1536]{2,1,0:T(8,128)(2,1)S(1)} %pad_maximum_fusion.8), channel_id=1, source_target_pairs={{0,16},{16,0},{1,17},{17,1},{2,18},{18,2},{3,19},{19,3},{4,20},{20... | collective-permute-start | bytes 294920 | tf_op jit(solution)/shard_map/planes_level3/ppermute | solution.py:30
  45.1 7.0 %collective-permute-done.4 = bf16[2,16,1536]{2,1,0:T(8,128)(2,1)S(1)} collective-permute-done((bf16[2,16,1536]{2,1,0:T(8,128)(2,1)S(1)}, bf16[2,16,1536]{2,1,0:T(8,128)(2,1)S(1)}, u32[]{:S(2)}, u32[]{:S(2)}) %collective-permute-start.4) | collective-permute-done | bytes 98336 | tf_op jit(solution)/shard_map/planes_level3/ppermute | solution.py:30
  52.1 1.9 %collective-permute-start.5 = (bf16[2,2,16,1536]{3,2,1,0:T(8,128)(2,1)S(1)}, bf16[2,2,16,1536]{3,2,1,0:T(8,128)(2,1)S(1)}, u32[]{:S(2)}, u32[]{:S(2)}) collective-permute-start(bf16[2,2,16,1536]{3,2,1,0:T(8,128)(2,1)S(1)} %pad_maximum_fusion.4), channel_id=1, source_target_pairs={{0,8},{8,0},{1,9},{9,1},{2,10},{10,2},{3,11},{11,3},{4,12},{12,4},... | collective-permute-start | bytes 589832 | tf_op jit(solution)/shard_map/planes_level3/ppermute | solution.py:30
  54.9 5.1 %collective-permute-done.5 = bf16[2,2,16,1536]{3,2,1,0:T(8,128)(2,1)S(1)} collective-permute-done((bf16[2,2,16,1536]{3,2,1,0:T(8,128)(2,1)S(1)}, bf16[2,2,16,1536]{3,2,1,0:T(8,128)(2,1)S(1)}, u32[]{:S(2)}, u32[]{:S(2)}) %collective-permute-start.5) | collective-permute-done | bytes 196640 | tf_op jit(solution)/shard_map/planes_level3/ppermute | solution.py:30
  61.4 5.8 %all-to-all-start.1 = ((bf16[16,16,384]{2,1,0:T(8,128)(2,1)}), bf16[16,16,384]{2,1,0:T(8,128)(2,1)S(1)}, u32[]{:S(2)}, u32[]{:S(2)}) async-start(bf16[16,16,384]{2,1,0:T(8,128)(2,1)} %broadcast_in_dim.24), calls=%async_computation.1 | async-start | bytes 393216 | tf_op jit(solution)/shard_map/level1_up/all_to_all | solution.py:17
  67.1 1.9 %collective-permute-start.6 = (bf16[2,8,16,128]{3,2,1,0:T(8,128)(2,1)S(1)}, bf16[2,8,16,128]{3,2,1,0:T(8,128)(2,1)S(1)}, u32[]{:S(2)}, u32[]{:S(2)}) collective-permute-start(bf16[2,8,16,128]{3,2,1,0:T(8,128)(2,1)S(1)} %bitcast.166), channel_id=1, source_target_pairs={{0,32},{32,0},{1,33},{33,1},{2,34},{34,2},{3,35},{35,3},{4,36},{36... | collective-permute-start | bytes 196616 | tf_op jit(solution)/shard_map/planes_columns/ppermute | solution.py:30
  69.1 1.9 %collective-permute-start.2 = (bf16[2,8,16,256]{3,2,1,0:T(8,128)(2,1)S(1)}, bf16[2,8,16,256]{3,2,1,0:T(8,128)(2,1)S(1)}, u32[]{:S(2)}, u32[]{:S(2)}) collective-permute-start(bf16[2,8,16,256]{3,2,1,0:T(8,128)(2,1)S(1)} %pad_maximum_fusion.5), channel_id=1, source_target_pairs={{0,16},{16,0},{1,17},{17,1},{2,18},{18,2},{3,19},{19,3},{4,20},{20... | collective-permute-start | bytes 393224 | tf_op jit(solution)/shard_map/planes_columns/ppermute | solution.py:30
  71.1 9.2 %collective-permute-done.6 = bf16[2,8,16,128]{3,2,1,0:T(8,128)(2,1)S(1)} collective-permute-done((bf16[2,8,16,128]{3,2,1,0:T(8,128)(2,1)S(1)}, bf16[2,8,16,128]{3,2,1,0:T(8,128)(2,1)S(1)}, u32[]{:S(2)}, u32[]{:S(2)}) %collective-permute-start.6) | collective-permute-done | bytes 65568 | tf_op jit(solution)/shard_map/planes_columns/ppermute | solution.py:30
  80.3 1.9 %collective-permute-start.7 = (bf16[2,2,8,16,128]{4,3,2,1,0:T(8,128)(2,1)S(1)}, bf16[2,2,8,16,128]{4,3,2,1,0:T(8,128)(2,1)S(1)}, u32[]{:S(2)}, u32[]{:S(2)}) collective-permute-start(bf16[2,2,8,16,128]{4,3,2,1,0:T(8,128)(2,1)S(1)} %pad_maximum_fusion.6), channel_id=1, source_target_pairs={{0,16},{16,0},{1,17},{17,1},{2,18},{18,2},{3,19},{19,3},{4,20},{20... | collective-permute-start | bytes 393224 | tf_op jit(solution)/shard_map/planes_columns/ppermute | solution.py:30
  82.8 7.1 %collective-permute-done.7 = bf16[2,2,8,16,128]{4,3,2,1,0:T(8,128)(2,1)S(1)} collective-permute-done((bf16[2,2,8,16,128]{4,3,2,1,0:T(8,128)(2,1)S(1)}, bf16[2,2,8,16,128]{4,3,2,1,0:T(8,128)(2,1)S(1)}, u32[]{:S(2)}, u32[]{:S(2)}) %collective-permute-start.7) | collective-permute-done | bytes 131104 | tf_op jit(solution)/shard_map/planes_columns/ppermute | solution.py:30
  90.8 4.1 %all-gather = bf16[32,128]{1,0:T(8,128)(2,1)S(1)} all-gather(bf16[16,128]{1,0:T(8,128)(2,1)S(1)} %fusion.53), channel_id=2, replica_groups=mesh['sub'=8,'a'=2,'b'=2,'c'=2,'front'=8] {'b'}, dimensions={0}, use_global_device_ids=true | all-gather | bytes 12288 | tf_op jit(solution)/shard_map/level2_up/all_gather | solution.py:165
  95.7 6.2 %all-to-all-start.2 = ((bf16[8,16,512]{2,1,0:T(8,128)(2,1)}), bf16[8,16,512]{2,1,0:T(8,128)(2,1)S(1)}, u32[]{:S(2)}, u32[]{:S(2)}) async-start(bf16[8,16,512]{2,1,0:T(8,128)(2,1)} %broadcast_in_dim.27), calls=%async_computation.2 | async-start | bytes 262144 | tf_op jit(solution)/shard_map/level2_up/all_to_all | solution.py:17
  102.0 5.1 %all-to-all-done.2 = bf16[8,16,512]{2,1,0:T(8,128)(2,1)S(1)} async-done(((bf16[8,16,512]{2,1,0:T(8,128)(2,1)}), bf16[8,16,512]{2,1,0:T(8,128)(2,1)S(1)}, u32[]{:S(2)}, u32[]{:S(2)}) %all-to-all-start.2) | async-done | bytes 131104 | tf_op jit(solution)/shard_map/level2_up/all_to_all | solution.py:17
  107.3 7.1 %all-gather.1 = bf16[32,128]{1,0:T(8,128)(2,1)S(1)} all-gather(bf16[16,128]{1,0:T(8,128)(2,1)S(1)} %fusion.9), channel_id=3, replica_groups=mesh['sub'=8,'a'=2,'b'=2,'c'=2,'front'=8] {'a'}, dimensions={0}, use_global_device_ids=true | all-gather | bytes 12288 | tf_op jit(solution)/shard_map/level3_up/all_gather | solution.py:173
  114.6 10.9 %all_to_all.30 = bf16[8,16,1024]{2,1,0:T(8,128)(2,1)S(1)} all-to-all(bf16[8,16,1024]{2,1,0:T(8,128)(2,1)S(1)} %broadcast_in_dim.29), channel_id=1, replica_groups=mesh['sub'=8,'a'=2,'b'=2,'c'=2,'front'=8] {'front'}, dimensions={0} | all-to-all | bytes 524288 | tf_op jit(solution)/shard_map/level3_up/all_to_all | solution.py:17
  126.6 4.3 %all-to-all-start.4 = ((bf16[8,16,512]{2,1,0:T(8,128)(2,1)}), bf16[8,16,512]{2,1,0:T(8,128)(2,1)S(1)}, u32[]{:S(2)}, u32[]{:S(2)}) async-start(bf16[8,16,512]{2,1,0:T(8,128)(2,1)} %broadcast_in_dim.56), calls=%async_computation.4 | async-start | bytes 262144 | tf_op jit(solution)/shard_map/level3_down/all_to_all | solution.py:17
  131.1 5.1 %all-to-all-done.4 = bf16[8,16,512]{2,1,0:T(8,128)(2,1)S(1)} async-done(((bf16[8,16,512]{2,1,0:T(8,128)(2,1)}), bf16[8,16,512]{2,1,0:T(8,128)(2,1)S(1)}, u32[]{:S(2)}, u32[]{:S(2)}) %all-to-all-start.4) | async-done | bytes 131104 | tf_op jit(solution)/shard_map/level3_down/all_to_all | solution.py:17
  139.3 1.9 %slice.189 = bf16[8,128,1024]{2,1,0:T(8,128)(2,1)S(1)} slice(bf16[8,192,1024]{2,1,0:T(8,128)(2,1)} %bitcast.140), slice={[0:8], [0:128], [0:1024]} | slice | bytes 4194304 | tf_op jit(solution)/shard_map/gather_down/slice | solution.py:123
  142.4 1.9 %fusion.5 = bf16[2048,128]{0,1:T(8,128)(2,1)S(1)} fusion(bf16[1024,128]{1,0:T(8,128)(2,1)S(1)} %bitcast.163, s32[1024]{0:T(1024)S(1)} %slice_bitcast_fusion.3), kind=kOutput, calls=%fused_computation.6 | convolution fusion | flops 539230208 | bytes 790528 | tf_op jit(solution)/shard_map/order/dot_general | solution.py:138
  144.5 8.1 %all_to_all.31 = bf16[8,16,256]{2,1,0:T(8,128)(2,1)S(1)} all-to-all(bf16[8,16,256]{2,1,0:T(8,128)(2,1)S(1)} %bitcast.164), channel_id=1, replica_groups=mesh['sub'=8,'a'=2,'b'=2,'c'=2,'front'=8] {'front'}, dimensions={0} | all-to-all | bytes 131072 | tf_op jit(solution)/shard_map/leaf_upper/all_to_all | solution.py:17
  (149 shorter events, 22.6 us)
Async XLA Ops:
  6.5 29.2 %copy-start = (bf16[128,1024]{1,0:T(8,128)(2,1)S(1)}, bf16[128,1024]{1,0:T(8,128)(2,1)}, u32[]{:S(2)}) copy-start(bf16[128,1024]{1,0:T(8,128)(2,1)} %param.12) | copy-start | bytes 786436
  6.5 20.1 %slice-start = ((bf16[16,1792]{1,0:T(8,128)(2,1)}), bf16[16,512]{1,0:T(8,128)(2,1)S(1)}, s32[]{:S(2)}) async-start(bf16[16,1792]{1,0:T(8,128)(2,1)} %param.16), calls=%async_computation.7 | async-start | bytes 32768 | tf_op jit(solution)/shard_map/first_exchange/slice | solution.py:72
  6.5 20.5 %slice-start.1 = ((bf16[16,1792]{1,0:T(8,128)(2,1)}), bf16[16,256]{1,0:T(8,128)(2,1)S(1)}, s32[]{:S(2)}) async-start(bf16[16,1792]{1,0:T(8,128)(2,1)} %param.16), calls=%async_computation.8 | async-start | bytes 16384 | tf_op jit(solution)/shard_map/first_exchange/slice | solution.py:61
  6.5 20.4 %copy-start.3 = (bf16[16,2048]{1,0:T(8,128)(2,1)S(1)}, bf16[16,2048]{1,0:T(8,128)(2,1)}, u32[]{:S(2)}) copy-start(bf16[16,2048]{1,0:T(8,128)(2,1)} %param.14) | copy-start | bytes 196612
  6.5 20.5 %copy-start.5 = (bf16[16,176]{1,0:T(8,128)(2,1)S(1)}, bf16[16,176]{1,0:T(8,128)(2,1)}, u32[]{:S(2)}) copy-start(bf16[16,176]{1,0:T(8,128)(2,1)} %param.10) | copy-start | bytes 16900
  8.1 34.4 %collective-permute-start.3 = (bf16[16,1536]{1,0:T(8,128)(2,1)S(1)}, bf16[16,1536]{1,0:T(8,128)(2,1)S(1)}, u32[]{:S(2)}, u32[]{:S(2)}) collective-permute-start(bf16[16,1536]{1,0:T(8,128)(2,1)S(1)} %pad_maximum_fusion.9), channel_id=1, source_target_pairs={{0,32},{32,0},{1,33},{33,1},{2,34},{34,2},{3,35},{35,3},{4,36},{36... | collective-permute-start | bytes 147464 | tf_op jit(solution)/shard_map/planes_level3/ppermute | solution.py:30
  19.3 19.9 %collective-permute-start = (bf16[16,768]{1,0:T(8,128)(2,1)S(1)}, bf16[16,768]{1,0:T(8,128)(2,1)S(1)}, u32[]{:S(2)}, u32[]{:S(2)}) collective-permute-start(bf16[16,768]{1,0:T(8,128)(2,1)S(1)} %pad_maximum_fusion.14), channel_id=1, source_target_pairs={{0,16},{16,0},{1,17},{17,1},{2,18},{18,2},{3,19},{19,3},{4,20},{20... | collective-permute-start | bytes 73736 | tf_op jit(solution)/shard_map/planes_level2/ppermute | solution.py:30
  26.4 8.7 %copy-start.4 = (s32[1,1408]{1,0:T(1,128)S(1)}, s32[1,1408]{1,0:T(1,128)}, u32[]{:S(2)}) copy-start(s32[1,1408]{1,0:T(1,128)} %param.11) | copy-start | bytes 16900
  28.0 32.1 %all-to-all-start = ((bf16[16,16,1024]{2,1,0:T(8,128)(2,1)}), bf16[16,16,1024]{2,1,0:T(8,128)(2,1)S(1)}, u32[]{:S(2)}, u32[]{:S(2)}) async-start(bf16[16,16,1024]{2,1,0:T(8,128)(2,1)} %pad_maximum_fusion), calls=%async_computation | async-start | bytes 1048576 | tf_op jit(solution)/shard_map/first_exchange/all_to_all | solution.py:17
  35.1 101.2 %all-gather.5.cloned.1.call-start = ((), (), s32[]{:S(2)}) async-start(), calls=%async_computation.6 | async-start | bytes 3538944 | tf_op jit(solution)/shard_map/gather_down/all_gather | solution.py:122
  37.6 16.5 %copy-start.1 = (bf16[128,1024]{1,0:T(8,128)(2,1)S(1)}, bf16[128,1024]{1,0:T(8,128)(2,1)}, u32[]{:S(2)}) copy-start(bf16[128,1024]{1,0:T(8,128)(2,1)} %param.13) | copy-start | bytes 786436
  39.2 5.7 %collective-permute-start.1 = (bf16[48,768]{1,0:T(8,128)(2,1)S(1)}, bf16[48,768]{1,0:T(8,128)(2,1)S(1)}, u32[]{:S(2)}, u32[]{:S(2)}) collective-permute-start(bf16[48,768]{1,0:T(8,128)(2,1)S(1)} %maximum_maximum_fusion), channel_id=1, source_target_pairs={{0,8},{8,0},{1,9},{9,1},{2,10},{10,2},{3,11},{11,3},{4,12},{12,4},... | collective-permute-start | bytes 221192 | tf_op jit(solution)/shard_map/planes_level2/ppermute | solution.py:30
  42.6 9.4 %collective-permute-start.4 = (bf16[2,16,1536]{2,1,0:T(8,128)(2,1)S(1)}, bf16[2,16,1536]{2,1,0:T(8,128)(2,1)S(1)}, u32[]{:S(2)}, u32[]{:S(2)}) collective-permute-start(bf16[2,16,1536]{2,1,0:T(8,128)(2,1)S(1)} %pad_maximum_fusion.8), channel_id=1, source_target_pairs={{0,16},{16,0},{1,17},{17,1},{2,18},{18,2},{3,19},{19,3},{4,20},{20... | collective-permute-start | bytes 294920 | tf_op jit(solution)/shard_map/planes_level3/ppermute | solution.py:30
  52.1 7.9 %collective-permute-start.5 = (bf16[2,2,16,1536]{3,2,1,0:T(8,128)(2,1)S(1)}, bf16[2,2,16,1536]{3,2,1,0:T(8,128)(2,1)S(1)}, u32[]{:S(2)}, u32[]{:S(2)}) collective-permute-start(bf16[2,2,16,1536]{3,2,1,0:T(8,128)(2,1)S(1)} %pad_maximum_fusion.4), channel_id=1, source_target_pairs={{0,8},{8,0},{1,9},{9,1},{2,10},{10,2},{3,11},{11,3},{4,12},{12,4},... | collective-permute-start | bytes 589832 | tf_op jit(solution)/shard_map/planes_level3/ppermute | solution.py:30
  61.4 28.6 %all-to-all-start.1 = ((bf16[16,16,384]{2,1,0:T(8,128)(2,1)}), bf16[16,16,384]{2,1,0:T(8,128)(2,1)S(1)}, u32[]{:S(2)}, u32[]{:S(2)}) async-start(bf16[16,16,384]{2,1,0:T(8,128)(2,1)} %broadcast_in_dim.24), calls=%async_computation.1 | async-start | bytes 393216 | tf_op jit(solution)/shard_map/level1_up/all_to_all | solution.py:17
  67.1 13.1 %collective-permute-start.6 = (bf16[2,8,16,128]{3,2,1,0:T(8,128)(2,1)S(1)}, bf16[2,8,16,128]{3,2,1,0:T(8,128)(2,1)S(1)}, u32[]{:S(2)}, u32[]{:S(2)}) collective-permute-start(bf16[2,8,16,128]{3,2,1,0:T(8,128)(2,1)S(1)} %bitcast.166), channel_id=1, source_target_pairs={{0,32},{32,0},{1,33},{33,1},{2,34},{34,2},{3,35},{35,3},{4,36},{36... | collective-permute-start | bytes 196616 | tf_op jit(solution)/shard_map/planes_columns/ppermute | solution.py:30
  69.1 13.6 %collective-permute-start.2 = (bf16[2,8,16,256]{3,2,1,0:T(8,128)(2,1)S(1)}, bf16[2,8,16,256]{3,2,1,0:T(8,128)(2,1)S(1)}, u32[]{:S(2)}, u32[]{:S(2)}) collective-permute-start(bf16[2,8,16,256]{3,2,1,0:T(8,128)(2,1)S(1)} %pad_maximum_fusion.5), channel_id=1, source_target_pairs={{0,16},{16,0},{1,17},{17,1},{2,18},{18,2},{3,19},{19,3},{4,20},{20... | collective-permute-start | bytes 393224 | tf_op jit(solution)/shard_map/planes_columns/ppermute | solution.py:30
  80.3 9.6 %collective-permute-start.7 = (bf16[2,2,8,16,128]{4,3,2,1,0:T(8,128)(2,1)S(1)}, bf16[2,2,8,16,128]{4,3,2,1,0:T(8,128)(2,1)S(1)}, u32[]{:S(2)}, u32[]{:S(2)}) collective-permute-start(bf16[2,2,8,16,128]{4,3,2,1,0:T(8,128)(2,1)S(1)} %pad_maximum_fusion.6), channel_id=1, source_target_pairs={{0,16},{16,0},{1,17},{17,1},{2,18},{18,2},{3,19},{19,3},{4,20},{20... | collective-permute-start | bytes 393224 | tf_op jit(solution)/shard_map/planes_columns/ppermute | solution.py:30
  95.7 11.4 %all-to-all-start.2 = ((bf16[8,16,512]{2,1,0:T(8,128)(2,1)}), bf16[8,16,512]{2,1,0:T(8,128)(2,1)S(1)}, u32[]{:S(2)}, u32[]{:S(2)}) async-start(bf16[8,16,512]{2,1,0:T(8,128)(2,1)} %broadcast_in_dim.27), calls=%async_computation.2 | async-start | bytes 262144 | tf_op jit(solution)/shard_map/level2_up/all_to_all | solution.py:17
  126.6 9.6 %all-to-all-start.4 = ((bf16[8,16,512]{2,1,0:T(8,128)(2,1)}), bf16[8,16,512]{2,1,0:T(8,128)(2,1)S(1)}, u32[]{:S(2)}, u32[]{:S(2)}) async-start(bf16[8,16,512]{2,1,0:T(8,128)(2,1)} %broadcast_in_dim.56), calls=%async_computation.4 | async-start | bytes 262144 | tf_op jit(solution)/shard_map/level3_down/all_to_all | solution.py:17
  141.1 0.8 copy-start.2
Sparse Core Ops, SparseCore 0:
  55.0 33.4 all-gather.4

commit v3 on v2

v3 whole, which is shorter than its diff:
```python
import jax
import jax.numpy as jnp
from jax import lax
from jax.sharding import Mesh, PartitionSpec as P

AXES = ("sub", "a", "b", "c", "front")
PAIR = ("c", "front")
BF = jnp.bfloat16
WIDE = 256


def mm(x, w):
    return lax.dot_general(x, w, (((1,), (1,)), ((), ())), preferred_element_type=jnp.float32)


def exchange(x, axes):
    return lax.all_to_all(x, axes, 0, 0)


def spread(x, axes):
    size = lax.axis_size(axes)
    return exchange(jnp.broadcast_to(x[None], (size,) + x.shape), axes)


def total(parts):
    return jnp.sum(parts.astype(jnp.float32), axis=0)


def swap(x, axis):
    return lax.ppermute(x, axis, [(0, 1), (1, 0)])


def ordered(mine, other, index, at):
    low = jnp.where(index == 0, mine, other)
    high = jnp.where(index == 0, other, mine)
    return jnp.stack([low, high], at)


def columns(m, index, width):
    return lax.dynamic_slice_in_dim(m, index * width, width, 1)


def local(
    basis,
    order,
    leaf_inverse,
    leaf_upper_inverse,
    leaf_coupling_low,
    leaf_coupling_up,
    sep_lower_inverse,
    sep_upper_inverse,
    sep_coupling_low,
    sep_coupling_up,
):
    ia, ib, ic = (lax.axis_index(n) for n in ("a", "b", "c"))
    f = lax.axis_index("front")
    leaf = 4 * ia + 2 * ib + ic

    with jax.named_scope("first_exchange"):

        def by_front(m, groups):
            m = jnp.transpose(m.reshape(16, groups, 8, 16), (2, 0, 1, 3))
            return m.reshape(8, 16, groups * 16)

        def per_front(m):
            return jnp.broadcast_to(m[None], (2,) + m.shape).reshape((16,) + m.shape[1:])

        def for_all(m):
            return jnp.broadcast_to(m[None], (16,) + m.shape)

        low = jnp.transpose(leaf_coupling_low.reshape(16, 16, 128), (1, 0, 2))
        moved = jnp.concatenate(
            [
                for_all(jnp.pad(basis, ((0, 0), (0, 16)))),
                per_front(by_front(sep_lower_inverse[:, 256:768], 4)),
                for_all(sep_lower_inverse[:, :256]),
                for_all(sep_upper_inverse[:, :256]),
                low,
                per_front(by_front(sep_lower_inverse[:, 768:], 8)),
                per_front(by_front(sep_coupling_up[:, 512:], 8)),
                per_front(by_front(sep_coupling_up[:, :512], 4)),
                jnp.zeros((16, 16, 64), BF),
            ],
            2,
        )
        got = exchange(moved, PAIR)

    with jax.named_scope("planes_level2"):
        g2 = sep_coupling_low[:, :512]
        b2 = sep_upper_inverse[:, 256:768]
        level2 = jnp.concatenate([columns(g2, ib, 256), b2], 1)
        other = swap(jnp.concatenate([columns(g2, 1 - ib, 256), b2], 1), "b")
        level2 = ordered(level2, other, ib, 0)
        other = swap(level2, "c")

    with jax.named_scope("planes_level3"):
        g3 = sep_coupling_low[:, 512:]
        b3 = sep_upper_inverse[:, 768:]
        level3 = jnp.concatenate([columns(g3, ia, 512), b3], 1)
        other3 = swap(jnp.concatenate([columns(g3, 1 - ia, 512), b3], 1), "a")

    got, level2, other, level3, other3 = lax.optimization_barrier((got, level2, other, level3, other3))

    with jax.named_scope("unpack"):
        grouped = lax.dynamic_slice_in_dim(got[:, :, :WIDE], ic * 8, 8, 0)
        a2 = got[:, :, 192:256]
        a1 = got[:, :, 256:512].reshape(256, 256)
        b1 = got[:, :, 512:768].reshape(256, 256)
        low_cols = got[:, :, 768:896].reshape(256, 128)
        a3 = got[:, :, 896:1024]
        h2 = got[:, :, 1024:1152]
        h1 = got[:, :, 1152:1216].reshape(256, 64)
        level2 = ordered(level2, other, ic, 1).reshape(64, 768)
        g2 = level2[:, :256]
        b2 = level2[:, 256:]
        level3 = ordered(level3, other3, ia, 0)
        mixed = jnp.concatenate([a2, jnp.zeros_like(a2), h2], 2).reshape(256, 256)
        a3 = a3.reshape(256, 128)

    with jax.named_scope("planes_middle"):
        mixed_other = swap(mixed, "b")
        a3_other = swap(a3, "a")
        level3_other = swap(level3, "b")

    with jax.named_scope("order"):
        place = (order[0] // 176) * WIDE + order[0] % 176
        slots = place.reshape(8, 176)
        leaf_place = slots[:, :128].reshape(1024)
        own_place = lax.dynamic_index_in_dim(slots, f, 0, keepdims=False)[128:]
        wide = 8 * WIDE
        hot = (leaf_place[:, None] == lax.broadcasted_iota(jnp.int32, (1024, wide), 1)).astype(BF)
        own_hot = (own_place[:, None] == lax.broadcasted_iota(jnp.int32, (48, wide), 1)).astype(BF)
        lower = lax.dot_general(leaf_inverse, hot, (((1,), (0,)), ((), ())), preferred_element_type=jnp.float32)
        lower = jnp.concatenate([lower.astype(BF), own_hot], 0)

    with jax.named_scope("weights1"):
        row = lax.broadcasted_iota(jnp.int32, (384, 48), 0)
        col = lax.broadcasted_iota(jnp.int32, (384, 48), 1)
        target = jnp.where(col < 16, (ic * 8 + f) * 16 + col, 240 + col)
        keep = (row == target).astype(BF)
        first = jnp.concatenate([jnp.pad(-low_cols, ((0, 128), (0, 0))), keep], 1)

    with jax.named_scope("leaf_lower"):
        grouped = jnp.transpose(grouped, (1, 0, 2)).reshape(16, wide)
        own = mm(grouped, lower).astype(BF)
        y_leaf = own[:, :128]

    with jax.named_scope("level1_up"):
        got = spread(mm(own, first).astype(BF), PAIR)
        c1 = total(got[:, :, :256]).astype(BF)
        rest = lax.dynamic_index_in_dim(got[:, :, 256:288].reshape(2, 8, 16, 32), f, 1, keepdims=False)
        rhs2 = jnp.transpose(rest[:, :, :16], (1, 0, 2)).reshape(16, 32)
        rhs3 = jnp.transpose(rest[:, :, 16:], (1, 0, 2)).reshape(16, 32)
        y1 = mm(c1, a1).astype(BF)

    with jax.named_scope("level2_up"):
        half = lax.broadcasted_iota(jnp.int32, (16, 64), 1) // 32
        part = jnp.where(half == ib, jnp.concatenate([rhs2, rhs2], 1).astype(jnp.float32), 0.0) - mm(y1, g2)
        part = jnp.concatenate([part.astype(BF), jnp.pad(rhs3, ((0, 0), (0, 32)))], 1)
        got = lax.all_gather(part, "b")
        got, mixed, mixed_other, a3, a3_other, level3, level3_other = lax.optimization_barrier(
            (got, mixed, mixed_other, a3, a3_other, level3, level3_other)
        )
        mixed = ordered(mixed, mixed_other, ib, 0).reshape(512, 256)
        a2 = mixed[:, :64]
        h2 = mixed[:, 128:]
        a3 = ordered(a3, a3_other, ia, 0)
        a3_other = swap(a3, "b")
        level3 = ordered(level3, level3_other, ib, 1)
        level3_other = swap(level3, "c")
        c2 = total(got[:, :, :64]).astype(BF)
        rhs3 = jnp.transpose(got[:, :, 64:96], (1, 0, 2)).reshape(16, 64)
        got = spread(mm(c2, a2).astype(BF), "front")
        got, level3, level3_other = lax.optimization_barrier((got, level3, level3_other))
        level3 = ordered(level3, level3_other, ic, 2).reshape(128, 1536)
        g3 = level3[:, :512]
        b3 = level3[:, 512:]
        y2 = total(got).astype(BF)

    with jax.named_scope("level3_up"):
        half = lax.broadcasted_iota(jnp.int32, (16, 128), 1) // 64
        part = jnp.where(half == ia, jnp.concatenate([rhs3, rhs3], 1).astype(jnp.float32), 0.0) - mm(y2, g3)
        part = part.astype(BF)
        up = jnp.transpose(leaf_upper_inverse.reshape(128, 8, 128), (1, 0, 2))
        up, part = lax.optimization_barrier((up, part))
        up = exchange(up, "front")
        got = lax.all_gather(part, "a")
        got, up, a3, a3_other = lax.optimization_barrier((got, up, a3, a3_other))
        up = up.reshape(1024, 128)
        a3 = ordered(a3, a3_other, ib, 1).reshape(1024, 128)
        c3 = total(got).astype(BF)
        y3 = total(spread(mm(c3, a3).astype(BF), "front")).astype(BF)

    with jax.named_scope("level3_down"):
        z3 = mm(y3, b3).astype(BF)
        upper = lax.dot_general(hot, up, (((0,), (0,)), ((), ())), preferred_element_type=jnp.float32)
        upper = jnp.concatenate([upper.astype(BF), own_hot.T], 1)
        got = spread(mm(z3, h2).astype(BF), "front")
        got, upper = lax.optimization_barrier((got, upper))
        w2 = (y2.astype(jnp.float32) - total(got)).astype(BF)

    with jax.named_scope("local_down"):
        z2 = mm(w2, b2).astype(BF)
        w1 = (y1.astype(jnp.float32) - total(spread(mm(z2, h1).astype(BF), "front"))).astype(BF)
        z1 = mm(w1, b1).astype(BF)
        w_leaf = (y_leaf.astype(jnp.float32) - mm(z1, leaf_coupling_up)).astype(BF)
        own = jnp.concatenate(
            [
                w_leaf,
                columns(z1, ic * 8 + f, 16),
                columns(z2, 2 * ib + ic, 16),
                columns(z3, leaf, 16),
            ],
            1,
        )

    with jax.named_scope("leaf_upper"):
        out = mm(own, upper).astype(BF)
        out = jnp.transpose(out.reshape(16, 8, WIDE), (1, 0, 2))
        return total(exchange(out, "front"))[:, :176].astype(BF)


def solution(mesh):
    fronts = mesh.shape["front"]
    grid = Mesh(mesh.devices.reshape(-1, 2, 2, 2, fronts), AXES)
    rows = P(AXES, None)
    in_specs = (P(None, AXES), P(AXES[:4], None)) + (rows,) * 8
    return jax.shard_map(local, mesh=grid, in_specs=in_specs, out_specs=P(None, AXES), check_vma=False)
```

time: 161 us -> 133 us (0.83)
  starting transfers between devices: 50.8 us -> 72.7 us
  waiting for transfers between devices: 39.6 us -> 19.6 us
  between operations: 14.2 us -> 0.85 us
  blocking collectives: 30.2 us -> 21.5 us
  local copies, waits for them, and re-layouts: 15.8 us -> 9.55 us
  other arithmetic: 3.35 us -> 1.72 us
    ppermute x8, waiting for transfers between devices: 29.3 us -> 5.23 us  [swap(): return lax.ppermute(x, axis, [(0, 1), (1, 0)])]
    all_to_all x4 -> x7, starting transfers between devices: 23.3 us -> 42.8 us  [exchange(): return lax.all_to_all(x, axes, 0, 0)]
    all_to_all x2 -> x1, blocking collectives: 19 us -> 8 us  [exchange(): return lax.all_to_all(x, axes, 0, 0)]
    slice x12 -> x4, local copies, waits for them, and re-layouts: 4.93 us -> 0.13 us  [the longest x1 0.09 us: local(): h1 = got[:, :, 1152:1216].reshape(256, 64)]
    all_to_all x4 -> x7, waiting for transfers between devices: 10.2 us -> 14.4 us  [exchange(): return lax.all_to_all(x, axes, 0, 0)]
    ppermute x8, starting transfers between devices: 27.4 us -> 29.9 us  [swap(): return lax.ppermute(x, axis, [(0, 1), (1, 0)])]
    all_gather x1, blocking collectives: 4.09 us -> 6.39 us  [local(): got = lax.all_gather(part, 'b')]
    broadcast_in_dim x4 -> x5, local copies, waits for them, and re-layouts: 2.17 us -> 3.51 us  [spread(): return exchange(jnp.broadcast_to(x[None], (size,) + x.shape), axes)]
  transfers between devices with their start and end apart: 13 -> 15, of which waited for: 8 -> 5; matrix products, arithmetic and copies ran while one was open for 9% -> 5% of each run, Pallas kernels for 0% -> 0%
where the time goes in v3:
time: 133 us; the launch traced here: 132 us
  starting transfers between devices  72.7 us (55%)
  blocking collectives  21.5 us (16%)
  waiting for transfers between devices  19.6 us (15%)
  local copies, waits for them, and re-layouts  9.55 us (7%)
  matrix products  6.09 us (5%)
  other arithmetic  1.72 us (1%)
    all_to_all x7, starting transfers between devices, exchange(): return lax.all_to_all(x, axes, 0, 0)  42.8 us
    ppermute x8, starting transfers between devices, swap(): return lax.ppermute(x, axis, [(0, 1), (1, 0)])  29.9 us
    all_to_all x7, waiting for transfers between devices, exchange(): return lax.all_to_all(x, axes, 0, 0)  14.4 us
    all_to_all x1, blocking collectives, exchange(): return lax.all_to_all(x, axes, 0, 0)  8 us
    all_gather x1, blocking collectives, local(): got = lax.all_gather(part, 'a')  7.1 us
    all_gather x1, blocking collectives, local(): got = lax.all_gather(part, 'b')  6.39 us
    ppermute x8, waiting for transfers between devices, swap(): return lax.ppermute(x, axis, [(0, 1), (1, 0)])  5.23 us
    broadcast_in_dim x5, local copies, waits for them, and re-layouts, spread(): return exchange(jnp.broadcast_to(x[None], (size,) + x.shape), axes)  3.51 us
  transfers between devices with their start and end apart: 15, of which 5 were waited for; matrix products, arithmetic and copies ran while one was open for 5% of the time, Pallas kernels for 0%

profile of v3, /device:TPU:1, one launch (start us, length us, event | category | flops | bytes accessed | tf_op | source)
XLA Modules:
  0.0 132.0 jit_solution(199696130654351761)
XLA Ops:
  4.0 10.4 %all-to-all-start = ((bf16[16,16,1280]{2,1,0:T(8,128)(2,1)}), bf16[16,16,1280]{2,1,0:T(8,128)(2,1)S(1)}, u32[]{:S(2)}, u32[]{:S(2)}) async-start(bf16[16,16,1280]{2,1,0:T(8,128)(2,1)} %concatenate.39), calls=%async_computation | async-start | bytes 1310720 | tf_op jit(solution)/shard_map/first_exchange/all_to_all | solution.py:17
  14.5 2.0 %collective-permute-start = (bf16[16,768]{1,0:T(8,128)(2,1)S(1)}, bf16[16,768]{1,0:T(8,128)(2,1)S(1)}, u32[]{:S(2)}, u32[]{:S(2)}) collective-permute-start(bf16[16,768]{1,0:T(8,128)(2,1)S(1)} %pad_maximum_fusion.12), channel_id=1, source_target_pairs={{0,16},{16,0},{1,17},{17,1},{2,18},{18,2},{3,19},{19,3},{4,20},{20... | collective-permute-start | bytes 73736 | tf_op jit(solution)/shard_map/planes_level2/ppermute | solution.py:30
  16.6 8.8 %collective-permute-start.2 = (bf16[16,1536]{1,0:T(8,128)(2,1)S(1)}, bf16[16,1536]{1,0:T(8,128)(2,1)S(1)}, u32[]{:S(2)}, u32[]{:S(2)}) collective-permute-start(bf16[16,1536]{1,0:T(8,128)(2,1)S(1)} %get-tuple-element.77), channel_id=1, source_target_pairs={{0,32},{32,0},{1,33},{33,1},{2,34},{34,2},{3,35},{35,3},{4,36},{36... | collective-permute-start | bytes 147464 | tf_op jit(solution)/shard_map/planes_level3/ppermute | solution.py:30
  26.0 1.8 %fusion.6 = bf16[128,2048]{1,0:T(8,128)(2,1)S(1)} fusion(bf16[128,1024]{1,0:T(8,128)(2,1)S(1)} %copy-done, s32[1024]{0:T(1024)S(1)} %slice_bitcast_fusion.3), kind=kOutput, calls=%fused_computation.7 | convolution fusion | flops 539230208 | bytes 790528 | tf_op jit(solution)/shard_map/order/dot_general | solution.py:133
  28.0 3.3 %collective-permute-start.1 = (bf16[2,16,768]{2,1,0:T(8,128)(2,1)S(1)}, bf16[2,16,768]{2,1,0:T(8,128)(2,1)S(1)}, u32[]{:S(2)}, u32[]{:S(2)}) collective-permute-start(bf16[2,16,768]{2,1,0:T(8,128)(2,1)S(1)} %pad_maximum_fusion.11), channel_id=1, source_target_pairs={{0,8},{8,0},{1,9},{9,1},{2,10},{10,2},{3,11},{11,3},{4,12},{12,4},... | collective-permute-start | bytes 147464 | tf_op jit(solution)/shard_map/planes_level2/ppermute | solution.py:30
  34.2 7.4 %all-to-all-start.1 = ((bf16[16,16,384]{2,1,0:T(8,128)(2,1)}), bf16[16,16,384]{2,1,0:T(8,128)(2,1)S(1)}, u32[]{:S(2)}, u32[]{:S(2)}) async-start(bf16[16,16,384]{2,1,0:T(8,128)(2,1)} %broadcast_in_dim.96), calls=%async_computation.1 | async-start | bytes 393216 | tf_op jit(solution)/shard_map/level1_up/all_to_all | solution.py:17
  41.7 1.9 %collective-permute-start.3 = (bf16[256,256]{1,0:T(8,128)(2,1)S(1)}, bf16[256,256]{1,0:T(8,128)(2,1)S(1)}, u32[]{:S(2)}, u32[]{:S(2)}) collective-permute-start(bf16[256,256]{1,0:T(8,128)(2,1)S(1)} %bitcast.133), channel_id=1, source_target_pairs={{0,16},{16,0},{1,17},{17,1},{2,18},{18,2},{3,19},{19,3},{4,20},{20... | collective-permute-start | bytes 393224 | tf_op jit(solution)/shard_map/planes_middle/ppermute | solution.py:30
  43.7 4.4 %collective-permute-start.4 = (bf16[256,128]{1,0:T(8,128)(2,1)S(1)}, bf16[256,128]{1,0:T(8,128)(2,1)S(1)}, u32[]{:S(2)}, u32[]{:S(2)}) collective-permute-start(bf16[256,128]{1,0:T(8,128)(2,1)S(1)} %bitcast.150), channel_id=1, source_target_pairs={{0,32},{32,0},{1,33},{33,1},{2,34},{34,2},{3,35},{35,3},{4,36},{36... | collective-permute-start | bytes 196616 | tf_op jit(solution)/shard_map/planes_middle/ppermute | solution.py:30
  48.1 4.3 %collective-permute-start.5 = (bf16[2,16,1536]{2,1,0:T(8,128)(2,1)S(1)}, bf16[2,16,1536]{2,1,0:T(8,128)(2,1)S(1)}, u32[]{:S(2)}, u32[]{:S(2)}) collective-permute-start(bf16[2,16,1536]{2,1,0:T(8,128)(2,1)S(1)} %pad_maximum_fusion.8), channel_id=1, source_target_pairs={{0,16},{16,0},{1,17},{17,1},{2,18},{18,2},{3,19},{19,3},{4,20},{20... | collective-permute-start | bytes 294920 | tf_op jit(solution)/shard_map/planes_middle/ppermute | solution.py:30
  53.1 6.4 %all-gather = bf16[32,128]{1,0:T(8,128)(2,1)S(1)} all-gather(bf16[16,128]{1,0:T(8,128)(2,1)S(1)} %fusion.39), channel_id=2, replica_groups=mesh['sub'=8,'a'=2,'b'=2,'c'=2,'front'=8] {'b'}, dimensions={0}, use_global_device_ids=true | all-gather | bytes 12288 | tf_op jit(solution)/shard_map/level2_up/all_gather | solution.py:160
  60.4 5.4 %all-to-all-start.2 = ((bf16[8,16,512]{2,1,0:T(8,128)(2,1)}), bf16[8,16,512]{2,1,0:T(8,128)(2,1)S(1)}, u32[]{:S(2)}, u32[]{:S(2)}) async-start(bf16[8,16,512]{2,1,0:T(8,128)(2,1)} %broadcast_in_dim.98), calls=%async_computation.2 | async-start | bytes 262144 | tf_op jit(solution)/shard_map/level2_up/all_to_all | solution.py:17
  65.9 2.2 %collective-permute-start.6 = (bf16[2,2,16,1536]{3,2,1,0:T(8,128)(2,1)S(1)}, bf16[2,2,16,1536]{3,2,1,0:T(8,128)(2,1)S(1)}, u32[]{:S(2)}, u32[]{:S(2)}) collective-permute-start(bf16[2,2,16,1536]{3,2,1,0:T(8,128)(2,1)S(1)} %pad_maximum_fusion.4), channel_id=1, source_target_pairs={{0,8},{8,0},{1,9},{9,1},{2,10},{10,2},{3,11},{11,3},{4,12},{12,4},... | collective-permute-start | bytes 589832 | tf_op jit(solution)/shard_map/level2_up/ppermute | solution.py:30
  68.3 3.1 %collective-permute-start.7 = (bf16[2,256,128]{2,1,0:T(8,128)(2,1)S(1)}, bf16[2,256,128]{2,1,0:T(8,128)(2,1)S(1)}, u32[]{:S(2)}, u32[]{:S(2)}) collective-permute-start(bf16[2,256,128]{2,1,0:T(8,128)(2,1)S(1)} %pad_maximum_fusion.6), channel_id=1, source_target_pairs={{0,16},{16,0},{1,17},{17,1},{2,18},{18,2},{3,19},{19,3},{4,20},{20... | collective-permute-start | bytes 393224 | tf_op jit(solution)/shard_map/level2_up/ppermute | solution.py:30
  71.4 4.5 %collective-permute-done.6 = bf16[2,2,16,1536]{3,2,1,0:T(8,128)(2,1)S(1)} collective-permute-done((bf16[2,2,16,1536]{3,2,1,0:T(8,128)(2,1)S(1)}, bf16[2,2,16,1536]{3,2,1,0:T(8,128)(2,1)S(1)}, u32[]{:S(2)}, u32[]{:S(2)}) %collective-permute-start.6) | collective-permute-done | bytes 196640 | tf_op jit(solution)/shard_map/level2_up/ppermute | solution.py:30
  76.2 5.2 %all-to-all-start.3 = ((bf16[8,128,128]{1,2,0:T(8,128)(2,1)}), bf16[8,128,128]{1,2,0:T(8,128)(2,1)S(1)}, u32[]{:S(2)}, u32[]{:S(2)}) async-start(bf16[8,128,128]{1,2,0:T(8,128)(2,1)} %bitcast.37), calls=%async_computation.3 | async-start | bytes 524288 | tf_op jit(solution)/shard_map/level3_up/all_to_all | solution.py:17
  81.5 7.1 %all-gather.1 = bf16[32,128]{1,0:T(8,128)(2,1)S(1)} all-gather(bf16[16,128]{1,0:T(8,128)(2,1)S(1)} %fusion.8), channel_id=3, replica_groups=mesh['sub'=8,'a'=2,'b'=2,'c'=2,'front'=8] {'a'}, dimensions={0}, use_global_device_ids=true | all-gather | bytes 12288 | tf_op jit(solution)/shard_map/level3_up/all_gather | solution.py:187
  89.6 6.0 %all-to-all-start.4 = ((bf16[8,16,1024]{2,1,0:T(8,128)(2,1)}), bf16[8,16,1024]{2,1,0:T(8,128)(2,1)S(1)}, u32[]{:S(2)}, u32[]{:S(2)}) async-start(bf16[8,16,1024]{2,1,0:T(8,128)(2,1)} %broadcast_in_dim.100), calls=%async_computation.4 | async-start | bytes 524288 | tf_op jit(solution)/shard_map/level3_up/all_to_all | solution.py:17
  95.7 1.9 %fusion.5 = bf16[2048,128]{0,1:T(8,128)(2,1)S(1)} fusion(bf16[1024,128]{1,0:T(8,128)(2,1)S(1)} %bitcast.146, s32[1024]{0:T(1024)S(1)} %slice_bitcast_fusion.3), kind=kOutput, calls=%fused_computation.6 | convolution fusion | flops 539230208 | bytes 790528 | tf_op jit(solution)/shard_map/level3_down/dot_general | solution.py:196
  97.6 4.4 %all-to-all-done.4 = bf16[8,16,1024]{2,1,0:T(8,128)(2,1)S(1)} async-done(((bf16[8,16,1024]{2,1,0:T(8,128)(2,1)}), bf16[8,16,1024]{2,1,0:T(8,128)(2,1)S(1)}, u32[]{:S(2)}, u32[]{:S(2)}) %all-to-all-start.4) | async-done | bytes 262176 | tf_op jit(solution)/shard_map/level3_up/all_to_all | solution.py:17
  103.1 4.3 %all-to-all-start.5 = ((bf16[8,16,512]{2,1,0:T(8,128)(2,1)}), bf16[8,16,512]{2,1,0:T(8,128)(2,1)S(1)}, u32[]{:S(2)}, u32[]{:S(2)}) async-start(bf16[8,16,512]{2,1,0:T(8,128)(2,1)} %broadcast_in_dim.101), calls=%async_computation.5 | async-start | bytes 262144 | tf_op jit(solution)/shard_map/level3_down/all_to_all | solution.py:17
  107.6 5.1 %all-to-all-done.5 = bf16[8,16,512]{2,1,0:T(8,128)(2,1)S(1)} async-done(((bf16[8,16,512]{2,1,0:T(8,128)(2,1)}), bf16[8,16,512]{2,1,0:T(8,128)(2,1)S(1)}, u32[]{:S(2)}, u32[]{:S(2)}) %all-to-all-start.5) | async-done | bytes 131104 | tf_op jit(solution)/shard_map/level3_down/all_to_all | solution.py:17
  113.7 4.1 %all-to-all-start.6 = ((bf16[8,16,256]{2,1,0:T(8,128)(2,1)}), bf16[8,16,256]{2,1,0:T(8,128)(2,1)S(1)}, u32[]{:S(2)}, u32[]{:S(2)}) async-start(bf16[8,16,256]{2,1,0:T(8,128)(2,1)} %broadcast_in_dim.102), calls=%async_computation.6 | async-start | bytes 131072 | tf_op jit(solution)/shard_map/local_down/all_to_all | solution.py:17
  117.9 4.8 %all-to-all-done.6 = bf16[8,16,256]{2,1,0:T(8,128)(2,1)S(1)} async-done(((bf16[8,16,256]{2,1,0:T(8,128)(2,1)}), bf16[8,16,256]{2,1,0:T(8,128)(2,1)S(1)}, u32[]{:S(2)}, u32[]{:S(2)}) %all-to-all-start.6) | async-done | bytes 65568 | tf_op jit(solution)/shard_map/local_down/all_to_all | solution.py:17
  123.4 8.0 %all_to_all.40 = bf16[8,16,256]{2,1,0:T(8,128)(2,1)S(1)} all-to-all(bf16[8,16,256]{2,1,0:T(8,128)(2,1)S(1)} %bitcast.147), channel_id=1, replica_groups=mesh['sub'=8,'a'=2,'b'=2,'c'=2,'front'=8] {'front'}, dimensions={0} | all-to-all | bytes 131072 | tf_op jit(solution)/shard_map/leaf_upper/all_to_all | solution.py:17
  (155 shorter events, 14.4 us)
Async XLA Ops:
  0.0 26.0 %copy-start = (bf16[128,1024]{1,0:T(8,128)(2,1)S(1)}, bf16[128,1024]{1,0:T(8,128)(2,1)}, u32[]{:S(2)}) copy-start(bf16[128,1024]{1,0:T(8,128)(2,1)} %param.12) | copy-start | bytes 786436
  0.0 1.2 slice-start.5
  4.0 10.4 %copy-start.2 = (bf16[16,1792]{1,0:T(8,128)(2,1)S(1)}, bf16[16,1792]{1,0:T(8,128)(2,1)}, u32[]{:S(2)}) copy-start(bf16[16,1792]{1,0:T(8,128)(2,1)} %param.17) | copy-start | bytes 172036
  4.0 10.4 %slice-start.6 = ((bf16[16,1536]{1,0:T(8,128)(2,1)}), bf16[16,512]{1,0:T(8,128)(2,1)S(1)}, s32[]{:S(2)}) async-start(bf16[16,1536]{1,0:T(8,128)(2,1)} %param.18), calls=%async_computation.14 | async-start | bytes 32768 | tf_op jit(solution)/shard_map/planes_level2/slice | solution.py:89
  4.0 12.5 %slice-start.7 = ((bf16[16,1536]{1,0:T(8,128)(2,1)}), bf16[16,1024]{1,0:T(8,128)(2,1)S(1)}, s32[]{:S(2)}) async-start(bf16[16,1536]{1,0:T(8,128)(2,1)} %param.18), calls=%async_computation.15 | async-start | bytes 65536 | tf_op jit(solution)/shard_map/planes_level3/slice | solution.py:97
  4.0 12.5 %slice-start.1 = ((bf16[16,1792]{1,0:T(8,128)(2,1)}), bf16[16,1024]{1,0:T(8,128)(2,1)S(1)}, s32[]{:S(2)}) async-start(bf16[16,1792]{1,0:T(8,128)(2,1)} %param.17), calls=%async_computation.9 | async-start | bytes 65536 | tf_op jit(solution)/shard_map/planes_level3/slice | solution.py:98
  4.0 21.4 %copy-start.5 = (s32[1,1408]{1,0:T(1,128)S(1)}, s32[1,1408]{1,0:T(1,128)}, u32[]{:S(2)}) copy-start(s32[1,1408]{1,0:T(1,128)} %param.11) | copy-start | bytes 16900
  4.0 28.8 %all-to-all-start = ((bf16[16,16,1280]{2,1,0:T(8,128)(2,1)}), bf16[16,16,1280]{2,1,0:T(8,128)(2,1)S(1)}, u32[]{:S(2)}, u32[]{:S(2)}) async-start(bf16[16,16,1280]{2,1,0:T(8,128)(2,1)} %concatenate.39), calls=%async_computation | async-start | bytes 1310720 | tf_op jit(solution)/shard_map/first_exchange/all_to_all | solution.py:17
  14.5 13.5 %collective-permute-start = (bf16[16,768]{1,0:T(8,128)(2,1)S(1)}, bf16[16,768]{1,0:T(8,128)(2,1)S(1)}, u32[]{:S(2)}, u32[]{:S(2)}) collective-permute-start(bf16[16,768]{1,0:T(8,128)(2,1)S(1)} %pad_maximum_fusion.12), channel_id=1, source_target_pairs={{0,16},{16,0},{1,17},{17,1},{2,18},{18,2},{3,19},{19,3},{4,20},{20... | collective-permute-start | bytes 73736 | tf_op jit(solution)/shard_map/planes_level2/ppermute | solution.py:30
  16.6 15.6 %collective-permute-start.2 = (bf16[16,1536]{1,0:T(8,128)(2,1)S(1)}, bf16[16,1536]{1,0:T(8,128)(2,1)S(1)}, u32[]{:S(2)}, u32[]{:S(2)}) collective-permute-start(bf16[16,1536]{1,0:T(8,128)(2,1)S(1)} %get-tuple-element.77), channel_id=1, source_target_pairs={{0,32},{32,0},{1,33},{33,1},{2,34},{34,2},{3,35},{35,3},{4,36},{36... | collective-permute-start | bytes 147464 | tf_op jit(solution)/shard_map/planes_level3/ppermute | solution.py:30
  26.0 5.3 %copy-start.1 = (bf16[128,1024]{1,0:T(8,128)(2,1)S(1)}, bf16[128,1024]{1,0:T(8,128)(2,1)}, u32[]{:S(2)}) copy-start(bf16[128,1024]{1,0:T(8,128)(2,1)} %param.13) | copy-start | bytes 786436
  28.0 4.8 %collective-permute-start.1 = (bf16[2,16,768]{2,1,0:T(8,128)(2,1)S(1)}, bf16[2,16,768]{2,1,0:T(8,128)(2,1)S(1)}, u32[]{:S(2)}, u32[]{:S(2)}) collective-permute-start(bf16[2,16,768]{2,1,0:T(8,128)(2,1)S(1)} %pad_maximum_fusion.11), channel_id=1, source_target_pairs={{0,8},{8,0},{1,9},{9,1},{2,10},{10,2},{3,11},{11,3},{4,12},{12,4},... | collective-permute-start | bytes 147464 | tf_op jit(solution)/shard_map/planes_level2/ppermute | solution.py:30
  34.2 18.2 %all-to-all-start.1 = ((bf16[16,16,384]{2,1,0:T(8,128)(2,1)}), bf16[16,16,384]{2,1,0:T(8,128)(2,1)S(1)}, u32[]{:S(2)}, u32[]{:S(2)}) async-start(bf16[16,16,384]{2,1,0:T(8,128)(2,1)} %broadcast_in_dim.96), calls=%async_computation.1 | async-start | bytes 393216 | tf_op jit(solution)/shard_map/level1_up/all_to_all | solution.py:17
  41.7 17.8 %collective-permute-start.3 = (bf16[256,256]{1,0:T(8,128)(2,1)S(1)}, bf16[256,256]{1,0:T(8,128)(2,1)S(1)}, u32[]{:S(2)}, u32[]{:S(2)}) collective-permute-start(bf16[256,256]{1,0:T(8,128)(2,1)S(1)} %bitcast.133), channel_id=1, source_target_pairs={{0,16},{16,0},{1,17},{17,1},{2,18},{18,2},{3,19},{19,3},{4,20},{20... | collective-permute-start | bytes 393224 | tf_op jit(solution)/shard_map/planes_middle/ppermute | solution.py:30
  43.7 15.9 %collective-permute-start.4 = (bf16[256,128]{1,0:T(8,128)(2,1)S(1)}, bf16[256,128]{1,0:T(8,128)(2,1)S(1)}, u32[]{:S(2)}, u32[]{:S(2)}) collective-permute-start(bf16[256,128]{1,0:T(8,128)(2,1)S(1)} %bitcast.150), channel_id=1, source_target_pairs={{0,32},{32,0},{1,33},{33,1},{2,34},{34,2},{3,35},{35,3},{4,36},{36... | collective-permute-start | bytes 196616 | tf_op jit(solution)/shard_map/planes_middle/ppermute | solution.py:30
  48.1 11.5 %collective-permute-start.5 = (bf16[2,16,1536]{2,1,0:T(8,128)(2,1)S(1)}, bf16[2,16,1536]{2,1,0:T(8,128)(2,1)S(1)}, u32[]{:S(2)}, u32[]{:S(2)}) collective-permute-start(bf16[2,16,1536]{2,1,0:T(8,128)(2,1)S(1)} %pad_maximum_fusion.8), channel_id=1, source_target_pairs={{0,16},{16,0},{1,17},{17,1},{2,18},{18,2},{3,19},{19,3},{4,20},{20... | collective-permute-start | bytes 294920 | tf_op jit(solution)/shard_map/planes_middle/ppermute | solution.py:30
  60.4 10.9 %all-to-all-start.2 = ((bf16[8,16,512]{2,1,0:T(8,128)(2,1)}), bf16[8,16,512]{2,1,0:T(8,128)(2,1)S(1)}, u32[]{:S(2)}, u32[]{:S(2)}) async-start(bf16[8,16,512]{2,1,0:T(8,128)(2,1)} %broadcast_in_dim.98), calls=%async_computation.2 | async-start | bytes 262144 | tf_op jit(solution)/shard_map/level2_up/all_to_all | solution.py:17
  65.9 10.0 %collective-permute-start.6 = (bf16[2,2,16,1536]{3,2,1,0:T(8,128)(2,1)S(1)}, bf16[2,2,16,1536]{3,2,1,0:T(8,128)(2,1)S(1)}, u32[]{:S(2)}, u32[]{:S(2)}) collective-permute-start(bf16[2,2,16,1536]{3,2,1,0:T(8,128)(2,1)S(1)} %pad_maximum_fusion.4), channel_id=1, source_target_pairs={{0,8},{8,0},{1,9},{9,1},{2,10},{10,2},{3,11},{11,3},{4,12},{12,4},... | collective-permute-start | bytes 589832 | tf_op jit(solution)/shard_map/level2_up/ppermute | solution.py:30
  68.3 20.3 %collective-permute-start.7 = (bf16[2,256,128]{2,1,0:T(8,128)(2,1)S(1)}, bf16[2,256,128]{2,1,0:T(8,128)(2,1)S(1)}, u32[]{:S(2)}, u32[]{:S(2)}) collective-permute-start(bf16[2,256,128]{2,1,0:T(8,128)(2,1)S(1)} %pad_maximum_fusion.6), channel_id=1, source_target_pairs={{0,16},{16,0},{1,17},{17,1},{2,18},{18,2},{3,19},{19,3},{4,20},{20... | collective-permute-start | bytes 393224 | tf_op jit(solution)/shard_map/level2_up/ppermute | solution.py:30
  76.2 12.4 %all-to-all-start.3 = ((bf16[8,128,128]{1,2,0:T(8,128)(2,1)}), bf16[8,128,128]{1,2,0:T(8,128)(2,1)S(1)}, u32[]{:S(2)}, u32[]{:S(2)}) async-start(bf16[8,128,128]{1,2,0:T(8,128)(2,1)} %bitcast.37), calls=%async_computation.3 | async-start | bytes 524288 | tf_op jit(solution)/shard_map/level3_up/all_to_all | solution.py:17
  89.6 12.5 %all-to-all-start.4 = ((bf16[8,16,1024]{2,1,0:T(8,128)(2,1)}), bf16[8,16,1024]{2,1,0:T(8,128)(2,1)S(1)}, u32[]{:S(2)}, u32[]{:S(2)}) async-start(bf16[8,16,1024]{2,1,0:T(8,128)(2,1)} %broadcast_in_dim.100), calls=%async_computation.4 | async-start | bytes 524288 | tf_op jit(solution)/shard_map/level3_up/all_to_all | solution.py:17
  103.1 9.6 %all-to-all-start.5 = ((bf16[8,16,512]{2,1,0:T(8,128)(2,1)}), bf16[8,16,512]{2,1,0:T(8,128)(2,1)S(1)}, u32[]{:S(2)}, u32[]{:S(2)}) async-start(bf16[8,16,512]{2,1,0:T(8,128)(2,1)} %broadcast_in_dim.101), calls=%async_computation.5 | async-start | bytes 262144 | tf_op jit(solution)/shard_map/level3_down/all_to_all | solution.py:17
  107.5 15.4 %copy-start.3 = (bf16[128,256]{1,0:T(8,128)(2,1)S(1)}, bf16[128,256]{1,0:T(8,128)(2,1)}, u32[]{:S(2)}) copy-start(bf16[128,256]{1,0:T(8,128)(2,1)} %param.15) | copy-start | bytes 196612
  113.7 9.0 %all-to-all-start.6 = ((bf16[8,16,256]{2,1,0:T(8,128)(2,1)}), bf16[8,16,256]{2,1,0:T(8,128)(2,1)S(1)}, u32[]{:S(2)}, u32[]{:S(2)}) async-start(bf16[8,16,256]{2,1,0:T(8,128)(2,1)} %broadcast_in_dim.102), calls=%async_computation.6 | async-start | bytes 131072 | tf_op jit(solution)/shard_map/local_down/all_to_all | solution.py:17
  (6 other events, 4.9 us)

commit v4 on v3

v4 whole, which is shorter than its diff:
```python
import jax
import jax.numpy as jnp
from jax import lax
from jax.sharding import Mesh, PartitionSpec as P

AXES = ("sub", "a", "b", "c", "front")
PAIR = ("c", "front")
BF = jnp.bfloat16
WIDE = 256


def mm(x, w):
    return lax.dot_general(x, w, (((1,), (1,)), ((), ())), preferred_element_type=jnp.float32)


def exchange(x, axes):
    return lax.all_to_all(x, axes, 0, 0)


def copies(x, axes):
    return jnp.broadcast_to(x[None], (lax.axis_size(axes),) + x.shape)


def total(parts):
    return jnp.sum(parts.astype(jnp.float32), axis=0)


def swap(x, axis):
    return lax.ppermute(x, axis, [(0, 1), (1, 0)])


def ordered(mine, other, index, at):
    low = jnp.where(index == 0, mine, other)
    high = jnp.where(index == 0, other, mine)
    return jnp.stack([low, high], at)


def after(x, y):
    return lax.optimization_barrier((x, y))[0]


def tiles(m):
    return [m[:, i : i + 128] for i in range(0, m.shape[1], 128)]


def columns(m, index, width):
    return lax.dynamic_slice_in_dim(m, index * width, width, 1)


def local(
    basis,
    order,
    leaf_inverse,
    leaf_upper_inverse,
    leaf_coupling_low,
    leaf_coupling_up,
    sep_lower_inverse,
    sep_upper_inverse,
    sep_coupling_low,
    sep_coupling_up,
):
    ia, ib, ic = (lax.axis_index(n) for n in ("a", "b", "c"))
    f = lax.axis_index("front")
    leaf = 4 * ia + 2 * ib + ic

    with jax.named_scope("first_exchange"):

        def by_front(m, groups):
            m = jnp.transpose(m.reshape(-1, groups, 8, 16), (2, 0, 1, 3))
            return m.reshape(8, -1, groups * 16)

        def per_front(m):
            return jnp.broadcast_to(m[None], (2,) + m.shape).reshape((16,) + m.shape[1:])

        def for_all(m):
            return jnp.broadcast_to(m[None], (16,) + m.shape)

        low = jnp.transpose(leaf_coupling_low.reshape(16, 16, 128), (1, 0, 2))
        moved = jnp.concatenate(
            [
                for_all(jnp.pad(basis, ((0, 0), (0, 16)))),
                per_front(by_front(sep_lower_inverse[:, 256:768], 4)),
                for_all(sep_lower_inverse[:, :256]),
                low,
                per_front(by_front(sep_lower_inverse[:, 768:], 8)),
                per_front(by_front(sep_coupling_up[:, 512:], 8)),
            ],
            2,
        )
        got = exchange(moved, PAIR)

    with jax.named_scope("order"):
        place = (order[0] // 176) * WIDE + order[0] % 176
        slots = place.reshape(8, 176)
        leaf_place = slots[:, :128].reshape(1024)
        own_place = lax.dynamic_index_in_dim(slots, f, 0, keepdims=False)[128:]
        wide = 8 * WIDE
        hot = (leaf_place[:, None] == lax.broadcasted_iota(jnp.int32, (1024, wide), 1)).astype(BF)
        own_hot = (own_place[:, None] == lax.broadcasted_iota(jnp.int32, (48, wide), 1)).astype(BF)
        lower = lax.dot_general(leaf_inverse, hot, (((1,), (0,)), ((), ())), preferred_element_type=jnp.float32)
        lower = jnp.concatenate([lower.astype(BF), own_hot], 0)

    with jax.named_scope("planes_first"):
        g2 = sep_coupling_low[:, :512]
        more = jnp.concatenate([sep_upper_inverse[:, 256:768], sep_coupling_low[:, 512:]], 1)
        rows = jnp.concatenate([columns(g2, ib, 256), more], 1)
        rows_other = jnp.concatenate([columns(g2, 1 - ib, 256), more], 1)
        lower, rows_other = lax.optimization_barrier((lower, rows_other))
        rows_other = swap(rows_other, "b")

    got, rows, rows_other = lax.optimization_barrier((got, rows, rows_other))

    with jax.named_scope("unpack"):
        grouped = lax.dynamic_slice_in_dim(got[:, :, :WIDE], ic * 8, 8, 0)
        a2 = got[:, :, 192:256].reshape(256, 64)
        a1 = got[:, :, 256:512].reshape(256, 256)
        low_cols = got[:, :, 512:640].reshape(256, 128)
        a3 = got[:, :, 640:768].reshape(256, 128)
        h2 = got[:, :, 768:896].reshape(256, 128)
        rows = ordered(rows, rows_other, ib, 0).reshape(32, 1792)

    with jax.named_scope("planes_second"):
        level1 = jnp.concatenate([sep_upper_inverse[:, :256], sep_coupling_up[:, :512]], 1)
        level2 = jnp.concatenate([rows[:, :768], level1], 0)
        g3 = rows[:, 768:]
        tail = tiles(sep_upper_inverse[:, 768:]) + [a3]
        level3 = jnp.concatenate(tiles(columns(g3, ia, 512)) + tail, 0)
        level3_other = jnp.concatenate(tiles(columns(g3, 1 - ia, 512)) + tail, 0)
    with jax.named_scope("weights1"):
        row = lax.broadcasted_iota(jnp.int32, (384, 48), 0)
        col = lax.broadcasted_iota(jnp.int32, (384, 48), 1)
        target = jnp.where(col < 16, (ic * 8 + f) * 16 + col, 240 + col)
        keep = (row == target).astype(BF)
        first = jnp.concatenate([jnp.pad(-low_cols, ((0, 128), (0, 0))), keep], 1)

    with jax.named_scope("leaf_lower"):
        grouped = jnp.transpose(grouped, (1, 0, 2)).reshape(16, wide)
        own = mm(grouped, lower).astype(BF)
        y_leaf = own[:, :128]

    with jax.named_scope("level1_up"):
        sent = copies(mm(own, first).astype(BF), PAIR)
        level2_other = swap(after(level2, sent), "c")
        level3_other = swap(after(level3_other, sent), "a")
        got = exchange(sent, PAIR)
        got, level2, level2_other = lax.optimization_barrier((got, level2, level2_other))
        level2 = ordered(level2, level2_other, ic, 0)
        level1 = level2[:, 32:].reshape(32, 768)
        level2 = jnp.transpose(level2[:, :32].reshape(2, 2, 16, 768), (1, 0, 2, 3)).reshape(64, 768)
        g2 = level2[:, :256]
        b2 = level2[:, 256:]
        b1 = level1[:, :256]
        h1 = level1[:, 256:]
        c1 = total(got[:, :, :256]).astype(BF)
        rest = lax.dynamic_index_in_dim(got[:, :, 256:288].reshape(2, 8, 16, 32), f, 1, keepdims=False)
        rhs2 = jnp.transpose(rest[:, :, :16], (1, 0, 2)).reshape(16, 32)
        rhs3 = jnp.transpose(rest[:, :, 16:], (1, 0, 2)).reshape(16, 32)
        y1 = mm(c1, a1).astype(BF)

    with jax.named_scope("level2_up"):
        half = lax.broadcasted_iota(jnp.int32, (16, 64), 1) // 32
        part = jnp.where(half == ib, jnp.concatenate([rhs2, rhs2], 1).astype(jnp.float32), 0.0) - mm(y1, g2)
        part = jnp.concatenate([part.astype(BF), jnp.pad(rhs3, ((0, 0), (0, 32)))], 1)
        a2 = jnp.concatenate([a2[:128], a2[128:]], 1)
        got = lax.all_gather(jnp.concatenate([part, a2], 0), "b")
        a2 = jnp.concatenate([got[:, 16:144, :64], got[:, 16:144, 64:]], 1).reshape(512, 64)
        c2 = total(got[:, :16, :64]).astype(BF)
        rhs3 = jnp.transpose(got[:, :16, 64:96], (1, 0, 2)).reshape(16, 64)
        sent = copies(mm(c2, a2).astype(BF), "front")
        level3, level3_other = after((level3, level3_other), sent)
        level3 = ordered(level3, level3_other, ia, 0)
        g3 = level3[:, :128].reshape(256, 128)
        g3_other = swap(g3, "c")
        mixed = [level3[:, 256:].reshape(512, 128), level3[:, 128:256].reshape(256, 128), h2]
        mixed = jnp.concatenate(mixed, 0)
        mixed, g3_other = lax.optimization_barrier((mixed, g3_other))
        mixed_other = swap(mixed, "b")
        got = exchange(sent, "front")
        got, g3, g3_other = lax.optimization_barrier((got, g3, g3_other))
        g3 = ordered(g3, g3_other, ic, 0).reshape(2, 2, 4, 2, 16, 128)
        g3 = jnp.transpose(g3, (1, 3, 0, 4, 2, 5)).reshape(128, 512)
        y2 = total(got).astype(BF)

    with jax.named_scope("level3_up"):
        half = lax.broadcasted_iota(jnp.int32, (16, 128), 1) // 64
        part = jnp.where(half == ia, jnp.concatenate([rhs3, rhs3], 1).astype(jnp.float32), 0.0) - mm(y2, g3)
        part = part.astype(BF)
        up = jnp.transpose(leaf_upper_inverse.reshape(128, 8, 128), (1, 0, 2))
        down = by_front(h1, 4)
        down = jnp.concatenate([down[:, :16], down[:, 16:]], 2)
        whole = jnp.broadcast_to(jnp.concatenate(tiles(b1), 0)[None], (8, 64, 128))
        up = jnp.concatenate([up, whole, down], 1)
        up = after(up, y2)
        up = exchange(up, "front")
        got = lax.all_gather(part, "a")
        got, up, mixed, mixed_other = lax.optimization_barrier((got, up, mixed, mixed_other))
        b1 = jnp.transpose(up[:, 128:192].reshape(8, 2, 2, 16, 128), (2, 0, 3, 1, 4)).reshape(256, 256)
        h1 = jnp.transpose(up[:, 192:].reshape(8, 16, 2, 64), (2, 0, 1, 3)).reshape(256, 64)
        up = up[:, :128].reshape(1024, 128)
        mixed = ordered(mixed, mixed_other, ib, 0)
        a3 = jnp.transpose(mixed[:, :512].reshape(2, 2, 256, 128), (1, 0, 2, 3)).reshape(1024, 128)
        b3 = mixed[:, 512:768].reshape(512, 128)
        h2 = mixed[:, 768:].reshape(512, 128)
        c3 = total(got).astype(BF)
        sent = copies(mm(c3, a3).astype(BF), "front")
        b3_other = swap(after(b3, sent), "c")
        got = exchange(sent, "front")
        got, b3, b3_other = lax.optimization_barrier((got, b3, b3_other))
        b3 = ordered(b3, b3_other, ic, 0).reshape(2, 2, 2, 8, 16, 128)
        b3 = jnp.transpose(b3, (2, 1, 0, 4, 3, 5)).reshape(128, 1024)
        y3 = total(got).astype(BF)

    with jax.named_scope("level3_down"):
        z3 = mm(y3, b3).astype(BF)
        upper = lax.dot_general(hot, up, (((0,), (0,)), ((), ())), preferred_element_type=jnp.float32)
        upper = jnp.concatenate([upper.astype(BF), own_hot.T], 1)
        got = exchange(copies(mm(z3, h2).astype(BF), "front"), "front")
        got, upper = lax.optimization_barrier((got, upper))
        w2 = (y2.astype(jnp.float32) - total(got)).astype(BF)

    with jax.named_scope("local_down"):
        z2 = mm(w2, b2).astype(BF)
        w1 = (y1.astype(jnp.float32) - total(exchange(copies(mm(z2, h1).astype(BF), "front"), "front"))).astype(BF)
        z1 = mm(w1, b1).astype(BF)
        w_leaf = (y_leaf.astype(jnp.float32) - mm(z1, leaf_coupling_up)).astype(BF)
        own = jnp.concatenate(
            [
                w_leaf,
                columns(z1, ic * 8 + f, 16),
                columns(z2, 2 * ib + ic, 16),
                columns(z3, leaf, 16),
            ],
            1,
        )

    with jax.named_scope("leaf_upper"):
        out = mm(own, upper).astype(BF)
        out = jnp.transpose(out.reshape(16, 8, WIDE), (1, 0, 2))
        return total(exchange(out, "front"))[:, :176].astype(BF)


def solution(mesh):
    fronts = mesh.shape["front"]
    grid = Mesh(mesh.devices.reshape(-1, 2, 2, 2, fronts), AXES)
    rows = P(AXES, None)
    in_specs = (P(None, AXES), P(AXES[:4], None)) + (rows,) * 8
    return jax.shard_map(local, mesh=grid, in_specs=in_specs, out_specs=P(None, AXES), check_vma=False)
```

time: 133 us -> 124 us (0.932)
  starting transfers between devices: 72.7 us -> 64.1 us
    ppermute x8 -> x6, starting transfers between devices: 29.9 us -> 21.1 us  [swap(): return lax.ppermute(x, axis, [(0, 1), (1, 0)])]
    ppermute x8 -> x6, waiting for transfers between devices: 5.23 us -> 8.36 us  [swap(): return lax.ppermute(x, axis, [(0, 1), (1, 0)])]
    all_to_all x7, waiting for transfers between devices: 14.4 us -> 11.5 us  [exchange(): return lax.all_to_all(x, axes, 0, 0)]
    broadcast_in_dim x5 -> x6, local copies, waits for them, and re-layouts: 3.51 us -> 3.54 us  [the longest x5 3.49 us: copies(): return jnp.broadcast_to(x[None], (lax.axis_size(axes),) + x.shape)]
  transfers between devices with their start and end apart: 15 -> 13, of which waited for: 5 -> 7; matrix products, arithmetic and copies ran while one was open for 5% -> 7% of each run, Pallas kernels for 0% -> 0%
where the time goes in v4:
time: 124 us; the launch traced here: 123 us
  starting transfers between devices  64.1 us (52%)
  blocking collectives  20.3 us (16%)
  waiting for transfers between devices  19.8 us (16%)
  local copies, waits for them, and re-layouts  10.2 us (8%)
  matrix products  6.09 us (5%)
  other arithmetic  1.88 us (2%)
    all_to_all x7, starting transfers between devices, exchange(): return lax.all_to_all(x, axes, 0, 0)  43 us
    ppermute x6, starting transfers between devices, swap(): return lax.ppermute(x, axis, [(0, 1), (1, 0)])  21.1 us
    all_to_all x7, waiting for transfers between devices, exchange(): return lax.all_to_all(x, axes, 0, 0)  11.5 us
    ppermute x6, waiting for transfers between devices, swap(): return lax.ppermute(x, axis, [(0, 1), (1, 0)])  8.36 us
    all_to_all x1, blocking collectives, exchange(): return lax.all_to_all(x, axes, 0, 0)  8 us
    all_gather x1, blocking collectives, local(): got = lax.all_gather(part, 'a')  7.1 us
    all_gather x1, blocking collectives, local(): got = lax.all_gather(jnp.concatenate([part, a2], 0), 'b')  5.19 us
    broadcast_in_dim x5, local copies, waits for them, and re-layouts, copies(): return jnp.broadcast_to(x[None], (lax.axis_size(axes),) + x.shape)  3.49 us
  transfers between devices with their start and end apart: 13, of which 7 were waited for; matrix products, arithmetic and copies ran while one was open for 7% of the time, Pallas kernels for 0%

profile of v4, /device:TPU:1, one launch (start us, length us, event | category | flops | bytes accessed | tf_op | source)
XLA Modules:
  0.0 123.3 jit_solution(11715658360720075050)
XLA Ops:
  3.4 10.3 %all-to-all-start = ((bf16[16,16,896]{2,1,0:T(8,128)(2,1)}), bf16[16,16,896]{2,1,0:T(8,128)(2,1)S(1)}, u32[]{:S(2)}, u32[]{:S(2)}) async-start(bf16[16,16,896]{2,1,0:T(8,128)(2,1)} %concatenate.68), calls=%async_computation | async-start | bytes 917504 | tf_op jit(solution)/shard_map/first_exchange/all_to_all | solution.py:17
  14.3 1.8 %fusion.6 = bf16[128,2048]{1,0:T(8,128)(2,1)S(1)} fusion(bf16[128,1024]{1,0:T(8,128)(2,1)S(1)} %copy-done, s32[1024]{0:T(1024)S(1)} %slice_bitcast_fusion.3), kind=kOutput, calls=%fused_computation.7 | convolution fusion | flops 539230208 | bytes 790528 | tf_op jit(solution)/shard_map/order/dot_general | solution.py:100
  16.3 2.1 %collective-permute-start = (bf16[16,1792]{1,0:T(8,128)(2,1)S(1)}, bf16[16,1792]{1,0:T(8,128)(2,1)S(1)}, u32[]{:S(2)}, u32[]{:S(2)}) collective-permute-start(bf16[16,1792]{1,0:T(8,128)(2,1)S(1)} %get-tuple-element.33), channel_id=1, source_target_pairs={{0,16},{16,0},{1,17},{17,1},{2,18},{18,2},{3,19},{19,3},{4,20},{20... | collective-permute-start | bytes 172040 | tf_op jit(solution)/shard_map/planes_first/ppermute | solution.py:29
  18.8 3.3 %collective-permute-done = bf16[16,1792]{1,0:T(8,128)(2,1)S(1)} collective-permute-done((bf16[16,1792]{1,0:T(8,128)(2,1)S(1)}, bf16[16,1792]{1,0:T(8,128)(2,1)S(1)}, u32[]{:S(2)}, u32[]{:S(2)}) %collective-permute-start) | collective-permute-done | bytes 57376 | tf_op jit(solution)/shard_map/planes_first/ppermute | solution.py:29
  24.2 6.5 %all-to-all-start.1 = ((bf16[16,16,384]{2,1,0:T(8,128)(2,1)}), bf16[16,16,384]{2,1,0:T(8,128)(2,1)S(1)}, u32[]{:S(2)}, u32[]{:S(2)}) async-start(bf16[16,16,384]{2,1,0:T(8,128)(2,1)} %broadcast_in_dim.44), calls=%async_computation.1 | async-start | bytes 393216 | tf_op jit(solution)/shard_map/level1_up/all_to_all | solution.py:17
  30.8 3.3 %collective-permute-start.1 = (bf16[48,768]{1,0:T(8,128)(2,1)S(1)}, bf16[48,768]{1,0:T(8,128)(2,1)S(1)}, u32[]{:S(2)}, u32[]{:S(2)}) collective-permute-start(bf16[48,768]{1,0:T(8,128)(2,1)S(1)} %maximum_maximum_fusion.1), channel_id=1, source_target_pairs={{0,8},{8,0},{1,9},{9,1},{2,10},{10,2},{3,11},{11,3},{4,12},{12,4},... | collective-permute-start | bytes 221192 | tf_op jit(solution)/shard_map/level1_up/ppermute | solution.py:29
  34.5 6.6 %collective-permute-start.2 = (bf16[512,128]{1,0:T(8,128)(2,1)S(1)}, bf16[512,128]{1,0:T(8,128)(2,1)S(1)}, u32[]{:S(2)}, u32[]{:S(2)}) collective-permute-start(bf16[512,128]{1,0:T(8,128)(2,1)S(1)} %get-tuple-element.42), channel_id=1, source_target_pairs={{0,32},{32,0},{1,33},{33,1},{2,34},{34,2},{3,35},{35,3},{4,36},{36... | collective-permute-start | bytes 393224 | tf_op jit(solution)/shard_map/level1_up/ppermute | solution.py:29
  41.9 5.2 %all-gather = bf16[288,128]{1,0:T(8,128)(2,1)S(1)} all-gather(bf16[144,128]{1,0:T(8,128)(2,1)S(1)} %fusion.35), channel_id=2, replica_groups=mesh['sub'=8,'a'=2,'b'=2,'c'=2,'front'=8] {'b'}, dimensions={0}, use_global_device_ids=true | all-gather | bytes 110592 | tf_op jit(solution)/shard_map/level2_up/all_gather | solution.py:165
  48.1 6.3 %all-to-all-start.2 = ((bf16[8,16,512]{2,1,0:T(8,128)(2,1)}), bf16[8,16,512]{2,1,0:T(8,128)(2,1)S(1)}, u32[]{:S(2)}, u32[]{:S(2)}) async-start(bf16[8,16,512]{2,1,0:T(8,128)(2,1)} %broadcast_in_dim.88), calls=%async_computation.2 | async-start | bytes 262144 | tf_op jit(solution)/shard_map/level2_up/all_to_all | solution.py:17
  54.5 2.0 %collective-permute-start.3 = (bf16[256,128]{1,0:T(8,128)(2,1)S(1)}, bf16[256,128]{1,0:T(8,128)(2,1)S(1)}, u32[]{:S(2)}, u32[]{:S(2)}) collective-permute-start(bf16[256,128]{1,0:T(8,128)(2,1)S(1)} %bitcast.179), channel_id=1, source_target_pairs={{0,8},{8,0},{1,9},{9,1},{2,10},{10,2},{3,11},{11,3},{4,12},{12,4},... | collective-permute-start | bytes 196616 | tf_op jit(solution)/shard_map/level2_up/ppermute | solution.py:29
  57.3 2.8 %collective-permute-done.3 = bf16[256,128]{1,0:T(8,128)(2,1)S(1)} collective-permute-done((bf16[256,128]{1,0:T(8,128)(2,1)S(1)}, bf16[256,128]{1,0:T(8,128)(2,1)S(1)}, u32[]{:S(2)}, u32[]{:S(2)}) %collective-permute-start.3) | collective-permute-done | bytes 65568 | tf_op jit(solution)/shard_map/level2_up/ppermute | solution.py:29
  60.1 4.3 %collective-permute-start.4 = (bf16[1024,128]{1,0:T(8,128)(2,1)S(1)}, bf16[1024,128]{1,0:T(8,128)(2,1)S(1)}, u32[]{:S(2)}, u32[]{:S(2)}) collective-permute-start(bf16[1024,128]{1,0:T(8,128)(2,1)S(1)} %pad_maximum_fusion.2), channel_id=1, source_target_pairs={{0,16},{16,0},{1,17},{17,1},{2,18},{18,2},{3,19},{19,3},{4,20},{20... | collective-permute-start | bytes 786440 | tf_op jit(solution)/shard_map/level2_up/ppermute | solution.py:29
  65.3 5.6 %all-to-all-start.3 = ((bf16[8,208,128]{2,1,0:T(8,128)(2,1)}), bf16[8,208,128]{2,1,0:T(8,128)(2,1)S(1)}, u32[]{:S(2)}, u32[]{:S(2)}) async-start(bf16[8,208,128]{2,1,0:T(8,128)(2,1)} %copy.110), calls=%async_computation.3 | async-start | bytes 851968 | tf_op jit(solution)/shard_map/level3_up/all_to_all | solution.py:17
  71.2 7.1 %all-gather.1 = bf16[32,128]{1,0:T(8,128)(2,1)S(1)} all-gather(bf16[16,128]{1,0:T(8,128)(2,1)S(1)} %fusion.8), channel_id=3, replica_groups=mesh['sub'=8,'a'=2,'b'=2,'c'=2,'front'=8] {'a'}, dimensions={0}, use_global_device_ids=true | all-gather | bytes 12288 | tf_op jit(solution)/shard_map/level3_up/all_gather | solution.py:195
  78.3 1.1 all-to-all-done.3
  80.5 4.9 %all-to-all-start.4 = ((bf16[8,16,1024]{2,1,0:T(8,128)(2,1)}), bf16[8,16,1024]{2,1,0:T(8,128)(2,1)S(1)}, u32[]{:S(2)}, u32[]{:S(2)}) async-start(bf16[8,16,1024]{2,1,0:T(8,128)(2,1)} %broadcast_in_dim.91), calls=%async_computation.4 | async-start | bytes 524288 | tf_op jit(solution)/shard_map/level3_up/all_to_all | solution.py:17
  85.4 2.8 %collective-permute-start.5 = (bf16[512,128]{1,0:T(8,128)(2,1)S(1)}, bf16[512,128]{1,0:T(8,128)(2,1)S(1)}, u32[]{:S(2)}, u32[]{:S(2)}) collective-permute-start(bf16[512,128]{1,0:T(8,128)(2,1)S(1)} %bitcast.159), channel_id=1, source_target_pairs={{0,8},{8,0},{1,9},{9,1},{2,10},{10,2},{3,11},{11,3},{4,12},{12,4},... | collective-permute-start | bytes 393224 | tf_op jit(solution)/shard_map/level3_up/ppermute | solution.py:29
  88.2 1.9 %fusion.5 = bf16[2048,128]{0,1:T(8,128)(2,1)S(1)} fusion(bf16[1024,128]{1,0:T(8,128)(2,1)S(1)} %bitcast.174, s32[1024]{0:T(1024)S(1)} %slice_bitcast_fusion.3), kind=kOutput, calls=%fused_computation.6 | convolution fusion | flops 539230208 | bytes 790528 | tf_op jit(solution)/shard_map/level3_down/dot_general | solution.py:215
  90.1 2.3 %collective-permute-done.5 = bf16[512,128]{1,0:T(8,128)(2,1)S(1)} collective-permute-done((bf16[512,128]{1,0:T(8,128)(2,1)S(1)}, bf16[512,128]{1,0:T(8,128)(2,1)S(1)}, u32[]{:S(2)}, u32[]{:S(2)}) %collective-permute-start.5) | collective-permute-done | bytes 131104 | tf_op jit(solution)/shard_map/level3_up/ppermute | solution.py:29
  93.6 5.2 %all-to-all-start.5 = ((bf16[8,16,512]{2,1,0:T(8,128)(2,1)}), bf16[8,16,512]{2,1,0:T(8,128)(2,1)S(1)}, u32[]{:S(2)}, u32[]{:S(2)}) async-start(bf16[8,16,512]{2,1,0:T(8,128)(2,1)} %broadcast_in_dim.92), calls=%async_computation.5 | async-start | bytes 262144 | tf_op jit(solution)/shard_map/level3_down/all_to_all | solution.py:17
  99.2 4.9 %all-to-all-done.5 = bf16[8,16,512]{2,1,0:T(8,128)(2,1)S(1)} async-done(((bf16[8,16,512]{2,1,0:T(8,128)(2,1)}), bf16[8,16,512]{2,1,0:T(8,128)(2,1)S(1)}, u32[]{:S(2)}, u32[]{:S(2)}) %all-to-all-start.5) | async-done | bytes 131104 | tf_op jit(solution)/shard_map/level3_down/all_to_all | solution.py:17
  105.0 4.1 %all-to-all-start.6 = ((bf16[8,16,256]{2,1,0:T(8,128)(2,1)}), bf16[8,16,256]{2,1,0:T(8,128)(2,1)S(1)}, u32[]{:S(2)}, u32[]{:S(2)}) async-start(bf16[8,16,256]{2,1,0:T(8,128)(2,1)} %broadcast_in_dim.93), calls=%async_computation.6 | async-start | bytes 131072 | tf_op jit(solution)/shard_map/local_down/all_to_all | solution.py:17
  109.2 4.8 %all-to-all-done.6 = bf16[8,16,256]{2,1,0:T(8,128)(2,1)S(1)} async-done(((bf16[8,16,256]{2,1,0:T(8,128)(2,1)}), bf16[8,16,256]{2,1,0:T(8,128)(2,1)S(1)}, u32[]{:S(2)}, u32[]{:S(2)}) %all-to-all-start.6) | async-done | bytes 65568 | tf_op jit(solution)/shard_map/local_down/all_to_all | solution.py:17
  114.7 8.0 %all_to_all.40 = bf16[8,16,256]{2,1,0:T(8,128)(2,1)S(1)} all-to-all(bf16[8,16,256]{2,1,0:T(8,128)(2,1)S(1)} %bitcast.177), channel_id=1, replica_groups=mesh['sub'=8,'a'=2,'b'=2,'c'=2,'front'=8] {'front'}, dimensions={0} | all-to-all | bytes 131072 | tf_op jit(solution)/shard_map/leaf_upper/all_to_all | solution.py:17
  (182 shorter events, 15.2 us)
Async XLA Ops:
  0.0 14.3 %copy-start = (bf16[128,1024]{1,0:T(8,128)(2,1)S(1)}, bf16[128,1024]{1,0:T(8,128)(2,1)}, u32[]{:S(2)}) copy-start(bf16[128,1024]{1,0:T(8,128)(2,1)} %param.12) | copy-start | bytes 786436
  0.0 1.2 slice-start.3
  3.4 10.4 %copy-start.5 = (s32[1,1408]{1,0:T(1,128)S(1)}, s32[1,1408]{1,0:T(1,128)}, u32[]{:S(2)}) copy-start(s32[1,1408]{1,0:T(1,128)} %param.11) | copy-start | bytes 16900
  3.4 19.5 %all-to-all-start = ((bf16[16,16,896]{2,1,0:T(8,128)(2,1)}), bf16[16,16,896]{2,1,0:T(8,128)(2,1)S(1)}, u32[]{:S(2)}, u32[]{:S(2)}) async-start(bf16[16,16,896]{2,1,0:T(8,128)(2,1)} %concatenate.68), calls=%async_computation | async-start | bytes 917504 | tf_op jit(solution)/shard_map/first_exchange/all_to_all | solution.py:17
  14.3 1.9 %slice-start.7 = ((bf16[16,1536]{1,0:T(8,128)(2,1)}), bf16[16,512]{1,0:T(8,128)(2,1)S(1)}, s32[]{:S(2)}) async-start(bf16[16,1536]{1,0:T(8,128)(2,1)} %param.18), calls=%async_computation.15 | async-start | bytes 32768 | tf_op jit(solution)/shard_map/planes_first/slice | solution.py:104
  14.3 1.9 %slice-start = ((bf16[16,1792]{1,0:T(8,128)(2,1)}), bf16[16,512]{1,0:T(8,128)(2,1)S(1)}, s32[]{:S(2)}) async-start(bf16[16,1792]{1,0:T(8,128)(2,1)} %param.17), calls=%async_computation.8 | async-start | bytes 32768 | tf_op jit(solution)/shard_map/planes_first/slice | solution.py:105
  14.3 1.9 %slice-start.6 = ((bf16[16,1536]{1,0:T(8,128)(2,1)}), bf16[16,1024]{1,0:T(8,128)(2,1)S(1)}, s32[]{:S(2)}) async-start(bf16[16,1536]{1,0:T(8,128)(2,1)} %param.18), calls=%async_computation.14 | async-start | bytes 65536 | tf_op jit(solution)/shard_map/planes_first/slice | solution.py:105
  16.3 2.2 %copy-start.1 = (bf16[128,1024]{1,0:T(8,128)(2,1)S(1)}, bf16[128,1024]{1,0:T(8,128)(2,1)}, u32[]{:S(2)}) copy-start(bf16[128,1024]{1,0:T(8,128)(2,1)} %param.13) | copy-start | bytes 786436
  16.3 5.8 %collective-permute-start = (bf16[16,1792]{1,0:T(8,128)(2,1)S(1)}, bf16[16,1792]{1,0:T(8,128)(2,1)S(1)}, u32[]{:S(2)}, u32[]{:S(2)}) collective-permute-start(bf16[16,1792]{1,0:T(8,128)(2,1)S(1)} %get-tuple-element.33), channel_id=1, source_target_pairs={{0,16},{16,0},{1,17},{17,1},{2,18},{18,2},{3,19},{19,3},{4,20},{20... | collective-permute-start | bytes 172040 | tf_op jit(solution)/shard_map/planes_first/ppermute | solution.py:29
  23.3 7.4 %slice-start.1 = ((bf16[16,1792]{1,0:T(8,128)(2,1)}), bf16[16,256]{1,0:T(8,128)(2,1)S(1)}, s32[]{:S(2)}) async-start(bf16[16,1792]{1,0:T(8,128)(2,1)} %param.17), calls=%async_computation.9 | async-start | bytes 16384 | tf_op jit(solution)/shard_map/planes_second/slice | solution.py:123
  23.3 7.4 %slice-start.5 = ((bf16[16,1536]{1,0:T(8,128)(2,1)}), bf16[16,512]{1,0:T(8,128)(2,1)S(1)}, s32[]{:S(2)}) async-start(bf16[16,1536]{1,0:T(8,128)(2,1)} %param.19), calls=%async_computation.13 | async-start | bytes 32768 | tf_op jit(solution)/shard_map/planes_second/slice | solution.py:123
  23.3 10.8 %copy-start.2 = (bf16[16,1792]{1,0:T(8,128)(2,1)S(1)}, bf16[16,1792]{1,0:T(8,128)(2,1)}, u32[]{:S(2)}) copy-start(bf16[16,1792]{1,0:T(8,128)(2,1)} %param.17) | copy-start | bytes 172036
  24.2 16.9 %all-to-all-start.1 = ((bf16[16,16,384]{2,1,0:T(8,128)(2,1)}), bf16[16,16,384]{2,1,0:T(8,128)(2,1)S(1)}, u32[]{:S(2)}, u32[]{:S(2)}) async-start(bf16[16,16,384]{2,1,0:T(8,128)(2,1)} %broadcast_in_dim.44), calls=%async_computation.1 | async-start | bytes 393216 | tf_op jit(solution)/shard_map/level1_up/all_to_all | solution.py:17
  30.8 10.3 %collective-permute-start.1 = (bf16[48,768]{1,0:T(8,128)(2,1)S(1)}, bf16[48,768]{1,0:T(8,128)(2,1)S(1)}, u32[]{:S(2)}, u32[]{:S(2)}) collective-permute-start(bf16[48,768]{1,0:T(8,128)(2,1)S(1)} %maximum_maximum_fusion.1), channel_id=1, source_target_pairs={{0,8},{8,0},{1,9},{9,1},{2,10},{10,2},{3,11},{11,3},{4,12},{12,4},... | collective-permute-start | bytes 221192 | tf_op jit(solution)/shard_map/level1_up/ppermute | solution.py:29
  34.5 19.9 %collective-permute-start.2 = (bf16[512,128]{1,0:T(8,128)(2,1)S(1)}, bf16[512,128]{1,0:T(8,128)(2,1)S(1)}, u32[]{:S(2)}, u32[]{:S(2)}) collective-permute-start(bf16[512,128]{1,0:T(8,128)(2,1)S(1)} %get-tuple-element.42), channel_id=1, source_target_pairs={{0,32},{32,0},{1,33},{33,1},{2,34},{34,2},{3,35},{35,3},{4,36},{36... | collective-permute-start | bytes 393224 | tf_op jit(solution)/shard_map/level1_up/ppermute | solution.py:29
  48.1 16.3 %all-to-all-start.2 = ((bf16[8,16,512]{2,1,0:T(8,128)(2,1)}), bf16[8,16,512]{2,1,0:T(8,128)(2,1)S(1)}, u32[]{:S(2)}, u32[]{:S(2)}) async-start(bf16[8,16,512]{2,1,0:T(8,128)(2,1)} %broadcast_in_dim.88), calls=%async_computation.2 | async-start | bytes 262144 | tf_op jit(solution)/shard_map/level2_up/all_to_all | solution.py:17
  54.5 5.5 %collective-permute-start.3 = (bf16[256,128]{1,0:T(8,128)(2,1)S(1)}, bf16[256,128]{1,0:T(8,128)(2,1)S(1)}, u32[]{:S(2)}, u32[]{:S(2)}) collective-permute-start(bf16[256,128]{1,0:T(8,128)(2,1)S(1)} %bitcast.179), channel_id=1, source_target_pairs={{0,8},{8,0},{1,9},{9,1},{2,10},{10,2},{3,11},{11,3},{4,12},{12,4},... | collective-permute-start | bytes 196616 | tf_op jit(solution)/shard_map/level2_up/ppermute | solution.py:29
  60.1 18.3 %collective-permute-start.4 = (bf16[1024,128]{1,0:T(8,128)(2,1)S(1)}, bf16[1024,128]{1,0:T(8,128)(2,1)S(1)}, u32[]{:S(2)}, u32[]{:S(2)}) collective-permute-start(bf16[1024,128]{1,0:T(8,128)(2,1)S(1)} %pad_maximum_fusion.2), channel_id=1, source_target_pairs={{0,16},{16,0},{1,17},{17,1},{2,18},{18,2},{3,19},{19,3},{4,20},{20... | collective-permute-start | bytes 786440 | tf_op jit(solution)/shard_map/level2_up/ppermute | solution.py:29
  65.3 14.1 %all-to-all-start.3 = ((bf16[8,208,128]{2,1,0:T(8,128)(2,1)}), bf16[8,208,128]{2,1,0:T(8,128)(2,1)S(1)}, u32[]{:S(2)}, u32[]{:S(2)}) async-start(bf16[8,208,128]{2,1,0:T(8,128)(2,1)} %copy.110), calls=%async_computation.3 | async-start | bytes 851968 | tf_op jit(solution)/shard_map/level3_up/all_to_all | solution.py:17
  80.5 11.9 %all-to-all-start.4 = ((bf16[8,16,1024]{2,1,0:T(8,128)(2,1)}), bf16[8,16,1024]{2,1,0:T(8,128)(2,1)S(1)}, u32[]{:S(2)}, u32[]{:S(2)}) async-start(bf16[8,16,1024]{2,1,0:T(8,128)(2,1)} %broadcast_in_dim.91), calls=%async_computation.4 | async-start | bytes 524288 | tf_op jit(solution)/shard_map/level3_up/all_to_all | solution.py:17
  85.4 7.0 %collective-permute-start.5 = (bf16[512,128]{1,0:T(8,128)(2,1)S(1)}, bf16[512,128]{1,0:T(8,128)(2,1)S(1)}, u32[]{:S(2)}, u32[]{:S(2)}) collective-permute-start(bf16[512,128]{1,0:T(8,128)(2,1)S(1)} %bitcast.159), channel_id=1, source_target_pairs={{0,8},{8,0},{1,9},{9,1},{2,10},{10,2},{3,11},{11,3},{4,12},{12,4},... | collective-permute-start | bytes 393224 | tf_op jit(solution)/shard_map/level3_up/ppermute | solution.py:29
  93.6 10.5 %all-to-all-start.5 = ((bf16[8,16,512]{2,1,0:T(8,128)(2,1)}), bf16[8,16,512]{2,1,0:T(8,128)(2,1)S(1)}, u32[]{:S(2)}, u32[]{:S(2)}) async-start(bf16[8,16,512]{2,1,0:T(8,128)(2,1)} %broadcast_in_dim.92), calls=%async_computation.5 | async-start | bytes 262144 | tf_op jit(solution)/shard_map/level3_down/all_to_all | solution.py:17
  98.9 15.4 %copy-start.3 = (bf16[128,256]{1,0:T(8,128)(2,1)S(1)}, bf16[128,256]{1,0:T(8,128)(2,1)}, u32[]{:S(2)}) copy-start(bf16[128,256]{1,0:T(8,128)(2,1)} %param.15) | copy-start | bytes 196612
  105.0 9.0 %all-to-all-start.6 = ((bf16[8,16,256]{2,1,0:T(8,128)(2,1)}), bf16[8,16,256]{2,1,0:T(8,128)(2,1)S(1)}, u32[]{:S(2)}, u32[]{:S(2)}) async-start(bf16[8,16,256]{2,1,0:T(8,128)(2,1)} %broadcast_in_dim.93), calls=%async_computation.6 | async-start | bytes 131072 | tf_op jit(solution)/shard_map/local_down/all_to_all | solution.py:17
  (4 other events, 3.5 us)

commit v5 on v4

--- a/solution.py
+++ b/solution.py
@@ -44,7 +44,11 @@
 
 
 def columns(m, index, width):
-    return lax.dynamic_slice_in_dim(m, index * width, width, 1)
+    return lax.dynamic_slice(m, (0, index * width), (m.shape[0], width), allow_negative_indices=False)
+
+
+def window(m, start):
+    return lax.dynamic_slice(m, (0, start), (m.shape[0], 16), allow_negative_indices=False)
 
 
 def local(
@@ -166,37 +170,32 @@
         a2 = jnp.concatenate([got[:, 16:144, :64], got[:, 16:144, 64:]], 1).reshape(512, 64)
         c2 = total(got[:, :16, :64]).astype(BF)
         rhs3 = jnp.transpose(got[:, :16, 64:96], (1, 0, 2)).reshape(16, 64)
-        sent = copies(mm(c2, a2).astype(BF), "front")
+        up = jnp.transpose(leaf_upper_inverse.reshape(8, 16, 8, 128), (2, 1, 0, 3)).reshape(8, 16, 1024)
+        whole = copies(jnp.concatenate([b1[:16], b1[16:]], 1), "front")
+        down = by_front(h1, 4)
+        extra = jnp.concatenate([up, whole, down[:, :16], down[:, 16:]], 2)
+        sent = jnp.concatenate([copies(mm(c2, a2).astype(BF), "front"), extra], 2)
         level3, level3_other = after((level3, level3_other), sent)
         level3 = ordered(level3, level3_other, ia, 0)
         g3 = level3[:, :128].reshape(256, 128)
-        g3_other = swap(g3, "c")
+        g3 = lax.all_gather(g3, "c")
         mixed = [level3[:, 256:].reshape(512, 128), level3[:, 128:256].reshape(256, 128), h2]
         mixed = jnp.concatenate(mixed, 0)
-        mixed, g3_other = lax.optimization_barrier((mixed, g3_other))
+        mixed, g3 = lax.optimization_barrier((mixed, g3))
         mixed_other = swap(mixed, "b")
         got = exchange(sent, "front")
-        got, g3, g3_other = lax.optimization_barrier((got, g3, g3_other))
-        g3 = ordered(g3, g3_other, ic, 0).reshape(2, 2, 4, 2, 16, 128)
+        got, g3 = lax.optimization_barrier((got, g3))
+        g3 = g3.reshape(2, 2, 4, 2, 16, 128)
         g3 = jnp.transpose(g3, (1, 3, 0, 4, 2, 5)).reshape(128, 512)
-        y2 = total(got).astype(BF)
+        y2 = total(got[:, :, :512]).astype(BF)
+        extra = got[:, :, 512:]
 
     with jax.named_scope("level3_up"):
         half = lax.broadcasted_iota(jnp.int32, (16, 128), 1) // 64
         part = jnp.where(half == ia, jnp.concatenate([rhs3, rhs3], 1).astype(jnp.float32), 0.0) - mm(y2, g3)
         part = part.astype(BF)
-        up = jnp.transpose(leaf_upper_inverse.reshape(128, 8, 128), (1, 0, 2))
-        down = by_front(h1, 4)
-        down = jnp.concatenate([down[:, :16], down[:, 16:]], 2)
-        whole = jnp.broadcast_to(jnp.concatenate(tiles(b1), 0)[None], (8, 64, 128))
-        up = jnp.concatenate([up, whole, down], 1)
-        up = after(up, y2)
-        up = exchange(up, "front")
         got = lax.all_gather(part, "a")
-        got, up, mixed, mixed_other = lax.optimization_barrier((got, up, mixed, mixed_other))
-        b1 = jnp.transpose(up[:, 128:192].reshape(8, 2, 2, 16, 128), (2, 0, 3, 1, 4)).reshape(256, 256)
-        h1 = jnp.transpose(up[:, 192:].reshape(8, 16, 2, 64), (2, 0, 1, 3)).reshape(256, 64)
-        up = up[:, :128].reshape(1024, 128)
+        got, mixed, mixed_other = lax.optimization_barrier((got, mixed, mixed_other))
         mixed = ordered(mixed, mixed_other, ib, 0)
         a3 = jnp.transpose(mixed[:, :512].reshape(2, 2, 256, 128), (1, 0, 2, 3)).reshape(1024, 128)
         b3 = mixed[:, 512:768].reshape(512, 128)
@@ -205,30 +204,37 @@
         sent = copies(mm(c3, a3).astype(BF), "front")
         b3_other = swap(after(b3, sent), "c")
         got = exchange(sent, "front")
-        got, b3, b3_other = lax.optimization_barrier((got, b3, b3_other))
+        extra = after(extra, sent)
+        up = jnp.transpose(extra[:, :, :1024].reshape(8, 16, 8, 128), (0, 2, 1, 3)).reshape(1024, 128)
+        b1 = jnp.transpose(extra[:, :, 1024:1536].reshape(8, 16, 2, 256), (2, 0, 1, 3)).reshape(256, 256)
+        h1 = jnp.transpose(extra[:, :, 1536:].reshape(8, 16, 2, 64), (2, 0, 1, 3)).reshape(256, 64)
+        upper = lax.dot_general(hot, up, (((0,), (0,)), ((), ())), preferred_element_type=jnp.float32)
+        upper = jnp.concatenate([upper.astype(BF), own_hot.T], 1)
+        got, b3, b3_other, upper, h1, b1, at1, at2, at3 = lax.optimization_barrier(
+            (got, b3, b3_other, upper, h1, b1, (ic * 8 + f) * 16, (2 * ib + ic) * 16, leaf * 16)
+        )
         b3 = ordered(b3, b3_other, ic, 0).reshape(2, 2, 2, 8, 16, 128)
         b3 = jnp.transpose(b3, (2, 1, 0, 4, 3, 5)).reshape(128, 1024)
         y3 = total(got).astype(BF)
 
     with jax.named_scope("level3_down"):
         z3 = mm(y3, b3).astype(BF)
-        upper = lax.dot_general(hot, up, (((0,), (0,)), ((), ())), preferred_element_type=jnp.float32)
-        upper = jnp.concatenate([upper.astype(BF), own_hot.T], 1)
+        z3, own3 = lax.optimization_barrier((z3, window(z3, at3)))
         got = exchange(copies(mm(z3, h2).astype(BF), "front"), "front")
-        got, upper = lax.optimization_barrier((got, upper))
         w2 = (y2.astype(jnp.float32) - total(got)).astype(BF)
 
     with jax.named_scope("local_down"):
         z2 = mm(w2, b2).astype(BF)
+        z2, own2 = lax.optimization_barrier((z2, window(z2, at2)))
         w1 = (y1.astype(jnp.float32) - total(exchange(copies(mm(z2, h1).astype(BF), "front"), "front"))).astype(BF)
         z1 = mm(w1, b1).astype(BF)
         w_leaf = (y_leaf.astype(jnp.float32) - mm(z1, leaf_coupling_up)).astype(BF)
         own = jnp.concatenate(
             [
                 w_leaf,
-                columns(z1, ic * 8 + f, 16),
-                columns(z2, 2 * ib + ic, 16),
-                columns(z3, leaf, 16),
+                window(z1, at1),
+                own2,
+                own3,
             ],
             1,
         )

time: 124 us -> 121 us (0.976)
  blocking collectives: 20.3 us -> 43.2 us
  starting transfers between devices: 64.1 us -> 46 us
  waiting for transfers between devices: 19.8 us -> 12 us
    all_to_all x1 -> x3, blocking collectives: 8 us -> 26.4 us  [exchange(): return lax.all_to_all(x, axes, 0, 0)]
    all_to_all x7 -> x4, starting transfers between devices: 43 us -> 28.1 us  [exchange(): return lax.all_to_all(x, axes, 0, 0)]
    all_to_all x7 -> x4, waiting for transfers between devices: 11.5 us -> 1.74 us  [exchange(): return lax.all_to_all(x, axes, 0, 0)]
    all_gather x0 -> x1, blocking collectives: none -> 4.39 us  [local(): g3 = lax.all_gather(g3, 'c')]
    ppermute x6 -> x5, starting transfers between devices: 21.1 us -> 17.9 us  [swap(): return lax.ppermute(x, axis, [(0, 1), (1, 0)])]
    broadcast_in_dim x5 -> x6, local copies, waits for them, and re-layouts: 3.49 us -> 1.53 us  [copies(): return jnp.broadcast_to(x[None], (lax.axis_size(axes),) + x.shape)]
    ppermute x6 -> x5, waiting for transfers between devices: 8.36 us -> 10.3 us  [swap(): return lax.ppermute(x, axis, [(0, 1), (1, 0)])]
    unnamed x32, local copies, waits for them, and re-layouts: 0.44 us -> 1.95 us
  transfers between devices with their start and end apart: 13 -> 9, of which waited for: 7 -> 5; matrix products, arithmetic and copies ran while one was open for 7% -> 7% of each run, Pallas kernels for 0% -> 0%
where the time goes in v5:
time: 121 us; the launch traced here: 120 us
  starting transfers between devices  46 us (38%)
  blocking collectives  43.2 us (36%)
  waiting for transfers between devices  12 us (10%)
  local copies, waits for them, and re-layouts  9.72 us (8%)
  matrix products  6.06 us (5%)
  other arithmetic  1.67 us (1%)
    all_to_all x4, starting transfers between devices, exchange(): return lax.all_to_all(x, axes, 0, 0)  28.1 us
    all_to_all x3, blocking collectives, exchange(): return lax.all_to_all(x, axes, 0, 0)  26.4 us
    ppermute x5, starting transfers between devices, swap(): return lax.ppermute(x, axis, [(0, 1), (1, 0)])  17.9 us
    ppermute x5, waiting for transfers between devices, swap(): return lax.ppermute(x, axis, [(0, 1), (1, 0)])  10.3 us
    all_gather x1, blocking collectives, local(): got = lax.all_gather(part, 'a')  7.1 us
    all_gather x1, blocking collectives, local(): got = lax.all_gather(jnp.concatenate([part, a2], 0), 'b')  5.31 us
    all_gather x1, blocking collectives, local(): g3 = lax.all_gather(g3, 'c')  4.39 us
  transfers between devices with their start and end apart: 9, of which 5 were waited for; matrix products, arithmetic and copies ran while one was open for 7% of the time, Pallas kernels for 0%

profile of v5, /device:TPU:1, one launch (start us, length us, event | category | flops | bytes accessed | tf_op | source)
XLA Modules:
  0.0 119.6 jit_solution(1697714606227762996)
XLA Ops:
  0.8 0.8 copy.125
  3.2 0.9 concatenate.64
  4.0 10.2 %all-to-all-start = ((bf16[16,16,896]{2,1,0:T(8,128)(2,1)}), bf16[16,16,896]{2,1,0:T(8,128)(2,1)S(1)}, u32[]{:S(2)}, u32[]{:S(2)}) async-start(bf16[16,16,896]{2,1,0:T(8,128)(2,1)} %concatenate.64), calls=%async_computation | async-start | bytes 917504 | tf_op jit(solution)/shard_map/first_exchange/all_to_all | solution.py:17
  14.9 1.8 %fusion.6 = bf16[128,2048]{1,0:T(8,128)(2,1)S(1)} fusion(bf16[128,1024]{1,0:T(8,128)(2,1)S(1)} %copy-done, s32[1024]{0:T(1024)S(1)} %slice_bitcast_fusion.4), kind=kOutput, calls=%fused_computation.7 | convolution fusion | flops 539230208 | bytes 790528 | tf_op jit(solution)/shard_map/order/dot_general | solution.py:104
  16.9 2.2 %collective-permute-start = (bf16[16,1792]{1,0:T(8,128)(2,1)S(1)}, bf16[16,1792]{1,0:T(8,128)(2,1)S(1)}, u32[]{:S(2)}, u32[]{:S(2)}) collective-permute-start(bf16[16,1792]{1,0:T(8,128)(2,1)S(1)} %get-tuple-element.39), channel_id=1, source_target_pairs={{0,16},{16,0},{1,17},{17,1},{2,18},{18,2},{3,19},{19,3},{4,20},{20... | collective-permute-start | bytes 172040 | tf_op jit(solution)/shard_map/planes_first/ppermute | solution.py:29
  19.7 3.2 %collective-permute-done = bf16[16,1792]{1,0:T(8,128)(2,1)S(1)} collective-permute-done((bf16[16,1792]{1,0:T(8,128)(2,1)S(1)}, bf16[16,1792]{1,0:T(8,128)(2,1)S(1)}, u32[]{:S(2)}, u32[]{:S(2)}) %collective-permute-start) | collective-permute-done | bytes 57376 | tf_op jit(solution)/shard_map/planes_first/ppermute | solution.py:29
  25.5 6.6 %all-to-all-start.1 = ((bf16[16,16,384]{2,1,0:T(8,128)(2,1)}), bf16[16,16,384]{2,1,0:T(8,128)(2,1)S(1)}, u32[]{:S(2)}, u32[]{:S(2)}) async-start(bf16[16,16,384]{2,1,0:T(8,128)(2,1)} %broadcast_in_dim.44), calls=%async_computation.1 | async-start | bytes 393216 | tf_op jit(solution)/shard_map/level1_up/all_to_all | solution.py:17
  32.2 3.3 %collective-permute-start.1 = (bf16[48,768]{1,0:T(8,128)(2,1)S(1)}, bf16[48,768]{1,0:T(8,128)(2,1)S(1)}, u32[]{:S(2)}, u32[]{:S(2)}) collective-permute-start(bf16[48,768]{1,0:T(8,128)(2,1)S(1)} %maximum_maximum_fusion), channel_id=1, source_target_pairs={{0,8},{8,0},{1,9},{9,1},{2,10},{10,2},{3,11},{11,3},{4,12},{12,4},... | collective-permute-start | bytes 221192 | tf_op jit(solution)/shard_map/level1_up/ppermute | solution.py:29
  35.7 6.5 %collective-permute-start.2 = (bf16[512,128]{1,0:T(8,128)(2,1)S(1)}, bf16[512,128]{1,0:T(8,128)(2,1)S(1)}, u32[]{:S(2)}, u32[]{:S(2)}) collective-permute-start(bf16[512,128]{1,0:T(8,128)(2,1)S(1)} %get-tuple-element.48), channel_id=1, source_target_pairs={{0,32},{32,0},{1,33},{33,1},{2,34},{34,2},{3,35},{35,3},{4,36},{36... | collective-permute-start | bytes 393224 | tf_op jit(solution)/shard_map/level1_up/ppermute | solution.py:29
  43.1 5.3 %all-gather = bf16[288,128]{1,0:T(8,128)(2,1)S(1)} all-gather(bf16[144,128]{1,0:T(8,128)(2,1)S(1)} %fusion.34), channel_id=2, replica_groups=mesh['sub'=8,'a'=2,'b'=2,'c'=2,'front'=8] {'b'}, dimensions={0}, use_global_device_ids=true | all-gather | bytes 110592 | tf_op jit(solution)/shard_map/level2_up/all_gather | solution.py:169
  49.2 1.0 concatenate.77
  50.2 6.4 %all-to-all-start.2 = ((bf16[8,16,2176]{2,1,0:T(8,128)(2,1)}), bf16[8,16,2176]{2,1,0:T(8,128)(2,1)S(1)}, u32[]{:S(2)}, u32[]{:S(2)}) async-start(bf16[8,16,2176]{2,1,0:T(8,128)(2,1)} %concatenate.77), calls=%async_computation.2 | async-start | bytes 1114112 | tf_op jit(solution)/shard_map/level2_up/all_to_all | solution.py:17
  56.7 4.4 %all_gather.17 = bf16[2,256,128]{2,1,0:T(8,128)(2,1)S(1)} all-gather(bf16[1,256,128]{2,1,0:T(8,128)(2,1)S(1)} %bitcast.191), channel_id=1, replica_groups=mesh['sub'=8,'a'=2,'b'=2,'c'=2,'front'=8] {'c'}, dimensions={0}, use_global_device_ids=true | all-gather | bytes 196608 | tf_op jit(solution)/shard_map/level2_up/all_gather | solution.py:181
  61.2 4.0 %collective-permute-start.3 = (bf16[1024,128]{1,0:T(8,128)(2,1)S(1)}, bf16[1024,128]{1,0:T(8,128)(2,1)S(1)}, u32[]{:S(2)}, u32[]{:S(2)}) collective-permute-start(bf16[1024,128]{1,0:T(8,128)(2,1)S(1)} %pad_maximum_fusion.2), channel_id=1, source_target_pairs={{0,16},{16,0},{1,17},{17,1},{2,18},{18,2},{3,19},{19,3},{4,20},{20... | collective-permute-start | bytes 786440 | tf_op jit(solution)/shard_map/level2_up/ppermute | solution.py:29
  65.2 1.1 all-to-all-done.2
  66.6 7.1 %all-gather.1 = bf16[32,128]{1,0:T(8,128)(2,1)S(1)} all-gather(bf16[16,128]{1,0:T(8,128)(2,1)S(1)} %fusion.8), channel_id=3, replica_groups=mesh['sub'=8,'a'=2,'b'=2,'c'=2,'front'=8] {'a'}, dimensions={0}, use_global_device_ids=true | all-gather | bytes 12288 | tf_op jit(solution)/shard_map/level3_up/all_gather | solution.py:197
  73.7 4.0 %collective-permute-done.3 = bf16[1024,128]{1,0:T(8,128)(2,1)S(1)} collective-permute-done((bf16[1024,128]{1,0:T(8,128)(2,1)S(1)}, bf16[1024,128]{1,0:T(8,128)(2,1)S(1)}, u32[]{:S(2)}, u32[]{:S(2)}) %collective-permute-start.3) | collective-permute-done | bytes 262176 | tf_op jit(solution)/shard_map/level2_up/ppermute | solution.py:29
  78.8 4.9 %all-to-all-start.3 = ((bf16[8,16,1024]{2,1,0:T(8,128)(2,1)}), bf16[8,16,1024]{2,1,0:T(8,128)(2,1)S(1)}, u32[]{:S(2)}, u32[]{:S(2)}) async-start(bf16[8,16,1024]{2,1,0:T(8,128)(2,1)} %broadcast_in_dim.91), calls=%async_computation.3 | async-start | bytes 524288 | tf_op jit(solution)/shard_map/level3_up/all_to_all | solution.py:17
  83.9 1.9 %collective-permute-start.4 = (bf16[512,128]{1,0:T(8,128)(2,1)S(1)}, bf16[512,128]{1,0:T(8,128)(2,1)S(1)}, u32[]{:S(2)}, u32[]{:S(2)}) collective-permute-start(bf16[512,128]{1,0:T(8,128)(2,1)S(1)} %bitcast.170), channel_id=1, source_target_pairs={{0,8},{8,0},{1,9},{9,1},{2,10},{10,2},{3,11},{11,3},{4,12},{12,4},... | collective-permute-start | bytes 393224 | tf_op jit(solution)/shard_map/level3_up/ppermute | solution.py:29
  85.8 1.9 %fusion.5 = bf16[2048,128]{0,1:T(8,128)(2,1)S(1)} fusion(bf16[1024,128]{1,0:T(8,128)(2,1)S(1)} %bitcast.188, s32[1024]{0:T(1024)S(1)} %slice_bitcast_fusion.4), kind=kOutput, calls=%fused_computation.6 | convolution fusion | flops 539230208 | bytes 790528 | tf_op jit(solution)/shard_map/level3_up/dot_general | solution.py:211
  87.8 3.1 %collective-permute-done.4 = bf16[512,128]{1,0:T(8,128)(2,1)S(1)} collective-permute-done((bf16[512,128]{1,0:T(8,128)(2,1)S(1)}, bf16[512,128]{1,0:T(8,128)(2,1)S(1)}, u32[]{:S(2)}, u32[]{:S(2)}) %collective-permute-start.4) | collective-permute-done | bytes 131104 | tf_op jit(solution)/shard_map/level3_up/ppermute | solution.py:29
  91.5 10.3 %all_to_all.35 = bf16[8,16,512]{2,1,0:T(8,128)(2,1)S(1)} all-to-all(bf16[8,16,512]{2,1,0:T(8,128)(2,1)S(1)} %broadcast_in_dim.92), channel_id=1, replica_groups=mesh['sub'=8,'a'=2,'b'=2,'c'=2,'front'=8] {'front'}, dimensions={0} | all-to-all | bytes 262144 | tf_op jit(solution)/shard_map/level3_down/all_to_all | solution.py:17
  102.2 8.1 %all_to_all.36 = bf16[8,16,256]{2,1,0:T(8,128)(2,1)S(1)} all-to-all(bf16[8,16,256]{2,1,0:T(8,128)(2,1)S(1)} %broadcast_in_dim.93), channel_id=1, replica_groups=mesh['sub'=8,'a'=2,'b'=2,'c'=2,'front'=8] {'front'}, dimensions={0} | all-to-all | bytes 131072 | tf_op jit(solution)/shard_map/local_down/all_to_all | solution.py:17
  111.0 8.0 %all_to_all.37 = bf16[8,16,256]{2,1,0:T(8,128)(2,1)S(1)} all-to-all(bf16[8,16,256]{2,1,0:T(8,128)(2,1)S(1)} %bitcast.192), channel_id=1, replica_groups=mesh['sub'=8,'a'=2,'b'=2,'c'=2,'front'=8] {'front'}, dimensions={0} | all-to-all | bytes 131072 | tf_op jit(solution)/shard_map/leaf_upper/all_to_all | solution.py:17
  (176 shorter events, 11.7 us)
Async XLA Ops:
  0.0 14.9 %copy-start = (bf16[128,1024]{1,0:T(8,128)(2,1)S(1)}, bf16[128,1024]{1,0:T(8,128)(2,1)}, u32[]{:S(2)}) copy-start(bf16[128,1024]{1,0:T(8,128)(2,1)} %param.12) | copy-start | bytes 786436
  0.0 2.0 %slice-start.5 = ((bf16[16,1792]{1,0:T(8,128)(2,1)}), bf16[16,1024]{1,0:T(8,128)(2,1)S(1)}, s32[]{:S(2)}) async-start(bf16[16,1792]{1,0:T(8,128)(2,1)} %param.16), calls=%async_computation.12 | async-start | bytes 65536 | tf_op jit(solution)/shard_map/first_exchange/slice | solution.py:89
  1.8 0.8 slice-start.2
  2.3 0.7 copy-start.5
  2.3 0.8 slice-start.4
  3.1 11.1 %copy-start.4 = (s32[1,1408]{1,0:T(1,128)S(1)}, s32[1,1408]{1,0:T(1,128)}, u32[]{:S(2)}) copy-start(s32[1,1408]{1,0:T(1,128)} %param.11) | copy-start | bytes 16900
  4.0 19.4 %all-to-all-start = ((bf16[16,16,896]{2,1,0:T(8,128)(2,1)}), bf16[16,16,896]{2,1,0:T(8,128)(2,1)S(1)}, u32[]{:S(2)}, u32[]{:S(2)}) async-start(bf16[16,16,896]{2,1,0:T(8,128)(2,1)} %concatenate.64), calls=%async_computation | async-start | bytes 917504 | tf_op jit(solution)/shard_map/first_exchange/all_to_all | solution.py:17
  14.9 1.9 %slice-start.6 = ((bf16[16,1536]{1,0:T(8,128)(2,1)}), bf16[16,512]{1,0:T(8,128)(2,1)S(1)}, s32[]{:S(2)}) async-start(bf16[16,1536]{1,0:T(8,128)(2,1)} %param.18), calls=%async_computation.13 | async-start | bytes 32768 | tf_op jit(solution)/shard_map/planes_first/slice | solution.py:108
  14.9 1.9 %slice-start = ((bf16[16,1792]{1,0:T(8,128)(2,1)}), bf16[16,512]{1,0:T(8,128)(2,1)S(1)}, s32[]{:S(2)}) async-start(bf16[16,1792]{1,0:T(8,128)(2,1)} %param.17), calls=%async_computation.7 | async-start | bytes 32768 | tf_op jit(solution)/shard_map/planes_first/slice | solution.py:109
  14.9 1.9 %slice-start.7 = ((bf16[16,1536]{1,0:T(8,128)(2,1)}), bf16[16,1024]{1,0:T(8,128)(2,1)S(1)}, s32[]{:S(2)}) async-start(bf16[16,1536]{1,0:T(8,128)(2,1)} %param.18), calls=%async_computation.14 | async-start | bytes 65536 | tf_op jit(solution)/shard_map/planes_first/slice | solution.py:109
  16.8 2.3 %copy-start.1 = (bf16[128,1024]{1,0:T(8,128)(2,1)S(1)}, bf16[128,1024]{1,0:T(8,128)(2,1)}, u32[]{:S(2)}) copy-start(bf16[128,1024]{1,0:T(8,128)(2,1)} %param.13) | copy-start | bytes 786436
  16.9 6.0 %collective-permute-start = (bf16[16,1792]{1,0:T(8,128)(2,1)S(1)}, bf16[16,1792]{1,0:T(8,128)(2,1)S(1)}, u32[]{:S(2)}, u32[]{:S(2)}) collective-permute-start(bf16[16,1792]{1,0:T(8,128)(2,1)S(1)} %get-tuple-element.39), channel_id=1, source_target_pairs={{0,16},{16,0},{1,17},{17,1},{2,18},{18,2},{3,19},{19,3},{4,20},{20... | collective-permute-start | bytes 172040 | tf_op jit(solution)/shard_map/planes_first/ppermute | solution.py:29
  23.5 0.8 copy-start.2
  24.6 7.5 %slice-start.1 = ((bf16[16,1792]{1,0:T(8,128)(2,1)}), bf16[16,256]{1,0:T(8,128)(2,1)S(1)}, s32[]{:S(2)}) async-start(bf16[16,1792]{1,0:T(8,128)(2,1)} %param.17), calls=%async_computation.8 | async-start | bytes 16384 | tf_op jit(solution)/shard_map/planes_second/slice | solution.py:127
  24.6 7.5 %slice-start.3 = ((bf16[16,1536]{1,0:T(8,128)(2,1)}), bf16[16,512]{1,0:T(8,128)(2,1)S(1)}, s32[]{:S(2)}) async-start(bf16[16,1536]{1,0:T(8,128)(2,1)} %param.19), calls=%async_computation.10 | async-start | bytes 32768 | tf_op jit(solution)/shard_map/planes_second/slice | solution.py:127
  25.5 16.7 %all-to-all-start.1 = ((bf16[16,16,384]{2,1,0:T(8,128)(2,1)}), bf16[16,16,384]{2,1,0:T(8,128)(2,1)S(1)}, u32[]{:S(2)}, u32[]{:S(2)}) async-start(bf16[16,16,384]{2,1,0:T(8,128)(2,1)} %broadcast_in_dim.44), calls=%async_computation.1 | async-start | bytes 393216 | tf_op jit(solution)/shard_map/level1_up/all_to_all | solution.py:17
  32.2 10.1 %collective-permute-start.1 = (bf16[48,768]{1,0:T(8,128)(2,1)S(1)}, bf16[48,768]{1,0:T(8,128)(2,1)S(1)}, u32[]{:S(2)}, u32[]{:S(2)}) collective-permute-start(bf16[48,768]{1,0:T(8,128)(2,1)S(1)} %maximum_maximum_fusion), channel_id=1, source_target_pairs={{0,8},{8,0},{1,9},{9,1},{2,10},{10,2},{3,11},{11,3},{4,12},{12,4},... | collective-permute-start | bytes 221192 | tf_op jit(solution)/shard_map/level1_up/ppermute | solution.py:29
  35.7 20.8 %collective-permute-start.2 = (bf16[512,128]{1,0:T(8,128)(2,1)S(1)}, bf16[512,128]{1,0:T(8,128)(2,1)S(1)}, u32[]{:S(2)}, u32[]{:S(2)}) collective-permute-start(bf16[512,128]{1,0:T(8,128)(2,1)S(1)} %get-tuple-element.48), channel_id=1, source_target_pairs={{0,32},{32,0},{1,33},{33,1},{2,34},{34,2},{3,35},{35,3},{4,36},{36... | collective-permute-start | bytes 393224 | tf_op jit(solution)/shard_map/level1_up/ppermute | solution.py:29
  50.2 16.2 %all-to-all-start.2 = ((bf16[8,16,2176]{2,1,0:T(8,128)(2,1)}), bf16[8,16,2176]{2,1,0:T(8,128)(2,1)S(1)}, u32[]{:S(2)}, u32[]{:S(2)}) async-start(bf16[8,16,2176]{2,1,0:T(8,128)(2,1)} %concatenate.77), calls=%async_computation.2 | async-start | bytes 1114112 | tf_op jit(solution)/shard_map/level2_up/all_to_all | solution.py:17
  61.2 16.6 %collective-permute-start.3 = (bf16[1024,128]{1,0:T(8,128)(2,1)S(1)}, bf16[1024,128]{1,0:T(8,128)(2,1)S(1)}, u32[]{:S(2)}, u32[]{:S(2)}) collective-permute-start(bf16[1024,128]{1,0:T(8,128)(2,1)S(1)} %pad_maximum_fusion.2), channel_id=1, source_target_pairs={{0,16},{16,0},{1,17},{17,1},{2,18},{18,2},{3,19},{19,3},{4,20},{20... | collective-permute-start | bytes 786440 | tf_op jit(solution)/shard_map/level2_up/ppermute | solution.py:29
  78.8 12.1 %all-to-all-start.3 = ((bf16[8,16,1024]{2,1,0:T(8,128)(2,1)}), bf16[8,16,1024]{2,1,0:T(8,128)(2,1)S(1)}, u32[]{:S(2)}, u32[]{:S(2)}) async-start(bf16[8,16,1024]{2,1,0:T(8,128)(2,1)} %broadcast_in_dim.91), calls=%async_computation.3 | async-start | bytes 524288 | tf_op jit(solution)/shard_map/level3_up/all_to_all | solution.py:17
  83.9 7.0 %collective-permute-start.4 = (bf16[512,128]{1,0:T(8,128)(2,1)S(1)}, bf16[512,128]{1,0:T(8,128)(2,1)S(1)}, u32[]{:S(2)}, u32[]{:S(2)}) collective-permute-start(bf16[512,128]{1,0:T(8,128)(2,1)S(1)} %bitcast.170), channel_id=1, source_target_pairs={{0,8},{8,0},{1,9},{9,1},{2,10},{10,2},{3,11},{11,3},{4,12},{12,4},... | collective-permute-start | bytes 393224 | tf_op jit(solution)/shard_map/level3_up/ppermute | solution.py:29
  91.3 19.2 %copy-start.3 = (bf16[128,256]{1,0:T(8,128)(2,1)S(1)}, bf16[128,256]{1,0:T(8,128)(2,1)}, u32[]{:S(2)}) copy-start(bf16[128,256]{1,0:T(8,128)(2,1)} %param.15) | copy-start | bytes 196612

commit v6 on v5

--- a/solution.py
+++ b/solution.py
@@ -1,6 +1,8 @@
 import jax
 import jax.numpy as jnp
 from jax import lax
+from jax.experimental import pallas as pl
+from jax.experimental.pallas import tpu as pltpu
 from jax.sharding import Mesh, PartitionSpec as P
 
 AXES = ("sub", "a", "b", "c", "front")
@@ -49,6 +51,32 @@
 
 def window(m, start):
     return lax.dynamic_slice(m, (0, start), (m.shape[0], 16), allow_negative_indices=False)
+
+
+def pack_kernel(basis, lower, upper, low, out):
+    group = lax.broadcasted_iota(jnp.int32, (16, 128), 1) // 16
+
+    def pick(ref, at, count, front, first):
+        chosen = jnp.zeros((16, 128), jnp.float32)
+        for i in range(count):
+            tile = ref[:, at + i * 128 : at + i * 128 + 128].astype(jnp.float32)
+            shift = (first + i - front) % 8 * 16
+            tile = pltpu.roll(tile, shift, 1) if shift else tile
+            chosen = jnp.where(group == first + i, tile, chosen)
+        return chosen
+
+    base = jnp.concatenate([basis[:, 128:176].astype(jnp.float32), jnp.zeros((16, 80), jnp.float32)], 1)
+    for front in range(8):
+        mixed = jnp.where(group < 4, base, pick(lower, 256, 4, front, 4)).astype(BF)
+        a3 = pick(lower, 768, 8, front, 0).astype(BF)
+        h2 = pick(upper, 512, 8, front, 0).astype(BF)
+        for peer in (front, front + 8):
+            out[peer, :, 0:128] = basis[:, 0:128]
+            out[peer, :, 128:256] = mixed
+            out[peer, :, 256:512] = lower[:, 0:256]
+            out[peer, :, 512:640] = low[:, peer * 128 : peer * 128 + 128]
+            out[peer, :, 640:768] = a3
+            out[peer, :, 768:896] = h2
 
 
 def local(
@@ -73,24 +101,12 @@
             m = jnp.transpose(m.reshape(-1, groups, 8, 16), (2, 0, 1, 3))
             return m.reshape(8, -1, groups * 16)
 
-        def per_front(m):
-            return jnp.broadcast_to(m[None], (2,) + m.shape).reshape((16,) + m.shape[1:])
-
-        def for_all(m):
-            return jnp.broadcast_to(m[None], (16,) + m.shape)
-
-        low = jnp.transpose(leaf_coupling_low.reshape(16, 16, 128), (1, 0, 2))
-        moved = jnp.concatenate(
-            [
-                for_all(jnp.pad(basis, ((0, 0), (0, 16)))),
-                per_front(by_front(sep_lower_inverse[:, 256:768], 4)),
-                for_all(sep_lower_inverse[:, :256]),
-                low,
-                per_front(by_front(sep_lower_inverse[:, 768:], 8)),
-                per_front(by_front(sep_coupling_up[:, 512:], 8)),
-            ],
-            2,
-        )
+        moved = pl.pallas_call(
+            pack_kernel,
+            out_shape=jax.ShapeDtypeStruct((16, 16, 896), BF),
+            in_specs=[pl.BlockSpec(memory_space=pltpu.VMEM)] * 4,
+            out_specs=pl.BlockSpec(memory_space=pltpu.VMEM),
+        )(basis, sep_lower_inverse, sep_coupling_up, leaf_coupling_low)
         got = exchange(moved, PAIR)
 
     with jax.named_scope("order"):
@@ -109,7 +125,9 @@
         more = jnp.concatenate([sep_upper_inverse[:, 256:768], sep_coupling_low[:, 512:]], 1)
         rows = jnp.concatenate([columns(g2, ib, 256), more], 1)
         rows_other = jnp.concatenate([columns(g2, 1 - ib, 256), more], 1)
-        lower, rows_other = lax.optimization_barrier((lower, rows_other))
+        level1 = jnp.concatenate([sep_upper_inverse[:, :256], sep_coupling_up[:, :512]], 1)
+        b3 = jnp.concatenate(tiles(sep_upper_inverse[:, 768:]), 0)
+        lower, rows_other, level1, b3 = lax.optimization_barrier((lower, rows_other, level1, b3))
         rows_other = swap(rows_other, "b")
 
     got, rows, rows_other = lax.optimization_barrier((got, rows, rows_other))
@@ -124,10 +142,9 @@
         rows = ordered(rows, rows_other, ib, 0).reshape(32, 1792)
 
     with jax.named_scope("planes_second"):
-        level1 = jnp.concatenate([sep_upper_inverse[:, :256], sep_coupling_up[:, :512]], 1)
         level2 = jnp.concatenate([rows[:, :768], level1], 0)
         g3 = rows[:, 768:]
-        tail = tiles(sep_upper_inverse[:, 768:]) + [a3]
+        tail = [b3, a3]
         level3 = jnp.concatenate(tiles(columns(g3, ia, 512)) + tail, 0)
         level3_other = jnp.concatenate(tiles(columns(g3, 1 - ia, 512)) + tail, 0)
     with jax.named_scope("weights1"):

time: 121 us -> 118 us (0.975)
  local copies, waits for them, and re-layouts: 9.72 us -> 5.24 us
  Pallas kernels: 0 us -> 1.95 us
    pallas_call x0 -> x1, Pallas kernels: none -> 1.95 us  [local(): pl.pallas_call(pack_kernel, out_shape=jax.ShapeDtypeStruct((16, 16, 896),...]
    unnamed x32 -> x30, local copies, waits for them, and re-layouts: 1.95 us -> 0.5 us
where the time goes in v6:
time: 118 us; the launch traced here: 117 us
  starting transfers between devices  46.2 us (39%)
  blocking collectives  43.2 us (37%)
  waiting for transfers between devices  11.9 us (10%)
  matrix products  6.06 us (5%)
  local copies, waits for them, and re-layouts  5.24 us (4%)
  Pallas kernels  1.95 us (2%)
  other arithmetic  1.67 us (1%)
    all_to_all x4, starting transfers between devices, exchange(): return lax.all_to_all(x, axes, 0, 0)  28.3 us
    all_to_all x3, blocking collectives, exchange(): return lax.all_to_all(x, axes, 0, 0)  26.4 us
    ppermute x5, starting transfers between devices, swap(): return lax.ppermute(x, axis, [(0, 1), (1, 0)])  17.9 us
    ppermute x5, waiting for transfers between devices, swap(): return lax.ppermute(x, axis, [(0, 1), (1, 0)])  10.3 us
    all_gather x1, blocking collectives, local(): got = lax.all_gather(part, 'a')  7.1 us
    all_gather x1, blocking collectives, local(): got = lax.all_gather(jnp.concatenate([part, a2], 0), 'b')  5.31 us
    all_gather x1, blocking collectives, local(): g3 = lax.all_gather(g3, 'c')  4.39 us
  transfers between devices with their start and end apart: 9, of which 5 were waited for; matrix products, arithmetic and copies ran while one was open for 7% of the time, Pallas kernels for 0%

profile of v6, /device:TPU:1, one launch (start us, length us, event | category | flops | bytes accessed | tf_op | source)
XLA Modules:
  0.0 117.0 jit_solution(17072944457253358527)
XLA Ops:
  0.0 1.9 %first_exchange.1 = bf16[16,16,896]{2,1,0:T(8,128)(2,1)} custom-call(bf16[16,176]{1,0:T(8,128)(2,1)} %basis.1, bf16[16,1792]{1,0:T(8,128)(2,1)} %lower.1, bf16[16,1536]{1,0:T(8,128)(2,1)} %upper.1, bf16[16,2048]{1,0:T(8,128)(2,1)} %low.1), custom_call_target="tpu_custom_call" | custom-call | tf_op jit(solution)/shard_map/first_exchange/pallas_call | solution.py:104
  2.0 10.2 %all-to-all-start = ((bf16[16,16,896]{2,1,0:T(8,128)(2,1)}), bf16[16,16,896]{2,1,0:T(8,128)(2,1)S(1)}, u32[]{:S(2)}, u32[]{:S(2)}) async-start(bf16[16,16,896]{2,1,0:T(8,128)(2,1)} %first_exchange.1), calls=%async_computation | async-start | bytes 917504 | tf_op jit(solution)/shard_map/first_exchange/all_to_all | solution.py:19
  13.0 1.8 %fusion.6 = bf16[128,2048]{1,0:T(8,128)(2,1)S(1)} fusion(bf16[128,1024]{1,0:T(8,128)(2,1)S(1)} %copy-done, s32[1024]{0:T(1024)S(1)} %slice_bitcast_fusion.3), kind=kOutput, calls=%fused_computation.7 | convolution fusion | flops 539230208 | bytes 790528 | tf_op jit(solution)/shard_map/order/dot_general | solution.py:120
  15.0 2.2 %collective-permute-start = (bf16[16,1792]{1,0:T(8,128)(2,1)S(1)}, bf16[16,1792]{1,0:T(8,128)(2,1)S(1)}, u32[]{:S(2)}, u32[]{:S(2)}) collective-permute-start(bf16[16,1792]{1,0:T(8,128)(2,1)S(1)} %get-tuple-element.41), channel_id=1, source_target_pairs={{0,16},{16,0},{1,17},{17,1},{2,18},{18,2},{3,19},{19,3},{4,20},{20... | collective-permute-start | bytes 172040 | tf_op jit(solution)/shard_map/planes_first/ppermute | solution.py:31
  17.8 3.1 %collective-permute-done = bf16[16,1792]{1,0:T(8,128)(2,1)S(1)} collective-permute-done((bf16[16,1792]{1,0:T(8,128)(2,1)S(1)}, bf16[16,1792]{1,0:T(8,128)(2,1)S(1)}, u32[]{:S(2)}, u32[]{:S(2)}) %collective-permute-start) | collective-permute-done | bytes 57376 | tf_op jit(solution)/shard_map/planes_first/ppermute | solution.py:31
  22.7 6.8 %all-to-all-start.1 = ((bf16[16,16,384]{2,1,0:T(8,128)(2,1)}), bf16[16,16,384]{2,1,0:T(8,128)(2,1)S(1)}, u32[]{:S(2)}, u32[]{:S(2)}) async-start(bf16[16,16,384]{2,1,0:T(8,128)(2,1)} %broadcast_in_dim.20), calls=%async_computation.1 | async-start | bytes 393216 | tf_op jit(solution)/shard_map/level1_up/all_to_all | solution.py:19
  29.5 3.3 %collective-permute-start.1 = (bf16[48,768]{1,0:T(8,128)(2,1)S(1)}, bf16[48,768]{1,0:T(8,128)(2,1)S(1)}, u32[]{:S(2)}, u32[]{:S(2)}) collective-permute-start(bf16[48,768]{1,0:T(8,128)(2,1)S(1)} %pad_maximum_fusion.6), channel_id=1, source_target_pairs={{0,8},{8,0},{1,9},{9,1},{2,10},{10,2},{3,11},{11,3},{4,12},{12,4},... | collective-permute-start | bytes 221192 | tf_op jit(solution)/shard_map/level1_up/ppermute | solution.py:31
  33.1 6.5 %collective-permute-start.2 = (bf16[512,128]{1,0:T(8,128)(2,1)S(1)}, bf16[512,128]{1,0:T(8,128)(2,1)S(1)}, u32[]{:S(2)}, u32[]{:S(2)}) collective-permute-start(bf16[512,128]{1,0:T(8,128)(2,1)S(1)} %get-tuple-element.52), channel_id=1, source_target_pairs={{0,32},{32,0},{1,33},{33,1},{2,34},{34,2},{3,35},{35,3},{4,36},{36... | collective-permute-start | bytes 393224 | tf_op jit(solution)/shard_map/level1_up/ppermute | solution.py:31
  40.4 5.3 %all-gather = bf16[288,128]{1,0:T(8,128)(2,1)S(1)} all-gather(bf16[144,128]{1,0:T(8,128)(2,1)S(1)} %fusion.34), channel_id=2, replica_groups=mesh['sub'=8,'a'=2,'b'=2,'c'=2,'front'=8] {'b'}, dimensions={0}, use_global_device_ids=true | all-gather | bytes 110592 | tf_op jit(solution)/shard_map/level2_up/all_gather | solution.py:186
  46.6 1.0 concatenate.77
  47.5 6.3 %all-to-all-start.2 = ((bf16[8,16,2176]{2,1,0:T(8,128)(2,1)}), bf16[8,16,2176]{2,1,0:T(8,128)(2,1)S(1)}, u32[]{:S(2)}, u32[]{:S(2)}) async-start(bf16[8,16,2176]{2,1,0:T(8,128)(2,1)} %concatenate.77), calls=%async_computation.2 | async-start | bytes 1114112 | tf_op jit(solution)/shard_map/level2_up/all_to_all | solution.py:19
  54.1 4.4 %all_gather.17 = bf16[2,256,128]{2,1,0:T(8,128)(2,1)S(1)} all-gather(bf16[1,256,128]{2,1,0:T(8,128)(2,1)S(1)} %bitcast.169), channel_id=1, replica_groups=mesh['sub'=8,'a'=2,'b'=2,'c'=2,'front'=8] {'c'}, dimensions={0}, use_global_device_ids=true | all-gather | bytes 196608 | tf_op jit(solution)/shard_map/level2_up/all_gather | solution.py:198
  58.5 4.0 %collective-permute-start.3 = (bf16[1024,128]{1,0:T(8,128)(2,1)S(1)}, bf16[1024,128]{1,0:T(8,128)(2,1)S(1)}, u32[]{:S(2)}, u32[]{:S(2)}) collective-permute-start(bf16[1024,128]{1,0:T(8,128)(2,1)S(1)} %pad_maximum_fusion.2), channel_id=1, source_target_pairs={{0,16},{16,0},{1,17},{17,1},{2,18},{18,2},{3,19},{19,3},{4,20},{20... | collective-permute-start | bytes 786440 | tf_op jit(solution)/shard_map/level2_up/ppermute | solution.py:31
  62.6 1.1 all-to-all-done.2
  64.0 7.1 %all-gather.1 = bf16[32,128]{1,0:T(8,128)(2,1)S(1)} all-gather(bf16[16,128]{1,0:T(8,128)(2,1)S(1)} %fusion.8), channel_id=3, replica_groups=mesh['sub'=8,'a'=2,'b'=2,'c'=2,'front'=8] {'a'}, dimensions={0}, use_global_device_ids=true | all-gather | bytes 12288 | tf_op jit(solution)/shard_map/level3_up/all_gather | solution.py:214
  71.1 4.0 %collective-permute-done.3 = bf16[1024,128]{1,0:T(8,128)(2,1)S(1)} collective-permute-done((bf16[1024,128]{1,0:T(8,128)(2,1)S(1)}, bf16[1024,128]{1,0:T(8,128)(2,1)S(1)}, u32[]{:S(2)}, u32[]{:S(2)}) %collective-permute-start.3) | collective-permute-done | bytes 262176 | tf_op jit(solution)/shard_map/level2_up/ppermute | solution.py:31
  75.4 0.7 broadcast_in_dim.25
  76.2 4.9 %all-to-all-start.3 = ((bf16[8,16,1024]{2,1,0:T(8,128)(2,1)}), bf16[8,16,1024]{2,1,0:T(8,128)(2,1)S(1)}, u32[]{:S(2)}, u32[]{:S(2)}) async-start(bf16[8,16,1024]{2,1,0:T(8,128)(2,1)} %broadcast_in_dim.25), calls=%async_computation.3 | async-start | bytes 524288 | tf_op jit(solution)/shard_map/level3_up/all_to_all | solution.py:19
  81.3 1.9 %collective-permute-start.4 = (bf16[512,128]{1,0:T(8,128)(2,1)S(1)}, bf16[512,128]{1,0:T(8,128)(2,1)S(1)}, u32[]{:S(2)}, u32[]{:S(2)}) collective-permute-start(bf16[512,128]{1,0:T(8,128)(2,1)S(1)} %bitcast.148), channel_id=1, source_target_pairs={{0,8},{8,0},{1,9},{9,1},{2,10},{10,2},{3,11},{11,3},{4,12},{12,4},... | collective-permute-start | bytes 393224 | tf_op jit(solution)/shard_map/level3_up/ppermute | solution.py:31
  83.2 1.9 %fusion.5 = bf16[2048,128]{0,1:T(8,128)(2,1)S(1)} fusion(bf16[1024,128]{1,0:T(8,128)(2,1)S(1)} %bitcast.166, s32[1024]{0:T(1024)S(1)} %slice_bitcast_fusion.3), kind=kOutput, calls=%fused_computation.6 | convolution fusion | flops 539230208 | bytes 790528 | tf_op jit(solution)/shard_map/level3_up/dot_general | solution.py:228
  85.1 3.1 %collective-permute-done.4 = bf16[512,128]{1,0:T(8,128)(2,1)S(1)} collective-permute-done((bf16[512,128]{1,0:T(8,128)(2,1)S(1)}, bf16[512,128]{1,0:T(8,128)(2,1)S(1)}, u32[]{:S(2)}, u32[]{:S(2)}) %collective-permute-start.4) | collective-permute-done | bytes 131104 | tf_op jit(solution)/shard_map/level3_up/ppermute | solution.py:31
  88.9 10.3 %all_to_all.35 = bf16[8,16,512]{2,1,0:T(8,128)(2,1)S(1)} all-to-all(bf16[8,16,512]{2,1,0:T(8,128)(2,1)S(1)} %broadcast_in_dim.26), channel_id=1, replica_groups=mesh['sub'=8,'a'=2,'b'=2,'c'=2,'front'=8] {'front'}, dimensions={0} | all-to-all | bytes 262144 | tf_op jit(solution)/shard_map/level3_down/all_to_all | solution.py:19
  99.6 8.1 %all_to_all.36 = bf16[8,16,256]{2,1,0:T(8,128)(2,1)S(1)} all-to-all(bf16[8,16,256]{2,1,0:T(8,128)(2,1)S(1)} %broadcast_in_dim.27), channel_id=1, replica_groups=mesh['sub'=8,'a'=2,'b'=2,'c'=2,'front'=8] {'front'}, dimensions={0} | all-to-all | bytes 131072 | tf_op jit(solution)/shard_map/local_down/all_to_all | solution.py:19
  108.4 8.0 %all_to_all.37 = bf16[8,16,256]{2,1,0:T(8,128)(2,1)S(1)} all-to-all(bf16[8,16,256]{2,1,0:T(8,128)(2,1)S(1)} %bitcast.170), channel_id=1, replica_groups=mesh['sub'=8,'a'=2,'b'=2,'c'=2,'front'=8] {'front'}, dimensions={0} | all-to-all | bytes 131072 | tf_op jit(solution)/shard_map/leaf_upper/all_to_all | solution.py:19
  (152 shorter events, 8.0 us)
Async XLA Ops:
  0.0 12.9 %copy-start = (bf16[128,1024]{1,0:T(8,128)(2,1)S(1)}, bf16[128,1024]{1,0:T(8,128)(2,1)}, u32[]{:S(2)}) copy-start(bf16[128,1024]{1,0:T(8,128)(2,1)} %param.12) | copy-start | bytes 786436
  0.0 12.2 %copy-start.5 = (s32[1,1408]{1,0:T(1,128)S(1)}, s32[1,1408]{1,0:T(1,128)}, u32[]{:S(2)}) copy-start(s32[1,1408]{1,0:T(1,128)} %param.11) | copy-start | bytes 16900
  0.0 12.3 %copy-start.3 = (bf16[16,1792]{1,0:T(8,128)(2,1)S(1)}, bf16[16,1792]{1,0:T(8,128)(2,1)}, u32[]{:S(2)}) copy-start(bf16[16,1792]{1,0:T(8,128)(2,1)} %param.17) | copy-start | bytes 172036
  2.0 19.4 %all-to-all-start = ((bf16[16,16,896]{2,1,0:T(8,128)(2,1)}), bf16[16,16,896]{2,1,0:T(8,128)(2,1)S(1)}, u32[]{:S(2)}, u32[]{:S(2)}) async-start(bf16[16,16,896]{2,1,0:T(8,128)(2,1)} %first_exchange.1), calls=%async_computation | async-start | bytes 917504 | tf_op jit(solution)/shard_map/first_exchange/all_to_all | solution.py:19
  12.9 1.9 %slice-start = ((bf16[16,1536]{1,0:T(8,128)(2,1)}), bf16[16,512]{1,0:T(8,128)(2,1)S(1)}, s32[]{:S(2)}) async-start(bf16[16,1536]{1,0:T(8,128)(2,1)} %param.18), calls=%async_computation.7 | async-start | bytes 32768 | tf_op jit(solution)/shard_map/planes_first/slice | solution.py:124
  12.9 1.9 %slice-start.1 = ((bf16[16,1536]{1,0:T(8,128)(2,1)}), bf16[16,1024]{1,0:T(8,128)(2,1)S(1)}, s32[]{:S(2)}) async-start(bf16[16,1536]{1,0:T(8,128)(2,1)} %param.18), calls=%async_computation.8 | async-start | bytes 65536 | tf_op jit(solution)/shard_map/planes_first/slice | solution.py:125
  12.9 1.9 %slice-start.3 = ((bf16[16,1792]{1,0:T(8,128)(2,1)}), bf16[16,512]{1,0:T(8,128)(2,1)S(1)}, s32[]{:S(2)}) async-start(bf16[16,1792]{1,0:T(8,128)(2,1)} %param.17), calls=%async_computation.10 | async-start | bytes 32768 | tf_op jit(solution)/shard_map/planes_first/slice | solution.py:125
  12.9 1.9 %copy-start.4 = (bf16[16,1792]{1,0:T(8,128)(2,1)S(1)}, bf16[16,1792]{1,0:T(8,128)(2,1)}, u32[]{:S(2)}) copy-start(bf16[16,1792]{1,0:T(8,128)(2,1)} %param.17) | copy-start | bytes 172036
  12.9 2.0 %slice-start.2 = ((bf16[16,1536]{1,0:T(8,128)(2,1)}), bf16[16,512]{1,0:T(8,128)(2,1)S(1)}, s32[]{:S(2)}) async-start(bf16[16,1536]{1,0:T(8,128)(2,1)} %upper.1), calls=%async_computation.9 | async-start | bytes 32768 | tf_op jit(solution)/shard_map/planes_first/slice | solution.py:128
  12.9 2.0 %slice-start.4 = ((bf16[16,1792]{1,0:T(8,128)(2,1)}), bf16[16,256]{1,0:T(8,128)(2,1)S(1)}, s32[]{:S(2)}) async-start(bf16[16,1792]{1,0:T(8,128)(2,1)} %param.17), calls=%async_computation.11 | async-start | bytes 16384 | tf_op jit(solution)/shard_map/planes_first/slice | solution.py:128
  14.9 2.3 %copy-start.1 = (bf16[128,1024]{1,0:T(8,128)(2,1)S(1)}, bf16[128,1024]{1,0:T(8,128)(2,1)}, u32[]{:S(2)}) copy-start(bf16[128,1024]{1,0:T(8,128)(2,1)} %param.13) | copy-start | bytes 786436
  15.0 6.0 %collective-permute-start = (bf16[16,1792]{1,0:T(8,128)(2,1)S(1)}, bf16[16,1792]{1,0:T(8,128)(2,1)S(1)}, u32[]{:S(2)}, u32[]{:S(2)}) collective-permute-start(bf16[16,1792]{1,0:T(8,128)(2,1)S(1)} %get-tuple-element.41), channel_id=1, source_target_pairs={{0,16},{16,0},{1,17},{17,1},{2,18},{18,2},{3,19},{19,3},{4,20},{20... | collective-permute-start | bytes 172040 | tf_op jit(solution)/shard_map/planes_first/ppermute | solution.py:31
  22.7 16.9 %all-to-all-start.1 = ((bf16[16,16,384]{2,1,0:T(8,128)(2,1)}), bf16[16,16,384]{2,1,0:T(8,128)(2,1)S(1)}, u32[]{:S(2)}, u32[]{:S(2)}) async-start(bf16[16,16,384]{2,1,0:T(8,128)(2,1)} %broadcast_in_dim.20), calls=%async_computation.1 | async-start | bytes 393216 | tf_op jit(solution)/shard_map/level1_up/all_to_all | solution.py:19
  29.5 10.1 %collective-permute-start.1 = (bf16[48,768]{1,0:T(8,128)(2,1)S(1)}, bf16[48,768]{1,0:T(8,128)(2,1)S(1)}, u32[]{:S(2)}, u32[]{:S(2)}) collective-permute-start(bf16[48,768]{1,0:T(8,128)(2,1)S(1)} %pad_maximum_fusion.6), channel_id=1, source_target_pairs={{0,8},{8,0},{1,9},{9,1},{2,10},{10,2},{3,11},{11,3},{4,12},{12,4},... | collective-permute-start | bytes 221192 | tf_op jit(solution)/shard_map/level1_up/ppermute | solution.py:31
  33.1 20.8 %collective-permute-start.2 = (bf16[512,128]{1,0:T(8,128)(2,1)S(1)}, bf16[512,128]{1,0:T(8,128)(2,1)S(1)}, u32[]{:S(2)}, u32[]{:S(2)}) collective-permute-start(bf16[512,128]{1,0:T(8,128)(2,1)S(1)} %get-tuple-element.52), channel_id=1, source_target_pairs={{0,32},{32,0},{1,33},{33,1},{2,34},{34,2},{3,35},{35,3},{4,36},{36... | collective-permute-start | bytes 393224 | tf_op jit(solution)/shard_map/level1_up/ppermute | solution.py:31
  47.5 16.2 %all-to-all-start.2 = ((bf16[8,16,2176]{2,1,0:T(8,128)(2,1)}), bf16[8,16,2176]{2,1,0:T(8,128)(2,1)S(1)}, u32[]{:S(2)}, u32[]{:S(2)}) async-start(bf16[8,16,2176]{2,1,0:T(8,128)(2,1)} %concatenate.77), calls=%async_computation.2 | async-start | bytes 1114112 | tf_op jit(solution)/shard_map/level2_up/all_to_all | solution.py:19
  58.5 16.6 %collective-permute-start.3 = (bf16[1024,128]{1,0:T(8,128)(2,1)S(1)}, bf16[1024,128]{1,0:T(8,128)(2,1)S(1)}, u32[]{:S(2)}, u32[]{:S(2)}) collective-permute-start(bf16[1024,128]{1,0:T(8,128)(2,1)S(1)} %pad_maximum_fusion.2), channel_id=1, source_target_pairs={{0,16},{16,0},{1,17},{17,1},{2,18},{18,2},{3,19},{19,3},{4,20},{20... | collective-permute-start | bytes 786440 | tf_op jit(solution)/shard_map/level2_up/ppermute | solution.py:31
  76.2 12.1 %all-to-all-start.3 = ((bf16[8,16,1024]{2,1,0:T(8,128)(2,1)}), bf16[8,16,1024]{2,1,0:T(8,128)(2,1)S(1)}, u32[]{:S(2)}, u32[]{:S(2)}) async-start(bf16[8,16,1024]{2,1,0:T(8,128)(2,1)} %broadcast_in_dim.25), calls=%async_computation.3 | async-start | bytes 524288 | tf_op jit(solution)/shard_map/level3_up/all_to_all | solution.py:19
  81.3 7.0 %collective-permute-start.4 = (bf16[512,128]{1,0:T(8,128)(2,1)S(1)}, bf16[512,128]{1,0:T(8,128)(2,1)S(1)}, u32[]{:S(2)}, u32[]{:S(2)}) collective-permute-start(bf16[512,128]{1,0:T(8,128)(2,1)S(1)} %bitcast.148), channel_id=1, source_target_pairs={{0,8},{8,0},{1,9},{9,1},{2,10},{10,2},{3,11},{11,3},{4,12},{12,4},... | collective-permute-start | bytes 393224 | tf_op jit(solution)/shard_map/level3_up/ppermute | solution.py:31
  88.6 19.2 %copy-start.2 = (bf16[128,256]{1,0:T(8,128)(2,1)S(1)}, bf16[128,256]{1,0:T(8,128)(2,1)}, u32[]{:S(2)}) copy-start(bf16[128,256]{1,0:T(8,128)(2,1)} %param.15) | copy-start | bytes 196612

commit v7 on v6

--- a/solution.py
+++ b/solution.py
@@ -56,10 +56,10 @@
 def pack_kernel(basis, lower, upper, low, out):
     group = lax.broadcasted_iota(jnp.int32, (16, 128), 1) // 16
 
-    def pick(ref, at, count, front, first):
+    def pick(ref, at, count, front, first, step=128):
         chosen = jnp.zeros((16, 128), jnp.float32)
         for i in range(count):
-            tile = ref[:, at + i * 128 : at + i * 128 + 128].astype(jnp.float32)
+            tile = ref[:, at + i * step : at + i * step + 128].astype(jnp.float32)
             shift = (first + i - front) % 8 * 16
             tile = pltpu.roll(tile, shift, 1) if shift else tile
             chosen = jnp.where(group == first + i, tile, chosen)
@@ -69,8 +69,8 @@
     for front in range(8):
         mixed = jnp.where(group < 4, base, pick(lower, 256, 4, front, 4)).astype(BF)
         a3 = pick(lower, 768, 8, front, 0).astype(BF)
-        h2 = pick(upper, 512, 8, front, 0).astype(BF)
         for peer in (front, front + 8):
+            h2 = pick(upper, 512 + peer // 8 * 128, 4, front, 0, 256).astype(BF)
             out[peer, :, 0:128] = basis[:, 0:128]
             out[peer, :, 128:256] = mixed
             out[peer, :, 256:512] = lower[:, 0:256]
@@ -93,7 +93,6 @@
 ):
     ia, ib, ic = (lax.axis_index(n) for n in ("a", "b", "c"))
     f = lax.axis_index("front")
-    leaf = 4 * ia + 2 * ib + ic
 
     with jax.named_scope("first_exchange"):
 
@@ -122,12 +121,13 @@
 
     with jax.named_scope("planes_first"):
         g2 = sep_coupling_low[:, :512]
-        more = jnp.concatenate([sep_upper_inverse[:, 256:768], sep_coupling_low[:, 512:]], 1)
-        rows = jnp.concatenate([columns(g2, ib, 256), more], 1)
-        rows_other = jnp.concatenate([columns(g2, 1 - ib, 256), more], 1)
+        g3 = sep_coupling_low[:, 512:]
+        rows = jnp.concatenate([columns(g2, ib, 256), g3], 1)
+        rows_other = jnp.concatenate([columns(g2, 1 - ib, 256), g3], 1)
         level1 = jnp.concatenate([sep_upper_inverse[:, :256], sep_coupling_up[:, :512]], 1)
         b3 = jnp.concatenate(tiles(sep_upper_inverse[:, 768:]), 0)
-        lower, rows_other, level1, b3 = lax.optimization_barrier((lower, rows_other, level1, b3))
+        b2 = jnp.concatenate(tiles(sep_upper_inverse[:, 256:768]), 0)
+        lower, rows_other, level1, b3, b2 = lax.optimization_barrier((lower, rows_other, level1, b3, b2))
         rows_other = swap(rows_other, "b")
 
     got, rows, rows_other = lax.optimization_barrier((got, rows, rows_other))
@@ -138,12 +138,13 @@
         a1 = got[:, :, 256:512].reshape(256, 256)
         low_cols = got[:, :, 512:640].reshape(256, 128)
         a3 = got[:, :, 640:768].reshape(256, 128)
-        h2 = got[:, :, 768:896].reshape(256, 128)
-        rows = ordered(rows, rows_other, ib, 0).reshape(32, 1792)
+        h2 = got[:, :, 768:832].reshape(256, 64)
+        rows = ordered(rows, rows_other, ib, 0).reshape(32, 1280)
 
     with jax.named_scope("planes_second"):
-        level2 = jnp.concatenate([rows[:, :768], level1], 0)
-        g3 = rows[:, 768:]
+        g2 = jnp.concatenate([rows[:16, :256], rows[16:, :256], rows[:16, :256]], 1)
+        level2 = jnp.concatenate([g2, level1], 0)
+        g3 = rows[:, 256:]
         tail = [b3, a3]
         level3 = jnp.concatenate(tiles(columns(g3, ia, 512)) + tail, 0)
         level3_other = jnp.concatenate(tiles(columns(g3, 1 - ia, 512)) + tail, 0)
@@ -166,10 +167,8 @@
         got = exchange(sent, PAIR)
         got, level2, level2_other = lax.optimization_barrier((got, level2, level2_other))
         level2 = ordered(level2, level2_other, ic, 0)
-        level1 = level2[:, 32:].reshape(32, 768)
-        level2 = jnp.transpose(level2[:, :32].reshape(2, 2, 16, 768), (1, 0, 2, 3)).reshape(64, 768)
-        g2 = level2[:, :256]
-        b2 = level2[:, 256:]
+        level1 = level2[:, 16:].reshape(32, 768)
+        g2 = jnp.stack([level2[:, :16, :256], level2[:, :16, 256:512]], 0).reshape(64, 256)
         b1 = level1[:, :256]
         h1 = level1[:, 256:]
         c1 = total(got[:, :, :256]).astype(BF)
@@ -194,10 +193,12 @@
         sent = jnp.concatenate([copies(mm(c2, a2).astype(BF), "front"), extra], 2)
         level3, level3_other = after((level3, level3_other), sent)
         level3 = ordered(level3, level3_other, ia, 0)
-        g3 = level3[:, :128].reshape(256, 128)
+        g3 = jnp.concatenate([level3[:, :128].reshape(256, 128), b2], 0)
         g3 = lax.all_gather(g3, "c")
-        mixed = [level3[:, 256:].reshape(512, 128), level3[:, 128:256].reshape(256, 128), h2]
-        mixed = jnp.concatenate(mixed, 0)
+        b2 = g3[:, 256:].reshape(128, 128)
+        g3 = g3[:, :256]
+        mixed = [level3[:, 256:].reshape(512, 128), level3[:, 128:256].reshape(256, 128)]
+        mixed = jnp.concatenate(mixed + [jnp.concatenate([h2[:128], h2[128:]], 1), b2], 0)
         mixed, g3 = lax.optimization_barrier((mixed, g3))
         mixed_other = swap(mixed, "b")
         got = exchange(sent, "front")
@@ -212,32 +213,31 @@
         part = jnp.where(half == ia, jnp.concatenate([rhs3, rhs3], 1).astype(jnp.float32), 0.0) - mm(y2, g3)
         part = part.astype(BF)
         got = lax.all_gather(part, "a")
-        got, mixed, mixed_other = lax.optimization_barrier((got, mixed, mixed_other))
-        mixed = ordered(mixed, mixed_other, ib, 0)
-        a3 = jnp.transpose(mixed[:, :512].reshape(2, 2, 256, 128), (1, 0, 2, 3)).reshape(1024, 128)
-        b3 = mixed[:, 512:768].reshape(512, 128)
-        h2 = mixed[:, 768:].reshape(512, 128)
-        c3 = total(got).astype(BF)
-        sent = copies(mm(c3, a3).astype(BF), "front")
-        b3_other = swap(after(b3, sent), "c")
-        got = exchange(sent, "front")
-        extra = after(extra, sent)
         up = jnp.transpose(extra[:, :, :1024].reshape(8, 16, 8, 128), (0, 2, 1, 3)).reshape(1024, 128)
         b1 = jnp.transpose(extra[:, :, 1024:1536].reshape(8, 16, 2, 256), (2, 0, 1, 3)).reshape(256, 256)
         h1 = jnp.transpose(extra[:, :, 1536:].reshape(8, 16, 2, 64), (2, 0, 1, 3)).reshape(256, 64)
         upper = lax.dot_general(hot, up, (((0,), (0,)), ((), ())), preferred_element_type=jnp.float32)
         upper = jnp.concatenate([upper.astype(BF), own_hot.T], 1)
-        got, b3, b3_other, upper, h1, b1, at1, at2, at3 = lax.optimization_barrier(
-            (got, b3, b3_other, upper, h1, b1, (ic * 8 + f) * 16, (2 * ib + ic) * 16, leaf * 16)
+        at1, at2, at3 = (ic * 8 + f) * 16, (2 * ib + ic) * 16, (2 * ia + ib) * 16
+        got, mixed, mixed_other, upper, h1, b1, at1, at2, at3 = lax.optimization_barrier(
+            (got, mixed, mixed_other, upper, h1, b1, at1, at2, at3)
         )
-        b3 = ordered(b3, b3_other, ic, 0).reshape(2, 2, 2, 8, 16, 128)
-        b3 = jnp.transpose(b3, (2, 1, 0, 4, 3, 5)).reshape(128, 1024)
+        mixed = ordered(mixed, mixed_other, ib, 0)
+        a3 = jnp.transpose(mixed[:, :512].reshape(2, 2, 256, 128), (1, 0, 2, 3)).reshape(1024, 128)
+        b3 = mixed[:, 512:768].reshape(2, 2, 8, 16, 128)
+        b3 = jnp.transpose(b3, (1, 0, 3, 2, 4)).reshape(64, 1024)
+        h2 = jnp.concatenate([mixed[:, 768:896, :64], mixed[:, 768:896, 64:]], 1).reshape(512, 64)
+        b2 = jnp.transpose(mixed[:, 896:].reshape(2, 2, 4, 16, 128), (0, 1, 3, 2, 4)).reshape(64, 512)
+        got, b3, b2, h2 = lax.optimization_barrier((got, b3, b2, h2))
+        c3 = total(got).astype(BF)
+        sent = copies(mm(c3, a3).astype(BF), "front")
+        got = exchange(sent, "front")
         y3 = total(got).astype(BF)
 
     with jax.named_scope("level3_down"):
         z3 = mm(y3, b3).astype(BF)
         z3, own3 = lax.optimization_barrier((z3, window(z3, at3)))
-        got = exchange(copies(mm(z3, h2).astype(BF), "front"), "front")
+        got = exchange(copies(mm(z3, h2).astype(BF), PAIR), PAIR)
         w2 = (y2.astype(jnp.float32) - total(got)).astype(BF)
 
     with jax.named_scope("local_down"):

time: 118 us -> 117 us (level)
  blocking collectives: 43.2 us -> 55.5 us
  starting transfers between devices: 46.2 us -> 39.1 us
  waiting for transfers between devices: 11.9 us -> 6.41 us
    all_to_all x3 -> x4, blocking collectives: 26.4 us -> 38.5 us  [exchange(): return lax.all_to_all(x, axes, 0, 0)]
    ppermute x5 -> x4, waiting for transfers between devices: 10.3 us -> 4.89 us  [swap(): return lax.ppermute(x, axis, [(0, 1), (1, 0)])]
    all_to_all x4 -> x3, starting transfers between devices: 28.3 us -> 23.3 us  [exchange(): return lax.all_to_all(x, axes, 0, 0)]
    ppermute x5 -> x4, starting transfers between devices: 17.9 us -> 15.7 us  [swap(): return lax.ppermute(x, axis, [(0, 1), (1, 0)])]
  transfers between devices with their start and end apart: 9 -> 7, of which waited for: 5 -> 4; matrix products, arithmetic and copies ran while one was open for 7% -> 7% of each run, Pallas kernels for 0% -> 0%
where the time goes in v7:
time: 117 us; the launch traced here: 116 us
  blocking collectives  55.5 us (47%)
  starting transfers between devices  39.1 us (33%)
  waiting for transfers between devices  6.41 us (5%)
  matrix products  6.03 us (5%)
  local copies, waits for them, and re-layouts  4.55 us (4%)
  Pallas kernels  1.96 us (2%)
  other arithmetic  1.83 us (2%)
    all_to_all x4, blocking collectives, exchange(): return lax.all_to_all(x, axes, 0, 0)  38.5 us
    all_to_all x3, starting transfers between devices, exchange(): return lax.all_to_all(x, axes, 0, 0)  23.3 us
    ppermute x4, starting transfers between devices, swap(): return lax.ppermute(x, axis, [(0, 1), (1, 0)])  15.7 us
    all_gather x1, blocking collectives, local(): got = lax.all_gather(part, 'a')  7.2 us
    all_gather x1, blocking collectives, local(): got = lax.all_gather(jnp.concatenate([part, a2], 0), 'b')  5.13 us
    ppermute x4, waiting for transfers between devices, swap(): return lax.ppermute(x, axis, [(0, 1), (1, 0)])  4.89 us
    all_gather x1, blocking collectives, local(): g3 = lax.all_gather(g3, 'c')  4.75 us
  transfers between devices with their start and end apart: 7, of which 4 were waited for; matrix products, arithmetic and copies ran while one was open for 7% of the time, Pallas kernels for 0%

profile of v7, /device:TPU:1, one launch (start us, length us, event | category | flops | bytes accessed | tf_op | source)
XLA Modules:
  0.0 116.2 jit_solution(16641066642912105042)
XLA Ops:
  0.0 2.0 %first_exchange.1 = bf16[16,16,896]{2,1,0:T(8,128)(2,1)} custom-call(bf16[16,176]{1,0:T(8,128)(2,1)} %basis.1, bf16[16,1792]{1,0:T(8,128)(2,1)} %lower.1, bf16[16,1536]{1,0:T(8,128)(2,1)} %upper.1, bf16[16,2048]{1,0:T(8,128)(2,1)} %low.1), custom_call_target="tpu_custom_call" | custom-call | tf_op jit(solution)/shard_map/first_exchange/pallas_call | solution.py:103
  2.0 10.4 %all-to-all-start = ((bf16[16,16,896]{2,1,0:T(8,128)(2,1)}), bf16[16,16,896]{2,1,0:T(8,128)(2,1)S(1)}, u32[]{:S(2)}, u32[]{:S(2)}) async-start(bf16[16,16,896]{2,1,0:T(8,128)(2,1)} %first_exchange.1), calls=%async_computation | async-start | bytes 917504 | tf_op jit(solution)/shard_map/first_exchange/all_to_all | solution.py:19
  13.1 1.8 %fusion.6 = bf16[128,2048]{1,0:T(8,128)(2,1)S(1)} fusion(bf16[128,1024]{1,0:T(8,128)(2,1)S(1)} %copy-done, s32[1024]{0:T(1024)S(1)} %slice_bitcast_fusion.3), kind=kOutput, calls=%fused_computation.7 | convolution fusion | flops 539230208 | bytes 790528 | tf_op jit(solution)/shard_map/order/dot_general | solution.py:119
  15.1 2.2 %collective-permute-start = (bf16[16,1280]{1,0:T(8,128)(2,1)S(1)}, bf16[16,1280]{1,0:T(8,128)(2,1)S(1)}, u32[]{:S(2)}, u32[]{:S(2)}) collective-permute-start(bf16[16,1280]{1,0:T(8,128)(2,1)S(1)} %get-tuple-element.41), channel_id=1, source_target_pairs={{0,16},{16,0},{1,17},{17,1},{2,18},{18,2},{3,19},{19,3},{4,20},{20... | collective-permute-start | bytes 122888 | tf_op jit(solution)/shard_map/planes_first/ppermute | solution.py:31
  17.9 3.0 %collective-permute-done = bf16[16,1280]{1,0:T(8,128)(2,1)S(1)} collective-permute-done((bf16[16,1280]{1,0:T(8,128)(2,1)S(1)}, bf16[16,1280]{1,0:T(8,128)(2,1)S(1)}, u32[]{:S(2)}, u32[]{:S(2)}) %collective-permute-start) | collective-permute-done | bytes 40992 | tf_op jit(solution)/shard_map/planes_first/ppermute | solution.py:31
  20.9 0.6 all-to-all-done
  22.1 0.7 broadcast_in_dim.20
  22.9 6.3 %all-to-all-start.1 = ((bf16[16,16,384]{2,1,0:T(8,128)(2,1)}), bf16[16,16,384]{2,1,0:T(8,128)(2,1)S(1)}, u32[]{:S(2)}, u32[]{:S(2)}) async-start(bf16[16,16,384]{2,1,0:T(8,128)(2,1)} %broadcast_in_dim.20), calls=%async_computation.1 | async-start | bytes 393216 | tf_op jit(solution)/shard_map/level1_up/all_to_all | solution.py:19
  29.2 3.3 %collective-permute-start.1 = (bf16[32,768]{1,0:T(8,128)(2,1)S(1)}, bf16[32,768]{1,0:T(8,128)(2,1)S(1)}, u32[]{:S(2)}, u32[]{:S(2)}) collective-permute-start(bf16[32,768]{1,0:T(8,128)(2,1)S(1)} %pad_maximum_fusion.10), channel_id=1, source_target_pairs={{0,8},{8,0},{1,9},{9,1},{2,10},{10,2},{3,11},{11,3},{4,12},{12,4},... | collective-permute-start | bytes 147464 | tf_op jit(solution)/shard_map/level1_up/ppermute | solution.py:31
  32.8 6.4 %collective-permute-start.2 = (bf16[512,128]{1,0:T(8,128)(2,1)S(1)}, bf16[512,128]{1,0:T(8,128)(2,1)S(1)}, u32[]{:S(2)}, u32[]{:S(2)}) collective-permute-start(bf16[512,128]{1,0:T(8,128)(2,1)S(1)} %get-tuple-element.52), channel_id=1, source_target_pairs={{0,32},{32,0},{1,33},{33,1},{2,34},{34,2},{3,35},{35,3},{4,36},{36... | collective-permute-start | bytes 393224 | tf_op jit(solution)/shard_map/level1_up/ppermute | solution.py:31
  40.0 5.1 %all-gather = bf16[288,128]{1,0:T(8,128)(2,1)S(1)} all-gather(bf16[144,128]{1,0:T(8,128)(2,1)S(1)} %fusion.32), channel_id=2, replica_groups=mesh['sub'=8,'a'=2,'b'=2,'c'=2,'front'=8] {'b'}, dimensions={0}, use_global_device_ids=true | all-gather | bytes 110592 | tf_op jit(solution)/shard_map/level2_up/all_gather | solution.py:185
  46.0 1.0 concatenate.90
  46.9 6.7 %all-to-all-start.2 = ((bf16[8,16,2176]{2,1,0:T(8,128)(2,1)}), bf16[8,16,2176]{2,1,0:T(8,128)(2,1)S(1)}, u32[]{:S(2)}, u32[]{:S(2)}) async-start(bf16[8,16,2176]{2,1,0:T(8,128)(2,1)} %concatenate.90), calls=%async_computation.2 | async-start | bytes 1114112 | tf_op jit(solution)/shard_map/level2_up/all_to_all | solution.py:19
  53.7 4.7 %all-gather.1 = bf16[640,128]{1,0:T(8,128)(2,1)S(1)} all-gather(bf16[320,128]{1,0:T(8,128)(2,1)S(1)} %pad_maximum_fusion.7), channel_id=3, replica_groups=mesh['sub'=8,'a'=2,'b'=2,'c'=2,'front'=8] {'c'}, dimensions={0}, use_global_device_ids=true | all-gather | bytes 245760 | tf_op jit(solution)/shard_map/level2_up/all_gather | solution.py:197
  58.7 3.8 %collective-permute-start.3 = (bf16[1024,128]{1,0:T(8,128)(2,1)S(1)}, bf16[1024,128]{1,0:T(8,128)(2,1)S(1)}, u32[]{:S(2)}, u32[]{:S(2)}) collective-permute-start(bf16[1024,128]{1,0:T(8,128)(2,1)S(1)} %pad_maximum_fusion.3), channel_id=1, source_target_pairs={{0,16},{16,0},{1,17},{17,1},{2,18},{18,2},{3,19},{19,3},{4,20},{20... | collective-permute-start | bytes 786440 | tf_op jit(solution)/shard_map/level2_up/ppermute | solution.py:31
  62.6 0.9 all-to-all-done.2
  63.5 1.9 %fusion.5 = bf16[2048,128]{0,1:T(8,128)(2,1)S(1)} fusion(bf16[1024,128]{1,0:T(8,128)(2,1)S(1)} %bitcast.177, s32[1024]{0:T(1024)S(1)} %slice_bitcast_fusion.3), kind=kOutput, calls=%fused_computation.6 | convolution fusion | flops 539230208 | bytes 790528 | tf_op jit(solution)/shard_map/level3_up/dot_general | solution.py:219
  65.8 7.2 %all-gather.2 = bf16[32,128]{1,0:T(8,128)(2,1)S(1)} all-gather(bf16[16,128]{1,0:T(8,128)(2,1)S(1)} %fusion.8), channel_id=4, replica_groups=mesh['sub'=8,'a'=2,'b'=2,'c'=2,'front'=8] {'a'}, dimensions={0}, use_global_device_ids=true | all-gather | bytes 12288 | tf_op jit(solution)/shard_map/level3_up/all_gather | solution.py:215
  73.1 1.9 %collective-permute-done.3 = bf16[1024,128]{1,0:T(8,128)(2,1)S(1)} collective-permute-done((bf16[1024,128]{1,0:T(8,128)(2,1)S(1)}, bf16[1024,128]{1,0:T(8,128)(2,1)S(1)}, u32[]{:S(2)}, u32[]{:S(2)}) %collective-permute-start.3) | collective-permute-done | bytes 262176 | tf_op jit(solution)/shard_map/level2_up/ppermute | solution.py:31
  75.6 11.4 %all_to_all.35 = bf16[8,16,1024]{2,1,0:T(8,128)(2,1)S(1)} all-to-all(bf16[8,16,1024]{2,1,0:T(8,128)(2,1)S(1)} %broadcast_in_dim.25), channel_id=1, replica_groups=mesh['sub'=8,'a'=2,'b'=2,'c'=2,'front'=8] {'front'}, dimensions={0} | all-to-all | bytes 524288 | tf_op jit(solution)/shard_map/level3_up/all_to_all | solution.py:19
  87.5 10.8 %all_to_all.36 = bf16[16,16,512]{2,1,0:T(8,128)(2,1)S(1)} all-to-all(bf16[16,16,512]{2,1,0:T(8,128)(2,1)S(1)} %broadcast_in_dim.26), channel_id=1, replica_groups=mesh['sub'=8,'a'=2,'b'=2,'c'=2,'front'=8] {'c','front'}, dimensions={0} | all-to-all | bytes 524288 | tf_op jit(solution)/shard_map/level3_down/all_to_all | solution.py:19
  98.7 8.2 %all_to_all.37 = bf16[8,16,256]{2,1,0:T(8,128)(2,1)S(1)} all-to-all(bf16[8,16,256]{2,1,0:T(8,128)(2,1)S(1)} %broadcast_in_dim.27), channel_id=1, replica_groups=mesh['sub'=8,'a'=2,'b'=2,'c'=2,'front'=8] {'front'}, dimensions={0} | all-to-all | bytes 131072 | tf_op jit(solution)/shard_map/local_down/all_to_all | solution.py:19
  107.6 8.0 %all_to_all.38 = bf16[8,16,256]{2,1,0:T(8,128)(2,1)S(1)} all-to-all(bf16[8,16,256]{2,1,0:T(8,128)(2,1)S(1)} %bitcast.183), channel_id=1, replica_groups=mesh['sub'=8,'a'=2,'b'=2,'c'=2,'front'=8] {'front'}, dimensions={0} | all-to-all | bytes 131072 | tf_op jit(solution)/shard_map/leaf_upper/all_to_all | solution.py:19
  115.6 0.6 reduce.5
  (151 shorter events, 6.4 us)
Async XLA Ops:
  0.0 13.0 %copy-start = (bf16[128,1024]{1,0:T(8,128)(2,1)S(1)}, bf16[128,1024]{1,0:T(8,128)(2,1)}, u32[]{:S(2)}) copy-start(bf16[128,1024]{1,0:T(8,128)(2,1)} %param.12) | copy-start | bytes 786436
  0.0 12.3 %copy-start.4 = (s32[1,1408]{1,0:T(1,128)S(1)}, s32[1,1408]{1,0:T(1,128)}, u32[]{:S(2)}) copy-start(s32[1,1408]{1,0:T(1,128)} %param.11) | copy-start | bytes 16900
  2.0 11.0 %copy-start.3 = (bf16[16,1792]{1,0:T(8,128)(2,1)S(1)}, bf16[16,1792]{1,0:T(8,128)(2,1)}, u32[]{:S(2)}) copy-start(bf16[16,1792]{1,0:T(8,128)(2,1)} %param.17) | copy-start | bytes 172036
  2.0 19.5 %all-to-all-start = ((bf16[16,16,896]{2,1,0:T(8,128)(2,1)}), bf16[16,16,896]{2,1,0:T(8,128)(2,1)S(1)}, u32[]{:S(2)}, u32[]{:S(2)}) async-start(bf16[16,16,896]{2,1,0:T(8,128)(2,1)} %first_exchange.1), calls=%async_computation | async-start | bytes 917504 | tf_op jit(solution)/shard_map/first_exchange/all_to_all | solution.py:19
  13.0 1.9 %slice-start = ((bf16[16,1536]{1,0:T(8,128)(2,1)}), bf16[16,512]{1,0:T(8,128)(2,1)S(1)}, s32[]{:S(2)}) async-start(bf16[16,1536]{1,0:T(8,128)(2,1)} %param.18), calls=%async_computation.7 | async-start | bytes 32768 | tf_op jit(solution)/shard_map/planes_first/slice | solution.py:123
  13.1 1.9 %slice-start.1 = ((bf16[16,1536]{1,0:T(8,128)(2,1)}), bf16[16,1024]{1,0:T(8,128)(2,1)S(1)}, s32[]{:S(2)}) async-start(bf16[16,1536]{1,0:T(8,128)(2,1)} %param.18), calls=%async_computation.8 | async-start | bytes 65536 | tf_op jit(solution)/shard_map/planes_first/slice | solution.py:124
  13.1 1.9 %slice-start.2 = ((bf16[16,1536]{1,0:T(8,128)(2,1)}), bf16[16,512]{1,0:T(8,128)(2,1)S(1)}, s32[]{:S(2)}) async-start(bf16[16,1536]{1,0:T(8,128)(2,1)} %upper.1), calls=%async_computation.9 | async-start | bytes 32768 | tf_op jit(solution)/shard_map/planes_first/slice | solution.py:127
  13.1 1.9 %slice-start.3 = ((bf16[16,1792]{1,0:T(8,128)(2,1)}), bf16[16,256]{1,0:T(8,128)(2,1)S(1)}, s32[]{:S(2)}) async-start(bf16[16,1792]{1,0:T(8,128)(2,1)} %param.17), calls=%async_computation.10 | async-start | bytes 16384 | tf_op jit(solution)/shard_map/planes_first/slice | solution.py:127
  15.0 2.5 %copy-start.1 = (bf16[128,1024]{1,0:T(8,128)(2,1)S(1)}, bf16[128,1024]{1,0:T(8,128)(2,1)}, u32[]{:S(2)}) copy-start(bf16[128,1024]{1,0:T(8,128)(2,1)} %param.13) | copy-start | bytes 786436
  15.1 5.8 %collective-permute-start = (bf16[16,1280]{1,0:T(8,128)(2,1)S(1)}, bf16[16,1280]{1,0:T(8,128)(2,1)S(1)}, u32[]{:S(2)}, u32[]{:S(2)}) collective-permute-start(bf16[16,1280]{1,0:T(8,128)(2,1)S(1)} %get-tuple-element.41), channel_id=1, source_target_pairs={{0,16},{16,0},{1,17},{17,1},{2,18},{18,2},{3,19},{19,3},{4,20},{20... | collective-permute-start | bytes 122888 | tf_op jit(solution)/shard_map/planes_first/ppermute | solution.py:31
  22.9 16.3 %all-to-all-start.1 = ((bf16[16,16,384]{2,1,0:T(8,128)(2,1)}), bf16[16,16,384]{2,1,0:T(8,128)(2,1)S(1)}, u32[]{:S(2)}, u32[]{:S(2)}) async-start(bf16[16,16,384]{2,1,0:T(8,128)(2,1)} %broadcast_in_dim.20), calls=%async_computation.1 | async-start | bytes 393216 | tf_op jit(solution)/shard_map/level1_up/all_to_all | solution.py:19
  29.2 10.0 %collective-permute-start.1 = (bf16[32,768]{1,0:T(8,128)(2,1)S(1)}, bf16[32,768]{1,0:T(8,128)(2,1)S(1)}, u32[]{:S(2)}, u32[]{:S(2)}) collective-permute-start(bf16[32,768]{1,0:T(8,128)(2,1)S(1)} %pad_maximum_fusion.10), channel_id=1, source_target_pairs={{0,8},{8,0},{1,9},{9,1},{2,10},{10,2},{3,11},{11,3},{4,12},{12,4},... | collective-permute-start | bytes 147464 | tf_op jit(solution)/shard_map/level1_up/ppermute | solution.py:31
  32.8 20.9 %collective-permute-start.2 = (bf16[512,128]{1,0:T(8,128)(2,1)S(1)}, bf16[512,128]{1,0:T(8,128)(2,1)S(1)}, u32[]{:S(2)}, u32[]{:S(2)}) collective-permute-start(bf16[512,128]{1,0:T(8,128)(2,1)S(1)} %get-tuple-element.52), channel_id=1, source_target_pairs={{0,32},{32,0},{1,33},{33,1},{2,34},{34,2},{3,35},{35,3},{4,36},{36... | collective-permute-start | bytes 393224 | tf_op jit(solution)/shard_map/level1_up/ppermute | solution.py:31
  46.9 16.5 %all-to-all-start.2 = ((bf16[8,16,2176]{2,1,0:T(8,128)(2,1)}), bf16[8,16,2176]{2,1,0:T(8,128)(2,1)S(1)}, u32[]{:S(2)}, u32[]{:S(2)}) async-start(bf16[8,16,2176]{2,1,0:T(8,128)(2,1)} %concatenate.90), calls=%async_computation.2 | async-start | bytes 1114112 | tf_op jit(solution)/shard_map/level2_up/all_to_all | solution.py:19
  58.7 16.2 %collective-permute-start.3 = (bf16[1024,128]{1,0:T(8,128)(2,1)S(1)}, bf16[1024,128]{1,0:T(8,128)(2,1)S(1)}, u32[]{:S(2)}, u32[]{:S(2)}) collective-permute-start(bf16[1024,128]{1,0:T(8,128)(2,1)S(1)} %pad_maximum_fusion.3), channel_id=1, source_target_pairs={{0,16},{16,0},{1,17},{17,1},{2,18},{18,2},{3,19},{19,3},{4,20},{20... | collective-permute-start | bytes 786440 | tf_op jit(solution)/shard_map/level2_up/ppermute | solution.py:31
  87.5 19.6 %copy-start.2 = (bf16[128,256]{1,0:T(8,128)(2,1)S(1)}, bf16[128,256]{1,0:T(8,128)(2,1)}, u32[]{:S(2)}) copy-start(bf16[128,256]{1,0:T(8,128)(2,1)} %param.15) | copy-start | bytes 196612

commit v8 on v7

--- a/solution.py
+++ b/solution.py
@@ -114,7 +114,8 @@
         leaf_place = slots[:, :128].reshape(1024)
         own_place = lax.dynamic_index_in_dim(slots, f, 0, keepdims=False)[128:]
         wide = 8 * WIDE
-        hot = (leaf_place[:, None] == lax.broadcasted_iota(jnp.int32, (1024, wide), 1)).astype(BF)
+        leaf_place = leaf_place.astype(jnp.int16)
+        hot = (leaf_place[:, None] == lax.broadcasted_iota(jnp.int16, (1024, wide), 1)).astype(BF)
         own_hot = (own_place[:, None] == lax.broadcasted_iota(jnp.int32, (48, wide), 1)).astype(BF)
         lower = lax.dot_general(leaf_inverse, hot, (((1,), (0,)), ((), ())), preferred_element_type=jnp.float32)
         lower = jnp.concatenate([lower.astype(BF), own_hot], 0)

time: 117 us -> 117 us (level)
  no operation moved by 1% of the time
where the time goes in v8:
time: 117 us; the launch traced here: 116 us
  blocking collectives  55.6 us (48%)
  starting transfers between devices  39.1 us (33%)
  waiting for transfers between devices  6.57 us (6%)
  matrix products  5.65 us (5%)
  local copies, waits for them, and re-layouts  4.55 us (4%)
  Pallas kernels  1.96 us (2%)
  other arithmetic  1.84 us (2%)
    all_to_all x4, blocking collectives, exchange(): return lax.all_to_all(x, axes, 0, 0)  38.7 us
    all_to_all x3, starting transfers between devices, exchange(): return lax.all_to_all(x, axes, 0, 0)  23.2 us
    ppermute x4, starting transfers between devices, swap(): return lax.ppermute(x, axis, [(0, 1), (1, 0)])  15.9 us
    all_gather x1, blocking collectives, local(): got = lax.all_gather(part, 'a')  7.2 us
    all_gather x1, blocking collectives, local(): got = lax.all_gather(jnp.concatenate([part, a2], 0), 'b')  4.93 us
    ppermute x4, waiting for transfers between devices, swap(): return lax.ppermute(x, axis, [(0, 1), (1, 0)])  4.86 us
    all_gather x1, blocking collectives, local(): g3 = lax.all_gather(g3, 'c')  4.75 us
  transfers between devices with their start and end apart: 7, of which 4 were waited for; matrix products, arithmetic and copies ran while one was open for 7% of the time, Pallas kernels for 0%

profile of v8, /device:TPU:1, one launch (start us, length us, event | category | flops | bytes accessed | tf_op | source)
XLA Modules:
  0.0 116.0 jit_solution(4348152854972383988)
XLA Ops:
  0.0 2.0 %first_exchange.1 = bf16[16,16,896]{2,1,0:T(8,128)(2,1)} custom-call(bf16[16,176]{1,0:T(8,128)(2,1)} %basis.1, bf16[16,1792]{1,0:T(8,128)(2,1)} %lower.1, bf16[16,1536]{1,0:T(8,128)(2,1)} %upper.1, bf16[16,2048]{1,0:T(8,128)(2,1)} %low.1), custom_call_target="tpu_custom_call" | custom-call | tf_op jit(solution)/shard_map/first_exchange/pallas_call | solution.py:103
  2.0 10.4 %all-to-all-start = ((bf16[16,16,896]{2,1,0:T(8,128)(2,1)}), bf16[16,16,896]{2,1,0:T(8,128)(2,1)S(1)}, u32[]{:S(2)}, u32[]{:S(2)}) async-start(bf16[16,16,896]{2,1,0:T(8,128)(2,1)} %first_exchange.1), calls=%async_computation | async-start | bytes 917504 | tf_op jit(solution)/shard_map/first_exchange/all_to_all | solution.py:19
  13.1 1.6 %fusion.4 = bf16[128,2048]{1,0:T(8,128)(2,1)S(1)} fusion(bf16[128,1024]{1,0:T(8,128)(2,1)S(1)} %copy-done, s16[1024]{0:T(1024)(128)(2,1)S(1)} %fusion.43), kind=kOutput, calls=%fused_computation.5 | convolution fusion | flops 539230208 | bytes 788480 | tf_op jit(solution)/shard_map/order/dot_general | solution.py:120
  14.9 2.2 %collective-permute-start = (bf16[16,1280]{1,0:T(8,128)(2,1)S(1)}, bf16[16,1280]{1,0:T(8,128)(2,1)S(1)}, u32[]{:S(2)}, u32[]{:S(2)}) collective-permute-start(bf16[16,1280]{1,0:T(8,128)(2,1)S(1)} %get-tuple-element.41), channel_id=1, source_target_pairs={{0,16},{16,0},{1,17},{17,1},{2,18},{18,2},{3,19},{19,3},{4,20},{20... | collective-permute-start | bytes 122888 | tf_op jit(solution)/shard_map/planes_first/ppermute | solution.py:31
  17.7 3.0 %collective-permute-done = bf16[16,1280]{1,0:T(8,128)(2,1)S(1)} collective-permute-done((bf16[16,1280]{1,0:T(8,128)(2,1)S(1)}, bf16[16,1280]{1,0:T(8,128)(2,1)S(1)}, u32[]{:S(2)}, u32[]{:S(2)}) %collective-permute-start) | collective-permute-done | bytes 40992 | tf_op jit(solution)/shard_map/planes_first/ppermute | solution.py:31
  20.7 0.8 all-to-all-done
  22.1 0.7 broadcast_in_dim.20
  22.9 6.1 %all-to-all-start.1 = ((bf16[16,16,384]{2,1,0:T(8,128)(2,1)}), bf16[16,16,384]{2,1,0:T(8,128)(2,1)S(1)}, u32[]{:S(2)}, u32[]{:S(2)}) async-start(bf16[16,16,384]{2,1,0:T(8,128)(2,1)} %broadcast_in_dim.20), calls=%async_computation.1 | async-start | bytes 393216 | tf_op jit(solution)/shard_map/level1_up/all_to_all | solution.py:19
  29.0 3.3 %collective-permute-start.1 = (bf16[32,768]{1,0:T(8,128)(2,1)S(1)}, bf16[32,768]{1,0:T(8,128)(2,1)S(1)}, u32[]{:S(2)}, u32[]{:S(2)}) collective-permute-start(bf16[32,768]{1,0:T(8,128)(2,1)S(1)} %pad_maximum_fusion.10), channel_id=1, source_target_pairs={{0,8},{8,0},{1,9},{9,1},{2,10},{10,2},{3,11},{11,3},{4,12},{12,4},... | collective-permute-start | bytes 147464 | tf_op jit(solution)/shard_map/level1_up/ppermute | solution.py:31
  32.6 6.6 %collective-permute-start.2 = (bf16[512,128]{1,0:T(8,128)(2,1)S(1)}, bf16[512,128]{1,0:T(8,128)(2,1)S(1)}, u32[]{:S(2)}, u32[]{:S(2)}) collective-permute-start(bf16[512,128]{1,0:T(8,128)(2,1)S(1)} %get-tuple-element.52), channel_id=1, source_target_pairs={{0,32},{32,0},{1,33},{33,1},{2,34},{34,2},{3,35},{35,3},{4,36},{36... | collective-permute-start | bytes 393224 | tf_op jit(solution)/shard_map/level1_up/ppermute | solution.py:31
  40.0 4.9 %all-gather = bf16[288,128]{1,0:T(8,128)(2,1)S(1)} all-gather(bf16[144,128]{1,0:T(8,128)(2,1)S(1)} %fusion.32), channel_id=2, replica_groups=mesh['sub'=8,'a'=2,'b'=2,'c'=2,'front'=8] {'b'}, dimensions={0}, use_global_device_ids=true | all-gather | bytes 110592 | tf_op jit(solution)/shard_map/level2_up/all_gather | solution.py:186
  45.8 1.0 concatenate.90
  46.7 6.7 %all-to-all-start.2 = ((bf16[8,16,2176]{2,1,0:T(8,128)(2,1)}), bf16[8,16,2176]{2,1,0:T(8,128)(2,1)S(1)}, u32[]{:S(2)}, u32[]{:S(2)}) async-start(bf16[8,16,2176]{2,1,0:T(8,128)(2,1)} %concatenate.90), calls=%async_computation.2 | async-start | bytes 1114112 | tf_op jit(solution)/shard_map/level2_up/all_to_all | solution.py:19
  53.5 4.7 %all-gather.1 = bf16[640,128]{1,0:T(8,128)(2,1)S(1)} all-gather(bf16[320,128]{1,0:T(8,128)(2,1)S(1)} %pad_maximum_fusion.7), channel_id=3, replica_groups=mesh['sub'=8,'a'=2,'b'=2,'c'=2,'front'=8] {'c'}, dimensions={0}, use_global_device_ids=true | all-gather | bytes 245760 | tf_op jit(solution)/shard_map/level2_up/all_gather | solution.py:198
  58.5 3.8 %collective-permute-start.3 = (bf16[1024,128]{1,0:T(8,128)(2,1)S(1)}, bf16[1024,128]{1,0:T(8,128)(2,1)S(1)}, u32[]{:S(2)}, u32[]{:S(2)}) collective-permute-start(bf16[1024,128]{1,0:T(8,128)(2,1)S(1)} %pad_maximum_fusion.3), channel_id=1, source_target_pairs={{0,16},{16,0},{1,17},{17,1},{2,18},{18,2},{3,19},{19,3},{4,20},{20... | collective-permute-start | bytes 786440 | tf_op jit(solution)/shard_map/level2_up/ppermute | solution.py:31
  62.4 0.9 all-to-all-done.2
  63.3 1.7 %fusion.3 = bf16[2048,128]{0,1:T(8,128)(2,1)S(1)} fusion(bf16[1024,128]{1,0:T(8,128)(2,1)S(1)} %bitcast.177, s16[1024]{0:T(1024)(128)(2,1)S(1)} %fusion.43), kind=kOutput, calls=%fused_computation.4 | convolution fusion | flops 539230208 | bytes 788480 | tf_op jit(solution)/shard_map/level3_up/dot_general | solution.py:220
  65.4 7.2 %all-gather.2 = bf16[32,128]{1,0:T(8,128)(2,1)S(1)} all-gather(bf16[16,128]{1,0:T(8,128)(2,1)S(1)} %fusion.8), channel_id=4, replica_groups=mesh['sub'=8,'a'=2,'b'=2,'c'=2,'front'=8] {'a'}, dimensions={0}, use_global_device_ids=true | all-gather | bytes 12288 | tf_op jit(solution)/shard_map/level3_up/all_gather | solution.py:216
  72.7 1.9 %collective-permute-done.3 = bf16[1024,128]{1,0:T(8,128)(2,1)S(1)} collective-permute-done((bf16[1024,128]{1,0:T(8,128)(2,1)S(1)}, bf16[1024,128]{1,0:T(8,128)(2,1)S(1)}, u32[]{:S(2)}, u32[]{:S(2)}) %collective-permute-start.3) | collective-permute-done | bytes 262176 | tf_op jit(solution)/shard_map/level2_up/ppermute | solution.py:31
  75.2 11.6 %all_to_all.35 = bf16[8,16,1024]{2,1,0:T(8,128)(2,1)S(1)} all-to-all(bf16[8,16,1024]{2,1,0:T(8,128)(2,1)S(1)} %broadcast_in_dim.25), channel_id=1, replica_groups=mesh['sub'=8,'a'=2,'b'=2,'c'=2,'front'=8] {'front'}, dimensions={0} | all-to-all | bytes 524288 | tf_op jit(solution)/shard_map/level3_up/all_to_all | solution.py:19
  87.3 10.8 %all_to_all.36 = bf16[16,16,512]{2,1,0:T(8,128)(2,1)S(1)} all-to-all(bf16[16,16,512]{2,1,0:T(8,128)(2,1)S(1)} %broadcast_in_dim.26), channel_id=1, replica_groups=mesh['sub'=8,'a'=2,'b'=2,'c'=2,'front'=8] {'c','front'}, dimensions={0} | all-to-all | bytes 524288 | tf_op jit(solution)/shard_map/level3_down/all_to_all | solution.py:19
  98.5 8.2 %all_to_all.37 = bf16[8,16,256]{2,1,0:T(8,128)(2,1)S(1)} all-to-all(bf16[8,16,256]{2,1,0:T(8,128)(2,1)S(1)} %broadcast_in_dim.27), channel_id=1, replica_groups=mesh['sub'=8,'a'=2,'b'=2,'c'=2,'front'=8] {'front'}, dimensions={0} | all-to-all | bytes 131072 | tf_op jit(solution)/shard_map/local_down/all_to_all | solution.py:19
  107.4 8.0 %all_to_all.38 = bf16[8,16,256]{2,1,0:T(8,128)(2,1)S(1)} all-to-all(bf16[8,16,256]{2,1,0:T(8,128)(2,1)S(1)} %bitcast.183), channel_id=1, replica_groups=mesh['sub'=8,'a'=2,'b'=2,'c'=2,'front'=8] {'front'}, dimensions={0} | all-to-all | bytes 131072 | tf_op jit(solution)/shard_map/leaf_upper/all_to_all | solution.py:19
  115.4 0.6 reduce.5
  (151 shorter events, 6.4 us)
Async XLA Ops:
  0.0 13.0 %copy-start = (bf16[128,1024]{1,0:T(8,128)(2,1)S(1)}, bf16[128,1024]{1,0:T(8,128)(2,1)}, u32[]{:S(2)}) copy-start(bf16[128,1024]{1,0:T(8,128)(2,1)} %param.12) | copy-start | bytes 786436
  0.0 12.3 %copy-start.4 = (s32[1,1408]{1,0:T(1,128)S(1)}, s32[1,1408]{1,0:T(1,128)}, u32[]{:S(2)}) copy-start(s32[1,1408]{1,0:T(1,128)} %param.11) | copy-start | bytes 16900
  2.0 11.0 %copy-start.3 = (bf16[16,1792]{1,0:T(8,128)(2,1)S(1)}, bf16[16,1792]{1,0:T(8,128)(2,1)}, u32[]{:S(2)}) copy-start(bf16[16,1792]{1,0:T(8,128)(2,1)} %param.17) | copy-start | bytes 172036
  2.0 19.5 %all-to-all-start = ((bf16[16,16,896]{2,1,0:T(8,128)(2,1)}), bf16[16,16,896]{2,1,0:T(8,128)(2,1)S(1)}, u32[]{:S(2)}, u32[]{:S(2)}) async-start(bf16[16,16,896]{2,1,0:T(8,128)(2,1)} %first_exchange.1), calls=%async_computation | async-start | bytes 917504 | tf_op jit(solution)/shard_map/first_exchange/all_to_all | solution.py:19
  13.0 1.7 %slice-start = ((bf16[16,1536]{1,0:T(8,128)(2,1)}), bf16[16,512]{1,0:T(8,128)(2,1)S(1)}, s32[]{:S(2)}) async-start(bf16[16,1536]{1,0:T(8,128)(2,1)} %param.18), calls=%async_computation.7 | async-start | bytes 32768 | tf_op jit(solution)/shard_map/planes_first/slice | solution.py:124
  13.1 1.7 %slice-start.1 = ((bf16[16,1536]{1,0:T(8,128)(2,1)}), bf16[16,1024]{1,0:T(8,128)(2,1)S(1)}, s32[]{:S(2)}) async-start(bf16[16,1536]{1,0:T(8,128)(2,1)} %param.18), calls=%async_computation.8 | async-start | bytes 65536 | tf_op jit(solution)/shard_map/planes_first/slice | solution.py:125
  13.1 1.7 %slice-start.2 = ((bf16[16,1536]{1,0:T(8,128)(2,1)}), bf16[16,512]{1,0:T(8,128)(2,1)S(1)}, s32[]{:S(2)}) async-start(bf16[16,1536]{1,0:T(8,128)(2,1)} %upper.1), calls=%async_computation.9 | async-start | bytes 32768 | tf_op jit(solution)/shard_map/planes_first/slice | solution.py:128
  13.1 1.7 %slice-start.3 = ((bf16[16,1792]{1,0:T(8,128)(2,1)}), bf16[16,256]{1,0:T(8,128)(2,1)S(1)}, s32[]{:S(2)}) async-start(bf16[16,1792]{1,0:T(8,128)(2,1)} %param.17), calls=%async_computation.10 | async-start | bytes 16384 | tf_op jit(solution)/shard_map/planes_first/slice | solution.py:128
  14.8 2.5 %copy-start.1 = (bf16[128,1024]{1,0:T(8,128)(2,1)S(1)}, bf16[128,1024]{1,0:T(8,128)(2,1)}, u32[]{:S(2)}) copy-start(bf16[128,1024]{1,0:T(8,128)(2,1)} %param.13) | copy-start | bytes 786436
  14.9 5.8 %collective-permute-start = (bf16[16,1280]{1,0:T(8,128)(2,1)S(1)}, bf16[16,1280]{1,0:T(8,128)(2,1)S(1)}, u32[]{:S(2)}, u32[]{:S(2)}) collective-permute-start(bf16[16,1280]{1,0:T(8,128)(2,1)S(1)} %get-tuple-element.41), channel_id=1, source_target_pairs={{0,16},{16,0},{1,17},{17,1},{2,18},{18,2},{3,19},{19,3},{4,20},{20... | collective-permute-start | bytes 122888 | tf_op jit(solution)/shard_map/planes_first/ppermute | solution.py:31
  22.9 16.3 %all-to-all-start.1 = ((bf16[16,16,384]{2,1,0:T(8,128)(2,1)}), bf16[16,16,384]{2,1,0:T(8,128)(2,1)S(1)}, u32[]{:S(2)}, u32[]{:S(2)}) async-start(bf16[16,16,384]{2,1,0:T(8,128)(2,1)} %broadcast_in_dim.20), calls=%async_computation.1 | async-start | bytes 393216 | tf_op jit(solution)/shard_map/level1_up/all_to_all | solution.py:19
  29.0 10.2 %collective-permute-start.1 = (bf16[32,768]{1,0:T(8,128)(2,1)S(1)}, bf16[32,768]{1,0:T(8,128)(2,1)S(1)}, u32[]{:S(2)}, u32[]{:S(2)}) collective-permute-start(bf16[32,768]{1,0:T(8,128)(2,1)S(1)} %pad_maximum_fusion.10), channel_id=1, source_target_pairs={{0,8},{8,0},{1,9},{9,1},{2,10},{10,2},{3,11},{11,3},{4,12},{12,4},... | collective-permute-start | bytes 147464 | tf_op jit(solution)/shard_map/level1_up/ppermute | solution.py:31
  32.6 20.9 %collective-permute-start.2 = (bf16[512,128]{1,0:T(8,128)(2,1)S(1)}, bf16[512,128]{1,0:T(8,128)(2,1)S(1)}, u32[]{:S(2)}, u32[]{:S(2)}) collective-permute-start(bf16[512,128]{1,0:T(8,128)(2,1)S(1)} %get-tuple-element.52), channel_id=1, source_target_pairs={{0,32},{32,0},{1,33},{33,1},{2,34},{34,2},{3,35},{35,3},{4,36},{36... | collective-permute-start | bytes 393224 | tf_op jit(solution)/shard_map/level1_up/ppermute | solution.py:31
  46.7 16.5 %all-to-all-start.2 = ((bf16[8,16,2176]{2,1,0:T(8,128)(2,1)}), bf16[8,16,2176]{2,1,0:T(8,128)(2,1)S(1)}, u32[]{:S(2)}, u32[]{:S(2)}) async-start(bf16[8,16,2176]{2,1,0:T(8,128)(2,1)} %concatenate.90), calls=%async_computation.2 | async-start | bytes 1114112 | tf_op jit(solution)/shard_map/level2_up/all_to_all | solution.py:19
  58.5 16.0 %collective-permute-start.3 = (bf16[1024,128]{1,0:T(8,128)(2,1)S(1)}, bf16[1024,128]{1,0:T(8,128)(2,1)S(1)}, u32[]{:S(2)}, u32[]{:S(2)}) collective-permute-start(bf16[1024,128]{1,0:T(8,128)(2,1)S(1)} %pad_maximum_fusion.3), channel_id=1, source_target_pairs={{0,16},{16,0},{1,17},{17,1},{2,18},{18,2},{3,19},{19,3},{4,20},{20... | collective-permute-start | bytes 786440 | tf_op jit(solution)/shard_map/level2_up/ppermute | solution.py:31
  87.3 19.6 %copy-start.2 = (bf16[128,256]{1,0:T(8,128)(2,1)S(1)}, bf16[128,256]{1,0:T(8,128)(2,1)}, u32[]{:S(2)}) copy-start(bf16[128,256]{1,0:T(8,128)(2,1)} %param.15) | copy-start | bytes 196612
